TPU v7x, 128 devices: a whole 4x4x4 slice. The times are simulated.
128 devices in a mesh: section: 2 (over x_hi), ctx: 16 (over z, x_lo, core), fsdp: 4 (over y).
Axes of the slice: x: 4 (x_hi: 2, x_lo: 2; x = x_hi * 2 + x_lo), y: 4, z: 4, core: 2. Of those that a mesh axis runs over, the one named last changes fastest.
Arguments:
- tokens: bfloat16 [2, 4, 2, 768, 960], P(None, 'fsdp', None, 'ctx'), may hold values from -6 to 6
- cotangent: bfloat16 [2, 4, 2, 768, 960], P(None, 'fsdp', None, 'ctx'), may hold values from -6 to 6
- norm_attn: bfloat16 [2, 960], P('section', 'fsdp'), may hold values from 0.25 to 1.75
- w_query: bfloat16 [2, 960, 960], P('section', 'fsdp'), may hold values from -0.1875 to 0.1875
- key_projection: bfloat16 [2, 960, 320], P('section', 'fsdp'), may hold values from -0.1875 to 0.1875
- value_projection: bfloat16 [2, 960, 320], P('section', 'fsdp'), may hold values from -0.1875 to 0.1875
- w_out: bfloat16 [2, 960, 960], P('section', 'fsdp'), may hold values from -3.5 to 3.5
- norm_ffn: bfloat16 [2, 960], P('section', 'fsdp'), may hold values from 0.25 to 1.75
- w_gate: bfloat16 [2, 960, 2560], P('section', 'fsdp'), may hold values from -0.1875 to 0.1875
- w_up: bfloat16 [2, 960, 2560], P('section', 'fsdp'), may hold values from -0.1875 to 0.1875
- w_down: bfloat16 [2, 2560, 960], P('section', 'fsdp'), may hold values from -0.125 to 0.125
Outputs:
- acts: bfloat16 [2, 2, 4, 2, 768, 960], P('section', None, 'fsdp', None, 'ctx')
- in_grads: float32 [2, 2, 4, 2, 768, 960], P('section', None, 'fsdp', None, 'ctx')
- grad_norm_attn: float32 [2, 960], P('section', 'fsdp')
- grad_query: float32 [2, 960, 960], P('section', 'fsdp')
- grad_key: float32 [2, 960, 320], P('section', 'fsdp')
- grad_value: float32 [2, 960, 320], P('section', 'fsdp')
- grad_out: float32 [2, 960, 960], P('section', 'fsdp')
- grad_norm_ffn: float32 [2, 960], P('section', 'fsdp')
- grad_gate: float32 [2, 960, 2560], P('section', 'fsdp')
- grad_up: float32 [2, 960, 2560], P('section', 'fsdp')
- grad_down: float32 [2, 2560, 960], P('section', 'fsdp')
All inputs are finite; a program needn't handle non-finite values.
Results may differ from a plain program's by a relative error of at most 0.03.
Values may be sent and summed in bfloat16 or wider, within the bound.
No kernel may reach another device: no remote copies, remote signals or barrier semaphores. Data moves between devices by JAX's collectives and lax.ppermute only.
A program may use at most 192 MiB of HBM per device.

v0:
```python
import math

import jax
import jax.numpy as jnp
from jax import lax
from jax.sharding import PartitionSpec as P

QUERY_HEADS = 15
KEY_VALUE_HEADS = 5
HEAD_DIMENSION = 64


EPSILON = 1e-05
THETA = 10000.0
MASKED = -1e30


def passed_along(block, axis, distance):
    devices = range(lax.axis_size(axis))
    route = [(i - distance, i) for i in devices if i - distance in devices]
    return lax.ppermute(block, axis, route)


def rotary_tables(positions, head_size):
    half_size = head_size // 2
    inverse = THETA ** (-(jnp.arange(half_size, dtype=jnp.float32) * 2.0) / head_size)
    angles = positions.astype(jnp.float32)[:, None] * inverse[None, :]
    return (jnp.cos(angles), jnp.sin(angles))


def apply_rotary(values, cosine_rows_table, sine_rows_table):
    half_size = values.shape[-1] // 2
    first_half = values[..., :half_size]
    second_half = values[..., half_size:]
    cos_rows = cosine_rows_table[:, None, :]
    sin_rows = sine_rows_table[:, None, :]
    return jnp.concatenate(
        [
            first_half * cos_rows - second_half * sin_rows,
            second_half * cos_rows + first_half * sin_rows,
        ],
        axis=-1,
    )


def rms_scale(values, gain):
    return values * lax.rsqrt(jnp.mean(values * values, axis=-1, keepdims=True) + EPSILON) * gain


def stored_positions(device, count, block_size, index):
    half_index = index // block_size % 2
    offset = index % block_size
    return jnp.where(
        half_index == 0,
        device * block_size + offset,
        (2 * count - 1 - device) * block_size + offset,
    )


def attention_scores(query_rows, key_row_block, row_positions, key_positions, query_group_count):
    grouped_queries = query_rows.reshape(
        query_rows.shape[0], KEY_VALUE_HEADS, query_group_count, HEAD_DIMENSION
    )
    key_head_split = key_row_block.reshape(key_row_block.shape[0], KEY_VALUE_HEADS, HEAD_DIMENSION)
    scores = jnp.einsum(
        "qgrd,kgd->grqk", grouped_queries, key_head_split, preferred_element_type=jnp.float32
    )
    allowed = key_positions[None, :] <= row_positions[:, None]
    return jnp.where(allowed, scores, MASKED)


def contract(left_side, right_side):
    return lax.dot_general(
        left_side, right_side, (((0,), (0,)), ((), ())), preferred_element_type=jnp.float32
    )


def on_device(
    tokens,
    cotangent,
    norm_attn,
    w_query,
    key_projection,
    value_projection,
    w_out,
    norm_ffn,
    w_gate,
    w_up,
    w_down,
):
    micro_count = tokens.shape[0]
    block_size = tokens.shape[3]
    model_width = tokens.shape[4]
    count_of_rows = 2 * block_size
    ctx_count = lax.axis_size("ctx")
    first_section = lax.axis_index("section") == 0
    query_group_count = QUERY_HEADS // KEY_VALUE_HEADS
    head_scale_factor = 1.0 / math.sqrt(HEAD_DIMENSION)
    local_index = jnp.arange(count_of_rows, dtype=jnp.int32)
    row_positions = stored_positions(lax.axis_index("ctx"), ctx_count, block_size, local_index)
    global_index = jnp.arange(count_of_rows * ctx_count, dtype=jnp.int32)
    key_positions = stored_positions(
        global_index // count_of_rows, ctx_count, block_size, global_index
    )
    cosine_table, sine_rows_table = rotary_tables(row_positions, HEAD_DIMENSION)

    def apply_rotary_inverse(values):
        unused, pull_back = jax.vjp(
            lambda inner_values: apply_rotary(inner_values, cosine_table, sine_rows_table), values
        )
        return pull_back(values)[0]

    gathered = (
        lax.all_gather(norm_attn[0], "fsdp", axis=0, tiled=True),
        lax.all_gather(w_query[0], "fsdp", axis=0, tiled=True),
        lax.all_gather(key_projection[0], "fsdp", axis=0, tiled=True),
        lax.all_gather(value_projection[0], "fsdp", axis=0, tiled=True),
        lax.all_gather(w_out[0], "fsdp", axis=0, tiled=True),
        lax.all_gather(norm_ffn[0], "fsdp", axis=0, tiled=True),
        lax.all_gather(w_gate[0], "fsdp", axis=0, tiled=True),
        lax.all_gather(w_up[0], "fsdp", axis=0, tiled=True),
        lax.all_gather(w_down[0], "fsdp", axis=0, tiled=True),
    )

    def fetch():
        return gathered

    def backward(grad_output, kept_state, params):
        (
            layer_input,
            mixed_rows,
            query_rows,
            gathered_keys,
            gathered_values,
            log_total,
            attended,
            gate_value,
            up_value,
        ) = kept_state
        (
            gain_attn,
            query_weight,
            key_matrix,
            value_matrix,
            out_weight,
            gain_ffn,
            gate_weight,
            up_weight,
            down_weight,
        ) = params
        grad_branch = grad_output.astype(jnp.bfloat16)
        swiglu_value, swiglu_back = jax.vjp(
            lambda gate_in, up_in: jax.nn.silu(gate_in) * up_in, gate_value, up_value
        )
        hidden = swiglu_value.astype(jnp.bfloat16)
        grad_hidden = jnp.dot(grad_branch, down_weight.T, preferred_element_type=jnp.float32)
        grad_gate, grad_up = swiglu_back(grad_hidden)
        grad_gate = grad_gate.astype(jnp.bfloat16)
        grad_up = grad_up.astype(jnp.bfloat16)
        normed_ffn_full, norm_ffn_back = jax.vjp(
            rms_scale, mixed_rows, gain_ffn.astype(jnp.float32)
        )
        normed_ffn = normed_ffn_full.astype(jnp.bfloat16)
        grad_normed_ffn = jnp.dot(
            grad_gate, gate_weight.T, preferred_element_type=jnp.float32
        ) + jnp.dot(grad_up, up_weight.T, preferred_element_type=jnp.float32)
        grad_mixed_norm, grad_gain_ffn = norm_ffn_back(grad_normed_ffn)
        grad_mixed = grad_output + grad_mixed_norm
        grad_attn_branch = grad_mixed.astype(jnp.bfloat16)
        attended_gradient = jnp.dot(
            grad_attn_branch, out_weight.T, preferred_element_type=jnp.float32
        ).astype(jnp.bfloat16)
        scores = attention_scores(
            query_rows, gathered_keys, row_positions, key_positions, query_group_count
        )
        weights = jnp.exp(scores - log_total)
        group_gradient = attended_gradient.reshape(
            count_of_rows, KEY_VALUE_HEADS, query_group_count, HEAD_DIMENSION
        )
        value_head_split = gathered_values.reshape(-1, KEY_VALUE_HEADS, HEAD_DIMENSION)
        key_head_split = gathered_keys.reshape(-1, KEY_VALUE_HEADS, HEAD_DIMENSION)
        grouped_queries = query_rows.reshape(
            count_of_rows, KEY_VALUE_HEADS, query_group_count, HEAD_DIMENSION
        )
        grad_weights = jnp.einsum(
            "qgrd,kgd->grqk", group_gradient, value_head_split, preferred_element_type=jnp.float32
        )
        inner_sum = jnp.sum(weights * grad_weights, axis=-1, keepdims=True)
        grad_scores = (weights * (grad_weights - inner_sum)).astype(jnp.bfloat16)
        grad_query_rot = jnp.einsum(
            "grqk,kgd->qgrd", grad_scores, key_head_split, preferred_element_type=jnp.float32
        ).reshape(count_of_rows, QUERY_HEADS, HEAD_DIMENSION)
        key_term = jnp.einsum(
            "grqk,qgrd->kgd", grad_scores, grouped_queries, preferred_element_type=jnp.float32
        ).reshape(-1, KEY_VALUE_HEADS * HEAD_DIMENSION)
        value_term = jnp.einsum(
            "grqk,qgrd->kgd",
            weights.astype(jnp.bfloat16),
            group_gradient,
            preferred_element_type=jnp.float32,
        ).reshape(-1, KEY_VALUE_HEADS * HEAD_DIMENSION)
        rotated_key_gradient, grad_value_sum = (
            lax.psum_scatter(
                key_term.astype(jnp.bfloat16), "ctx", scatter_dimension=0, tiled=True
            ).astype(jnp.float32),
            lax.psum_scatter(
                value_term.astype(jnp.bfloat16), "ctx", scatter_dimension=0, tiled=True
            ).astype(jnp.float32),
        )
        grad_query = (
            apply_rotary_inverse(grad_query_rot * head_scale_factor)
            .reshape(count_of_rows, QUERY_HEADS * HEAD_DIMENSION)
            .astype(jnp.bfloat16)
        )
        grad_key = (
            apply_rotary_inverse(
                rotated_key_gradient.reshape(count_of_rows, KEY_VALUE_HEADS, HEAD_DIMENSION)
            )
            .reshape(count_of_rows, KEY_VALUE_HEADS * HEAD_DIMENSION)
            .astype(jnp.bfloat16)
        )
        grad_value = grad_value_sum.astype(jnp.bfloat16)
        normed_full, norm_attn_back = jax.vjp(rms_scale, layer_input, gain_attn.astype(jnp.float32))
        normalized_input = normed_full.astype(jnp.bfloat16)
        grad_normed = jnp.dot(grad_query, query_weight.T, preferred_element_type=jnp.float32)
        grad_normed = grad_normed + jnp.dot(
            grad_key, key_matrix.T, preferred_element_type=jnp.float32
        )
        grad_normed = grad_normed + jnp.dot(
            grad_value, value_matrix.T, preferred_element_type=jnp.float32
        )
        grad_input_norm, grad_gain_attn = norm_attn_back(grad_normed)
        grad_input = grad_mixed + grad_input_norm
        operands = (
            normalized_input,
            grad_query,
            grad_key,
            grad_value,
            attended,
            grad_attn_branch,
            normed_ffn,
            grad_gate,
            grad_up,
            hidden,
            grad_branch,
        )
        return (grad_input, (grad_gain_attn, grad_gain_ffn), operands)

    def pick(section_zero, section_one):
        return jax.tree.map(
            lambda zero_item, one_item: jnp.where(first_section, zero_item, one_item),
            section_zero,
            section_one,
        )

    inputs_all = tokens.reshape(micro_count, count_of_rows, model_width)
    upstream_all = cotangent.reshape(micro_count, count_of_rows, model_width)
    received = jnp.zeros((count_of_rows, model_width), jnp.bfloat16)
    kept_list = []
    sent_list = []
    for step_index in range(micro_count + 1):
        own_input = inputs_all[min(step_index, micro_count - 1)]
        layer_input = jnp.where(first_section, own_input, received).astype(jnp.float32)
        (
            forward_gain_attn,
            forward_query_weight,
            forward_key_matrix,
            forward_value_matrix,
            forward_out_weight,
            forward_gain_ffn,
            forward_gate_weight,
            forward_up_weight,
            forward_down_weight,
        ) = fetch()
        forward_normalized_input = rms_scale(
            layer_input, forward_gain_attn.astype(jnp.float32)
        ).astype(jnp.bfloat16)
        query_lin = jnp.dot(
            forward_normalized_input, forward_query_weight, preferred_element_type=jnp.float32
        ).reshape(count_of_rows, QUERY_HEADS, HEAD_DIMENSION)
        key_lin = jnp.dot(
            forward_normalized_input, forward_key_matrix, preferred_element_type=jnp.float32
        ).reshape(count_of_rows, KEY_VALUE_HEADS, HEAD_DIMENSION)
        value_new = jnp.dot(
            forward_normalized_input, forward_value_matrix, preferred_element_type=jnp.float32
        ).astype(jnp.bfloat16)
        forward_query_rows = (
            apply_rotary(query_lin, cosine_table, sine_rows_table) * head_scale_factor
        ).astype(jnp.bfloat16)
        key_new = (
            apply_rotary(key_lin, cosine_table, sine_rows_table)
            .astype(jnp.bfloat16)
            .reshape(count_of_rows, KEY_VALUE_HEADS * HEAD_DIMENSION)
        )
        forward_gathered_keys = lax.all_gather(key_new, "ctx", axis=0, tiled=True)
        forward_gathered_values = lax.all_gather(value_new, "ctx", axis=0, tiled=True)
        forward_scores = attention_scores(
            forward_query_rows,
            forward_gathered_keys,
            row_positions,
            key_positions,
            query_group_count,
        )
        row_max = jnp.max(forward_scores, axis=-1, keepdims=True)
        forward_weights = jnp.exp(forward_scores - row_max)
        totals = jnp.sum(forward_weights, axis=-1, keepdims=True)
        weights_low = (forward_weights / totals).astype(jnp.bfloat16)
        forward_log_total = row_max + jnp.log(totals)
        forward_value_head_split = forward_gathered_values.reshape(
            -1, KEY_VALUE_HEADS, HEAD_DIMENSION
        )
        forward_attended = jnp.einsum(
            "grqk,kgd->qgrd",
            weights_low,
            forward_value_head_split,
            preferred_element_type=jnp.float32,
        )
        forward_attended = forward_attended.reshape(
            count_of_rows, QUERY_HEADS * HEAD_DIMENSION
        ).astype(jnp.bfloat16)
        forward_mixed_rows = layer_input + jnp.dot(
            forward_attended, forward_out_weight, preferred_element_type=jnp.float32
        )
        forward_normed_ffn = rms_scale(
            forward_mixed_rows, forward_gain_ffn.astype(jnp.float32)
        ).astype(jnp.bfloat16)
        forward_gate_value = jnp.dot(
            forward_normed_ffn, forward_gate_weight, preferred_element_type=jnp.float32
        )
        forward_up_value = jnp.dot(
            forward_normed_ffn, forward_up_weight, preferred_element_type=jnp.float32
        )
        forward_hidden = (jax.nn.silu(forward_gate_value) * forward_up_value).astype(jnp.bfloat16)
        layer_output = forward_mixed_rows + jnp.dot(
            forward_hidden, forward_down_weight, preferred_element_type=jnp.float32
        )
        layer_output, kept_state = (
            layer_output,
            (
                layer_input,
                forward_mixed_rows,
                forward_query_rows,
                forward_gathered_keys,
                forward_gathered_values,
                forward_log_total,
                forward_attended,
                forward_gate_value,
                forward_up_value,
            ),
        )
        sent_rows = layer_output.astype(jnp.bfloat16)
        kept_list.append(kept_state)
        sent_list.append(sent_rows)
        if step_index < micro_count:
            received = passed_along(sent_rows, "section", 1)
    back_received = jnp.zeros((count_of_rows, model_width), jnp.bfloat16)
    grad_list = []
    rounded_list = []
    gain_list = []
    operand_list = []
    for step_index in range(micro_count + 1):
        earlier = kept_list[max(step_index - 1, 0)]
        latter = kept_list[min(step_index + 1, micro_count)]
        kept_state = pick(earlier, latter)
        upstream = upstream_all[min(step_index, micro_count - 1)]
        grad_output = jnp.where(first_section, back_received, upstream).astype(jnp.float32)
        grad_input, gain_grads, operands = backward(grad_output, kept_state, fetch())
        grad_rounded = grad_input.astype(jnp.bfloat16)
        grad_list.append(grad_input)
        rounded_list.append(grad_rounded)
        gain_list.append(gain_grads)
        operand_list.append(operands)
        if step_index < micro_count:
            back_received = passed_along(grad_rounded, "section", -1)
    acts_rows = []
    grad_rows = []
    chosen_operands = []
    gain_attn_total = jnp.zeros_like(gain_list[0][0])
    gain_ffn_total = jnp.zeros_like(gain_list[0][1])
    for micro_index in range(micro_count):
        acts_rows.append(pick(sent_list[micro_index], sent_list[micro_index + 1]))
        grad_rows.append(
            jnp.where(
                first_section,
                grad_list[micro_index + 1],
                rounded_list[micro_index].astype(jnp.float32),
            )
        )
        chosen_operands.append(pick(operand_list[micro_index + 1], operand_list[micro_index]))
        chosen_gains = pick(gain_list[micro_index + 1], gain_list[micro_index])
        gain_attn_total = gain_attn_total + chosen_gains[0]
        gain_ffn_total = gain_ffn_total + chosen_gains[1]
    stacked = jax.tree.map(lambda *pieces: jnp.concatenate(pieces, axis=0), *chosen_operands)
    (
        normed_all,
        dquery_all,
        dkey_all,
        dvalue_all,
        attended_all,
        dattn_all,
        normed_ffn_all,
        dgate_all,
        dup_all,
        hidden_all,
        dbranch_all,
    ) = stacked
    query_full = contract(normed_all, dquery_all)
    key_full = contract(normed_all, dkey_all)
    value_full = contract(normed_all, dvalue_all)
    out_full = contract(attended_all, dattn_all)
    gate_full = contract(normed_ffn_all, dgate_all)
    up_full = contract(normed_ffn_all, dup_all)
    down_full = contract(hidden_all, dbranch_all)
    (
        gain_attn_part,
        query_part,
        key_part,
        value_part,
        out_part,
        gain_ffn_part,
        gate_part,
        up_part,
        down_part,
    ) = (
        lax.psum_scatter(
            gain_attn_total.astype(jnp.bfloat16), "fsdp", scatter_dimension=0, tiled=True
        ).astype(jnp.float32),
        lax.psum_scatter(
            query_full.astype(jnp.bfloat16), "fsdp", scatter_dimension=0, tiled=True
        ).astype(jnp.float32),
        lax.psum_scatter(
            key_full.astype(jnp.bfloat16), "fsdp", scatter_dimension=0, tiled=True
        ).astype(jnp.float32),
        lax.psum_scatter(
            value_full.astype(jnp.bfloat16), "fsdp", scatter_dimension=0, tiled=True
        ).astype(jnp.float32),
        lax.psum_scatter(
            out_full.astype(jnp.bfloat16), "fsdp", scatter_dimension=0, tiled=True
        ).astype(jnp.float32),
        lax.psum_scatter(
            gain_ffn_total.astype(jnp.bfloat16), "fsdp", scatter_dimension=0, tiled=True
        ).astype(jnp.float32),
        lax.psum_scatter(
            gate_full.astype(jnp.bfloat16), "fsdp", scatter_dimension=0, tiled=True
        ).astype(jnp.float32),
        lax.psum_scatter(
            up_full.astype(jnp.bfloat16), "fsdp", scatter_dimension=0, tiled=True
        ).astype(jnp.float32),
        lax.psum_scatter(
            down_full.astype(jnp.bfloat16), "fsdp", scatter_dimension=0, tiled=True
        ).astype(jnp.float32),
    )
    results = (
        lax.psum(gain_attn_part.astype(jnp.bfloat16), "ctx").astype(jnp.float32),
        lax.psum(query_part.astype(jnp.bfloat16), "ctx").astype(jnp.float32),
        lax.psum(key_part.astype(jnp.bfloat16), "ctx").astype(jnp.float32),
        lax.psum(value_part.astype(jnp.bfloat16), "ctx").astype(jnp.float32),
        lax.psum(out_part.astype(jnp.bfloat16), "ctx").astype(jnp.float32),
        lax.psum(gain_ffn_part.astype(jnp.bfloat16), "ctx").astype(jnp.float32),
        lax.psum(gate_part.astype(jnp.bfloat16), "ctx").astype(jnp.float32),
        lax.psum(up_part.astype(jnp.bfloat16), "ctx").astype(jnp.float32),
        lax.psum(down_part.astype(jnp.bfloat16), "ctx").astype(jnp.float32),
    )
    local_shape = (1, micro_count, 1, 2, block_size, model_width)
    acts = jnp.stack(acts_rows).reshape(local_shape)
    in_grads = jnp.stack(grad_rows).reshape(local_shape)
    return (
        acts,
        in_grads,
        results[0][None],
        results[1][None],
        results[2][None],
        results[3][None],
        results[4][None],
        results[5][None],
        results[6][None],
        results[7][None],
        results[8][None],
    )


def solution(mesh):
    in_specs = (
        P(None, "fsdp", None, "ctx", None),
        P(None, "fsdp", None, "ctx", None),
        P("section", "fsdp"),
        P("section", "fsdp", None),
        P("section", "fsdp", None),
        P("section", "fsdp", None),
        P("section", "fsdp", None),
        P("section", "fsdp"),
        P("section", "fsdp", None),
        P("section", "fsdp", None),
        P("section", "fsdp", None),
    )
    out_specs = (
        P("section", None, "fsdp", None, "ctx", None),
        P("section", None, "fsdp", None, "ctx", None),
        P("section", "fsdp"),
        P("section", "fsdp", None),
        P("section", "fsdp", None),
        P("section", "fsdp", None),
        P("section", "fsdp", None),
        P("section", "fsdp"),
        P("section", "fsdp", None),
        P("section", "fsdp", None),
        P("section", "fsdp", None),
    )
    return jax.shard_map(
        on_device, mesh=mesh, in_specs=in_specs, out_specs=out_specs, check_vma=False
    )
```

profile of v0, /device:TPU:1, one launch (start us, length us, event | category | flops | bytes accessed | tf_op | source)
XLA Modules:
  0.0 1370.4 jit_solution(15474916029521148382)
XLA Ops:
  25.9 27.3 %all-gather.1 = bf16[1,960,320]{2,0,1:T(2,128)(2,1)S(1)} all-gather(bf16[1,240,320]{2,0,1:T(2,128)(2,1)S(1)} %copy.128), channel_id=3, replica_groups=mesh['section'=2,'ctx'=16,'fsdp'=4] {'fsdp'}, dimensions={1}, use_global_device_ids=true | all-gather | bytes 768000 | tf_op jit(solution)/shard_map/all_gather | solution.py:117
  56.1 26.9 %all_gather.47 = bf16[1536,320]{1,0:T(8,128)(2,1)S(1)} all-gather(bf16[96,320]{1,0:T(8,128)(2,1)S(1)} %convolution_convert_fusion.9), channel_id=1, replica_groups=mesh['section'=2,'ctx'=16,'fsdp'=4] {'ctx'}, dimensions={0}, use_global_device_ids=true | all-gather | bytes 1044480 | tf_op jit(solution)/shard_map/all_gather | solution.py:296
  85.9 15.2 %all-gather.2 = bf16[1,960,320]{2,0,1:T(2,128)(2,1)} all-gather(bf16[1,240,320]{2,0,1:T(2,128)(2,1)S(1)} %copy.131), channel_id=4, replica_groups=mesh['section'=2,'ctx'=16,'fsdp'=4] {'fsdp'}, dimensions={1}, use_global_device_ids=true | all-gather | bytes 768000 | tf_op jit(solution)/shard_map/all_gather | solution.py:116
  105.5 27.7 %all_gather.49 = bf16[1536,320]{1,0:T(8,128)(2,1)S(1)} all-gather(bf16[96,320]{1,0:T(8,128)(2,1)S(1)} %copy.133), channel_id=1, replica_groups=mesh['section'=2,'ctx'=16,'fsdp'=4] {'ctx'}, dimensions={0}, use_global_device_ids=true | all-gather | bytes 1044480 | tf_op jit(solution)/shard_map/all_gather | solution.py:295
  154.9 42.2 %all-gather.19.cloned.1.call-done = bf16[1,960,2560]{2,1,0:T(8,128)(2,1)} async-done(((bf16[1,240,2560]{2,1,0:T(8,128)(2,1)}), bf16[1,960,2560]{2,1,0:T(8,128)(2,1)}) %all-gather.19.cloned.1.call-update) | async-done | bytes 4915216 | tf_op jit(solution)/shard_map/all_gather | solution.py:120
  201.5 51.9 %all-gather.23.cloned.1.call-done = bf16[1,2560,960]{1,2,0:T(8,128)(2,1)} async-done(((bf16[1,640,960]{1,2,0:T(8,128)(2,1)}), bf16[1,2560,960]{1,2,0:T(8,128)(2,1)}) %all-gather.23.cloned.1.call-update) | async-done | bytes 4915216 | tf_op jit(solution)/shard_map/all_gather | solution.py:122
  267.9 26.3 %all_gather.57 = bf16[1536,320]{1,0:T(8,128)(2,1)S(1)} all-gather(bf16[96,320]{1,0:T(8,128)(2,1)S(1)} %copy.138), channel_id=1, replica_groups=mesh['section'=2,'ctx'=16,'fsdp'=4] {'ctx'}, dimensions={0}, use_global_device_ids=true | all-gather | bytes 1044480 | tf_op jit(solution)/shard_map/all_gather | solution.py:295
  299.2 24.0 %all_gather.56 = bf16[1536,320]{1,0:T(8,128)(2,1)} all-gather(bf16[96,320]{1,0:T(8,128)(2,1)S(1)} %convolution_convert_fusion.8), channel_id=1, replica_groups=mesh['section'=2,'ctx'=16,'fsdp'=4] {'ctx'}, dimensions={0}, use_global_device_ids=true | all-gather | bytes 1044480 | tf_op jit(solution)/shard_map/all_gather | solution.py:296
  401.2 31.2 %reduce-scatter.40.cloned.1.call-done = bf16[96,320]{1,0:T(8,128)(2,1)} async-done(((bf16[1536,320]{1,0:T(8,128)(2,1)}), bf16[96,320]{1,0:T(8,128)(2,1)}) %reduce-scatter.40.cloned.1.call-update) | async-done | bytes 61456
  436.7 59.1 %reduce-scatter.42.cloned.1.call-done = bf16[96,320]{1,0:T(8,128)(2,1)} async-done(((bf16[1536,320]{1,0:T(8,128)(2,1)}), bf16[96,320]{1,0:T(8,128)(2,1)}) %reduce-scatter.42.cloned.1.call-update) | async-done | bytes 61456
  502.8 29.4 %all_gather.58 = bf16[1536,320]{1,0:T(8,128)(2,1)} all-gather(bf16[96,320]{1,0:T(8,128)(2,1)S(1)} %convolution_convert_fusion.7), channel_id=1, replica_groups=mesh['section'=2,'ctx'=16,'fsdp'=4] {'ctx'}, dimensions={0}, use_global_device_ids=true | all-gather | bytes 1044480 | tf_op jit(solution)/shard_map/all_gather | solution.py:296
  537.8 24.3 %all_gather.59 = bf16[1536,320]{1,0:T(8,128)(2,1)} all-gather(bf16[96,320]{1,0:T(8,128)(2,1)} %copy.143), channel_id=1, replica_groups=mesh['section'=2,'ctx'=16,'fsdp'=4] {'ctx'}, dimensions={0}, use_global_device_ids=true | all-gather | bytes 1044480 | tf_op jit(solution)/shard_map/all_gather | solution.py:295
  649.3 40.3 %reduce-scatter.44.cloned.1.call-done = bf16[96,320]{1,0:T(8,128)(2,1)} async-done(((bf16[1536,320]{1,0:T(8,128)(2,1)}), bf16[96,320]{1,0:T(8,128)(2,1)}) %reduce-scatter.44.cloned.1.call-update) | async-done | bytes 61456
  693.8 59.2 %reduce-scatter.46.cloned.1.call-done = bf16[96,320]{1,0:T(8,128)(2,1)} async-done(((bf16[1536,320]{1,0:T(8,128)(2,1)}), bf16[96,320]{1,0:T(8,128)(2,1)}) %reduce-scatter.46.cloned.1.call-update) | async-done | bytes 61456
  805.9 53.8 %reduce-scatter.48.cloned.1.call-done = bf16[96,320]{1,0:T(8,128)(2,1)} async-done(((bf16[1536,320]{1,0:T(8,128)(2,1)}), bf16[96,320]{1,0:T(8,128)(2,1)}) %reduce-scatter.48.cloned.1.call-update) | async-done | bytes 61456
  863.6 59.5 %reduce-scatter.50.cloned.1.call-done = bf16[96,320]{1,0:T(8,128)(2,1)} async-done(((bf16[1536,320]{1,0:T(8,128)(2,1)}), bf16[96,320]{1,0:T(8,128)(2,1)}) %reduce-scatter.50.cloned.1.call-update) | async-done | bytes 61456
  963.1 11.2 reduce-scatter.54.cloned.1.call-done
  976.0 56.8 %reduce-scatter.56.cloned.1.call-done = bf16[640,960]{1,0:T(8,128)(2,1)} async-done(((bf16[2560,960]{1,0:T(8,128)(2,1)}), bf16[640,960]{1,0:T(8,128)(2,1)}) %reduce-scatter.56.cloned.1.call-update) | async-done | bytes 1228816
  1035.2 28.8 %reduce-scatter.32.cloned.1.call-done = bf16[240,960]{1,0:T(8,128)(2,1)} async-done(((bf16[960,960]{1,0:T(8,128)(2,1)}), bf16[240,960]{1,0:T(8,128)(2,1)}) %reduce-scatter.32.cloned.1.call-update) | async-done | bytes 460816 | tf_op jit(solution)/shard_map/reduce_scatter | solution.py:428
  1064.1 31.2 %reduce-scatter.34.cloned.1.call-done = bf16[240,960]{1,0:T(8,128)(2,1)} async-done(((bf16[960,960]{1,0:T(8,128)(2,1)}), bf16[240,960]{1,0:T(8,128)(2,1)}) %reduce-scatter.34.cloned.1.call-update) | async-done | bytes 460816 | tf_op jit(solution)/shard_map/reduce_scatter | solution.py:437
  1095.3 54.8 %reduce-scatter.36.cloned.1.call-done = bf16[240,2560]{1,0:T(8,128)(2,1)} async-done(((bf16[960,2560]{1,0:T(8,128)(2,1)}), bf16[240,2560]{1,0:T(8,128)(2,1)}) %reduce-scatter.36.cloned.1.call-update) | async-done | bytes 1228816 | tf_op jit(solution)/shard_map/reduce_scatter | solution.py:443
  1150.1 54.9 %reduce-scatter.38.cloned.1.call-done = bf16[240,2560]{1,0:T(8,128)(2,1)} async-done(((bf16[960,2560]{1,0:T(8,128)(2,1)}), bf16[240,2560]{1,0:T(8,128)(2,1)}) %reduce-scatter.38.cloned.1.call-update) | async-done | bytes 1228816 | tf_op jit(solution)/shard_map/reduce_scatter | solution.py:446
  1219.3 29.4 %all-reduce.16 = (bf16[1,240]{1,0:T(2,128)(2,1)S(1)}, bf16[1,240]{1,0:T(2,128)(2,1)S(1)}) all-reduce(bf16[1,240]{1,0:T(2,128)(2,1)S(1)} %broadcast_in_dim.83, bf16[1,240]{1,0:T(2,128)(2,1)S(1)} %broadcast_in_dim.179), channel_id=1, replica_groups=mesh['section'=2,'ctx'=16,'fsdp'=4] {'ctx'}, use_global_device_ids=true, to_apply=%region_37.38 | all-reduce | flops 480 | bytes 1920 | tf_op jit(solution)/shard_map/psum | solution.py:454
  1251.9 97.6 %all-reduce.22.cloned.1.call-done = (bf16[1,240,960]{2,1,0:T(8,128)(2,1)}, bf16[1,240,320]{1,2,0:T(8,128)(2,1)}, bf16[1,240,320]{1,2,0:T(8,128)(2,1)}, bf16[1,24...) async-done(((bf16[1,240,960]{2,1,0:T(8,128)(2,1)}, bf16[1,240,320]{1,2,0:T(8,128)(2,1)}, ...) | async-done | bytes 4915216 | tf_op jit(solution)/shard_map/psum | solution.py:455
  (613 shorter events, 388.8 us)
Async XLA Ops:
  7.2 128.5 %all-gather.15.cloned.1.call-start = ((), (), s32[]{:S(2)}) async-start(), calls=%async_computation.17 | async-start | bytes 2457600 | tf_op jit(solution)/shard_map/all_gather | solution.py:115
  7.9 140.0 %all-gather.17.cloned.1.call-start = ((), (), s32[]{:S(2)}) async-start(), calls=%async_computation.18 | async-start | bytes 2457600 | tf_op jit(solution)/shard_map/all_gather | solution.py:118
  8.7 141.5 %all-gather.21.cloned.1.call-start = ((), (), s32[]{:S(2)}) async-start(), calls=%async_computation.20 | async-start | bytes 6144000 | tf_op jit(solution)/shard_map/all_gather | solution.py:121
  9.4 187.8 %all-gather.19.cloned.1.call-start = ((), (), s32[]{:S(2)}) async-start(), calls=%async_computation.19 | async-start | bytes 6144000 | tf_op jit(solution)/shard_map/all_gather | solution.py:120
  10.0 243.4 %all-gather.23.cloned.1.call-start = ((), (), s32[]{:S(2)}) async-start(), calls=%async_computation.21 | async-start | bytes 6144000 | tf_op jit(solution)/shard_map/all_gather | solution.py:122
  10.6 421.8 %reduce-scatter.40.cloned.1.call-start = ((), (), s32[]{:S(2)}) async-start(), calls=%async_computation.22 | async-start | bytes 1253376
  258.0 8.1 collective-permute-start
  374.7 121.1 %reduce-scatter.42.cloned.1.call-start = ((), (), s32[]{:S(2)}) async-start(), calls=%async_computation.23 | async-start | bytes 1253376
  383.9 305.7 %reduce-scatter.44.cloned.1.call-start = ((), (), s32[]{:S(2)}) async-start(), calls=%async_computation.24 | async-start | bytes 1253376
  389.4 107.6 %collective-permute-start.1 = (bf16[96,960]{1,0:T(8,128)(2,1)}, bf16[96,960]{1,0:T(8,128)(2,1)}, u32[]{:S(2)}, u32[]{:S(2)}) collective-permute-start(bf16[96,960]{1,0:T(8,128)(2,1)} %get-tuple-element.148), channel_id=1, source_target_pairs={{0,64},{1,65},{2,66},{3,67},{4,68},{5,69},{6,70},{7,71},{8,72},{9,... | collective-permute-start | bytes 552968 | tf_op jit(solution)/shard_map/ppermute | solution.py:21
  579.9 20.0 %collective-permute-start.2 = (bf16[96,960]{1,0:T(8,128)(2,1)}, bf16[96,960]{1,0:T(8,128)(2,1)}, u32[]{:S(2)}, u32[]{:S(2)}) collective-permute-start(bf16[96,960]{1,0:T(8,128)(2,1)} %fusion.240), channel_id=1, source_target_pairs={{64,0},{65,1},{66,2},{67,3},{68,4},{69,5},{70,6},{71,7},{72,8},{73... | collective-permute-start | bytes 552968 | tf_op jit(solution)/shard_map/ppermute | solution.py:21
  632.2 120.8 %reduce-scatter.46.cloned.1.call-start = ((), (), s32[]{:S(2)}) async-start(), calls=%async_computation.25 | async-start | bytes 1253376
  641.5 218.2 %reduce-scatter.48.cloned.1.call-start = ((), (), s32[]{:S(2)}) async-start(), calls=%async_computation.26 | async-start | bytes 1253376
  759.0 8.5 collective-permute-start.3
  796.7 126.5 %reduce-scatter.50.cloned.1.call-start = ((), (), s32[]{:S(2)}) async-start(), calls=%async_computation.27 | async-start | bytes 1253376
  804.0 157.3 %reduce-scatter.52.cloned.1.call-start = ((), (), s32[]{:S(2)}) async-start(), calls=%async_computation.28 | async-start | bytes 921600
  863.3 111.0 %reduce-scatter.54.cloned.1.call-start = ((), (), s32[]{:S(2)}) async-start(), calls=%async_computation.29 | async-start | bytes 921600
  926.7 106.2 %reduce-scatter.56.cloned.1.call-start = ((), (), s32[]{:S(2)}) async-start(), calls=%async_computation.30 | async-start | bytes 6553600
  939.3 124.7 %reduce-scatter.32.cloned.1.call-start = ((), (), s32[]{:S(2)}) async-start(), calls=%async_computation.13 | async-start | bytes 2457600 | tf_op jit(solution)/shard_map/reduce_scatter | solution.py:428
  949.5 145.8 %reduce-scatter.34.cloned.1.call-start = ((), (), s32[]{:S(2)}) async-start(), calls=%async_computation.14 | async-start | bytes 2457600 | tf_op jit(solution)/shard_map/reduce_scatter | solution.py:437
  952.1 198.0 %reduce-scatter.36.cloned.1.call-start = ((), (), s32[]{:S(2)}) async-start(), calls=%async_computation.15 | async-start | bytes 6144000 | tf_op jit(solution)/shard_map/reduce_scatter | solution.py:443
  957.1 247.8 %reduce-scatter.38.cloned.1.call-start = ((), (), s32[]{:S(2)}) async-start(), calls=%async_computation.16 | async-start | bytes 6144000 | tf_op jit(solution)/shard_map/reduce_scatter | solution.py:446
  960.9 244.8 %copy-start.60 = (f32[96,960]{1,0:T(8,128)S(1)}, f32[96,960]{1,0:T(8,128)}, u32[]{:S(2)}) copy-start(f32[96,960]{1,0:T(8,128)} %get-tuple-element.146) | copy-start | bytes 1105924
  960.9 388.6 %all-reduce.22.cloned.1.call-start = ((), (), s32[]{:S(2)}) async-start(), calls=%async_computation.31 | async-start | bytes 9994240 | tf_op jit(solution)/shard_map/psum | solution.py:455
  (164 other events, 3183.2 us)
Sparse Core Ops, SparseCore 0:
  9.7 43.7 all-gather.14
  55.2 29.7 all-gather.16
  86.6 55.3 all-gather.20
  143.6 53.5 all-gather.18
  198.7 54.6 all-gather.22
  374.8 57.5 reduce-scatter.39
  435.4 60.4 reduce-scatter.41
  632.3 57.2 reduce-scatter.43
  692.6 60.4 reduce-scatter.45
  796.8 62.8 reduce-scatter.47
  862.6 60.4 reduce-scatter.49
  926.0 23.2 reduce-scatter.51
  952.3 21.9 reduce-scatter.53
  976.6 56.2 reduce-scatter.55
  1035.7 28.3 reduce-scatter.31
  1066.9 28.3 reduce-scatter.33
  1097.6 52.4 reduce-scatter.35
  1152.5 52.4 reduce-scatter.37
  1209.2 140.2 all-reduce.21
where the time goes:
time: 1380 us; the launch traced here: 1370 us
  waiting for transfers between devices  739 us (54%)
  blocking collectives  247 us (18%)
  matrix products  191 us (14%)
  local copies, waits for them, and re-layouts  94.3 us (7%)
  other arithmetic  64.8 us (5%)
  between operations  18.4 us (1%)
  starting transfers between devices  16.1 us (1%)
    unnamed x28, waiting for transfers between devices  374 us
    psum x1, waiting for transfers between devices, on_device(): lax.psum(query_part.astype(jnp.bfloat16), 'ctx').astype(jnp.float32)  97.6 us
    all_gather x3, blocking collectives, on_device(): lax.all_gather(value_new, 'ctx', axis=0, tiled=True)  80.4 us
    all_gather x3, blocking collectives, on_device(): forward_gathered_keys = lax.all_gather(key_new, 'ctx', axis=0, tiled=True)  78.3 us
    reduce_scatter x1, waiting for transfers between devices, on_device(): lax.psum_scatter(up_full.astype(jnp.bfloat16), 'fsdp', scatter_dimension=...  54.9 us
    reduce_scatter x1, waiting for transfers between devices, on_device(): lax.psum_scatter(gate_full.astype(jnp.bfloat16), 'fsdp', scatter_dimensio...  54.8 us
    unnamed x357, local copies, waits for them, and re-layouts  52.7 us
    all_gather x1, waiting for transfers between devices, on_device(): lax.all_gather(w_down[0], 'fsdp', axis=0, tiled=True)  51.9 us
  transfers between devices with their start and end apart: 23, of which 16 were waited for; matrix products, arithmetic and copies ran while one was open for 13% of the time, Pallas kernels for 0%

commit v1 on v0

v1 whole, which is shorter than its diff:
```python
import functools

import jax
import jax.numpy as jnp
from jax import lax
from jax.experimental import pallas as pl
from jax.experimental.pallas import tpu as pltpu
from jax.sharding import PartitionSpec as P

WIDTH = 960
HEADS = 15
KV_HEADS = 5
GROUP = HEADS // KV_HEADS
HEAD = 64
FF = 2560
BLK = 48
ROWS = 2 * BLK
CTX = 16
FSDP = 4
LENGTH = ROWS * CTX
SHARD = WIDTH // FSDP
FF_SHARD = FF // FSDP
QK_COLS = (HEADS + KV_HEADS) * HEAD
QKV_COLS = QK_COLS + KV_HEADS * HEAD
SLICE = 16
SLICES = SHARD // SLICE
DOWN_SLICE = FF_SHARD // CTX
TILE = 256

EPSILON = 1e-05
THETA = 10000.0
MASKED = -1e30

F32 = jnp.float32
BF16 = jnp.bfloat16


def sds(shape, dtype):
    return jax.ShapeDtypeStruct(shape, dtype)


def call(body, outs, *args, scratch=(), flops=0):
    size = sum(a.size * a.dtype.itemsize for a in (*args, *outs))
    return pl.pallas_call(
        body,
        out_shape=outs,
        scratch_shapes=list(scratch),
        compiler_params=pltpu.CompilerParams(vmem_limit_bytes=56 * 1024 * 1024),
        cost_estimate=pl.CostEstimate(flops=flops, bytes_accessed=size, transcendentals=0),
    )(*args)


def dot(a, b):
    return jnp.dot(a, b, preferred_element_type=F32)


def dot_t(a, b):
    return lax.dot_general(a, b, (((1,), (1,)), ((), ())), preferred_element_type=F32)


def t_dot(a, b):
    return lax.dot_general(a, b, (((0,), (0,)), ((), ())), preferred_element_type=F32)


def inverse_rms(x):
    return lax.rsqrt(jnp.mean(x * x, axis=-1, keepdims=True) + EPSILON)


def norm_backward(d, x, gain):
    r = inverse_rms(x)
    n = x * r
    t = d * gain
    return (t - n * jnp.mean(t * n, axis=-1, keepdims=True)) * r, jnp.sum(d * n, axis=0, keepdims=True)


def swap_halves(x):
    cols = x.shape[1]
    lane = lax.broadcasted_iota(jnp.int32, x.shape, 1)
    ahead = pltpu.roll(x, cols - HEAD // 2, 1)
    behind = pltpu.roll(x, HEAD // 2, 1)
    return jnp.where(lane % HEAD < HEAD // 2, ahead, behind)


def source_block(b):
    return (b, 0) if b < CTX else (2 * CTX - 1 - b, 1)


def qkv_body(count, *refs):
    parts, (gain, w, cos, sin) = refs[:count], refs[count : count + 4]
    x_out, a_out, send = refs[count + 4 :]
    x = parts[0][...].astype(F32)
    for part in parts[1:]:
        x = x + part[...].astype(F32)
    low = x.astype(BF16)
    x_out[...] = low
    x = low.astype(F32)
    a = x * inverse_rms(x) * gain[...]
    for k in range(FSDP):
        a_out[k] = a[:, k * SHARD : (k + 1) * SHARD].astype(BF16)
    out = dot(a.astype(BF16), w[...])
    qk = out[:, :QK_COLS]
    qk = qk * cos[...] + swap_halves(qk) * sin[...]
    v = out[:, QK_COLS:]
    for h in range(HEADS):
        g = h // GROUP
        q_h = qk[:, h * HEAD : (h + 1) * HEAD]
        k_g = qk[:, (HEADS + g) * HEAD : (HEADS + g + 1) * HEAD]
        v_g = v[:, g * HEAD : (g + 1) * HEAD]
        send[h, 0:ROWS] = jnp.concatenate([q_h, k_g], axis=1).astype(BF16)
        send[h, ROWS:] = jnp.concatenate([v_g[:BLK], v_g[BLK:]], axis=1).astype(BF16)
    for h in range(HEADS, CTX):
        send[h] = jnp.zeros(send.shape[1:], BF16)


def unpack_heads(recv, q_s, k_s, v_s):
    for b in range(2 * CTX):
        c, half = source_block(b)
        rows = slice(b * BLK, (b + 1) * BLK)
        qk = recv[c, half * BLK : (half + 1) * BLK, :].astype(F32)
        v = recv[c, ROWS : ROWS + BLK, :].astype(F32)
        q_s[rows, :] = qk[:, :HEAD].astype(BF16)
        k_s[rows, :] = qk[:, HEAD:].astype(BF16)
        v_s[rows, :] = v[:, half * HEAD : (half + 1) * HEAD].astype(BF16)


def probabilities(q, keys, start):
    scores = dot_t(q, keys)
    row = lax.broadcasted_iota(jnp.int32, scores.shape, 0) + start
    col = lax.broadcasted_iota(jnp.int32, scores.shape, 1)
    scores = jnp.where(col <= row, scores, MASKED)
    weights = jnp.exp(scores - jnp.max(scores, axis=-1, keepdims=True))
    return weights / jnp.sum(weights, axis=-1, keepdims=True)


def attend_body(recv, send, q_s, k_s, v_s, out_s):
    unpack_heads(recv, q_s, k_s, v_s)
    for i in range(LENGTH // TILE):
        start, stop = i * TILE, (i + 1) * TILE
        p = probabilities(q_s[start:stop, :], k_s[:stop, :], start)
        out_s[start:stop, :] = dot(p.astype(BF16), v_s[:stop, :])
    for c in range(CTX):
        last = 2 * CTX - 1 - c
        pair = [out_s[c * BLK : (c + 1) * BLK, :], out_s[last * BLK : (last + 1) * BLK, :]]
        send[c] = jnp.concatenate(pair, axis=1).astype(BF16)


def mix_body(x, recv, w_out, gain, mixed_out, b_out, att_out, att_s):
    for h in range(HEADS):
        pair = recv[h].astype(F32)
        cols = slice(h * HEAD, (h + 1) * HEAD)
        att_s[0:BLK, cols] = pair[:, :HEAD].astype(BF16)
        att_s[BLK:, cols] = pair[:, HEAD:].astype(BF16)
    att = att_s[...]
    for k in range(FSDP):
        att_out[k] = att_s[:, k * SHARD : (k + 1) * SHARD]
    mixed = x[...].astype(F32) + dot(att, w_out[...])
    mixed_out[...] = mixed
    b_out[...] = (mixed * inverse_rms(mixed) * gain[...]).astype(BF16)


def spread(total, outs):
    outs[0][...] = total[0:ROWS]
    for k in range(1, FSDP):
        outs[k][...] = total[k * ROWS : (k + 1) * ROWS].astype(BF16)


def ffn_body(*refs):
    parts, (w_gu, w_down), (gate_out, up_out), outs = refs[:4], refs[4:6], refs[6:8], refs[8:12]
    rows = jnp.concatenate([p[...] for p in parts], axis=0)
    gate = dot(rows, w_gu[:, :FF_SHARD])
    up = dot(rows, w_gu[:, FF_SHARD:])
    gate_out[...] = gate
    up_out[...] = up
    hidden = (gate * jax.nn.sigmoid(gate) * up).astype(BF16)
    spread(dot(hidden, w_down[...]), outs)


def ffn_back_body(*refs):
    parts, (gate_ref, up_ref, w_gu, w_down) = refs[:4], refs[4:8]
    hidden_out, d_gu_out = refs[8:10]
    outs = refs[10:14]
    rows = jnp.concatenate([p[...] for p in parts], axis=0)
    gate, up = gate_ref[...], up_ref[...]
    sig = jax.nn.sigmoid(gate)
    act = gate * sig
    hidden_out[...] = (act * up).astype(BF16)
    d_hidden = dot_t(rows, w_down[...])
    d_gate = (d_hidden * up * (sig * (1.0 + gate * (1.0 - sig)))).astype(BF16)
    d_up = (d_hidden * act).astype(BF16)
    d_gu_out[:, :FF_SHARD] = d_gate
    d_gu_out[:, FF_SHARD:] = d_up
    spread(dot_t(d_gate, w_gu[:, :FF_SHARD]) + dot_t(d_up, w_gu[:, FF_SHARD:]), outs)


def mix_back_body(g, p0, p1, p2, p3, mixed, gain, w_out, d_mixed_out, ga_out, gain_out, send):
    d_b = p0[...] + p1[...].astype(F32) + p2[...].astype(F32) + p3[...].astype(F32)
    d_in, d_gain = norm_backward(d_b, mixed[...], gain[...])
    d_mixed = g[...].astype(F32) + d_in
    d_mixed_out[...] = d_mixed
    gain_out[...] = d_gain
    ga = d_mixed.astype(BF16)
    ga_out[...] = ga
    d_att = dot_t(ga, w_out[...])
    for h in range(HEADS):
        piece = d_att[:, h * HEAD : (h + 1) * HEAD]
        send[h] = jnp.concatenate([piece[:BLK], piece[BLK:]], axis=1).astype(BF16)
    for h in range(HEADS, CTX):
        send[h] = jnp.zeros(send.shape[1:], BF16)


def attend_back_body(recv, d_recv, cos, sin, send, q_s, k_s, v_s, d_s, dq_s, dk_s, dv_s):
    unpack_heads(recv, q_s, k_s, v_s)
    for b in range(2 * CTX):
        c, half = source_block(b)
        pair = d_recv[c].astype(F32)
        d_s[b * BLK : (b + 1) * BLK, :] = pair[:, half * HEAD : (half + 1) * HEAD].astype(BF16)
    dk_s[...] = jnp.zeros(dk_s.shape, F32)
    dv_s[...] = jnp.zeros(dv_s.shape, F32)
    for i in range(LENGTH // TILE):
        start, stop = i * TILE, (i + 1) * TILE
        q, d_att = q_s[start:stop, :], d_s[start:stop, :]
        p = probabilities(q, k_s[:stop, :], start)
        d_p = dot_t(d_att, v_s[:stop, :])
        inner = jnp.sum(p * d_p, axis=-1, keepdims=True)
        d_scores = (p * (d_p - inner)).astype(BF16)
        dq_s[start:stop, :] = dot(d_scores, k_s[:stop, :])
        dk_s[:, :stop] += t_dot(q, d_scores)
        dv_s[:, :stop] += t_dot(d_att, p.astype(BF16))
    dk = dk_s[...].T
    dv = dv_s[...].T
    both = jnp.concatenate([dq_s[...] * (HEAD**-0.5), dk], axis=1)
    both = both * cos[...] + swap_halves(both) * sin[...]
    for c in range(CTX):
        last = 2 * CTX - 1 - c
        send[c, 0:BLK] = both[c * BLK : (c + 1) * BLK].astype(BF16)
        send[c, BLK:ROWS] = both[last * BLK : (last + 1) * BLK].astype(BF16)
        pair = [dv[c * BLK : (c + 1) * BLK], dv[last * BLK : (last + 1) * BLK]]
        send[c, ROWS:] = jnp.concatenate(pair, axis=1).astype(BF16)


def qkv_back_body(recv, d_mixed, x_ref, gain, w, gain_ffn, d_x_out, low_out, rows_out):
    for g in range(KV_HEADS):
        d_k = jnp.zeros((ROWS, HEAD), F32)
        d_v = jnp.zeros((BLK, 2 * HEAD), F32)
        for h in range(g * GROUP, (g + 1) * GROUP):
            qk = recv[h, 0:ROWS].astype(F32)
            rows_out[0:ROWS, h * HEAD : (h + 1) * HEAD] = qk[:, :HEAD].astype(BF16)
            d_k = d_k + qk[:, HEAD:]
            d_v = d_v + recv[h, ROWS:].astype(F32)
        k_cols = slice((HEADS + g) * HEAD, (HEADS + g + 1) * HEAD)
        v_cols = slice(QK_COLS + g * HEAD, QK_COLS + (g + 1) * HEAD)
        rows_out[0:ROWS, k_cols] = d_k.astype(BF16)
        rows_out[0:BLK, v_cols] = d_v[:, :HEAD].astype(BF16)
        rows_out[BLK:ROWS, v_cols] = d_v[:, HEAD:].astype(BF16)
    d_a = dot_t(rows_out[0:ROWS, :], w[...])
    d_in, d_gain = norm_backward(d_a, x_ref[...].astype(F32), gain[...])
    d_x = d_mixed[...] + d_in
    d_x_out[...] = d_x
    low_out[...] = d_x.astype(BF16)
    pad = jnp.zeros((6, WIDTH), F32)
    gains = jnp.concatenate([d_gain, gain_ffn[...], pad, jnp.zeros((8, WIDTH), F32)], axis=0)
    rows_out[ROWS:, :] = jnp.concatenate([gains, jnp.zeros((16, QKV_COLS - WIDTH), F32)], axis=1).astype(BF16)


def shifted(x, axis, distance):
    n = lax.axis_size(axis)
    return lax.ppermute(x, axis, [(i, (i + distance) % n) for i in range(n)])


def around(x):
    return [x] + [shifted(x, "fsdp", k) for k in range(1, FSDP)]


def back_around(parts):
    return [parts[0]] + [shifted(parts[k], "fsdp", -k) for k in range(1, FSDP)]


def exchange_blocks(blocks, index):
    pick = lambda k: lax.dynamic_index_in_dim(blocks, (index + k) % FSDP, 0, keepdims=False)
    return [pick(0)] + [shifted(pick(k), "fsdp", k) for k in range(1, FSDP)]


def swap_sections(x):
    return lax.ppermute(x, "section", [(0, 1), (1, 0)])


def all_to_all(x, axis):
    return lax.all_to_all(x, axis, 0, 0)


def on_device(
    tokens,
    cotangent,
    norm_attn,
    w_query,
    key_projection,
    value_projection,
    w_out,
    norm_ffn,
    w_gate,
    w_up,
    w_down,
):
    section = lax.axis_index("section")
    ctx = lax.axis_index("ctx")
    fsdp = lax.axis_index("fsdp")
    first = section == 0

    def my_slice(rows):
        padded = jnp.pad(rows, ((0, CTX * SLICE - SHARD), (0, 0)))
        return lax.dynamic_slice_in_dim(padded, ctx * SLICE, SLICE, 0)

    gains = jnp.stack([norm_attn[0], norm_ffn[0]])
    gains = lax.all_gather(gains, ("section", "fsdp")).reshape(2, FSDP, 2, SHARD)
    gains = gains.transpose(0, 2, 1, 3).reshape(2, 2, 1, WIDTH).astype(F32)

    qkv_slice = my_slice(jnp.concatenate([w_query[0], key_projection[0], value_projection[0]], axis=1))
    qkv_slices = all_to_all(
        jnp.broadcast_to(qkv_slice[None], (2 * FSDP, SLICE, QKV_COLS)), ("section", "fsdp")
    ).reshape(2, FSDP, SLICE, QKV_COLS)

    out_slice = my_slice(w_out[0])
    gate_slice = my_slice(w_gate[0]).reshape(SLICE, FSDP, FF_SHARD)
    up_slice = my_slice(w_up[0]).reshape(SLICE, FSDP, FF_SHARD)
    rest = jnp.concatenate(
        [jnp.broadcast_to(out_slice[:, None], (SLICE, FSDP, WIDTH)), gate_slice, up_slice], axis=2
    ).transpose(1, 0, 2)
    rest = jnp.broadcast_to(rest[None], (2,) + rest.shape).reshape((2 * FSDP,) + rest.shape[1:])
    rest_slices = all_to_all(rest, ("section", "fsdp")).reshape((2, FSDP) + rest.shape[1:])

    down_slice = lax.dynamic_slice_in_dim(w_down[0], ctx * DOWN_SLICE, DOWN_SLICE, 0)
    down_other = swap_sections(down_slice)
    down_slices = (jnp.where(first, down_slice, down_other), jnp.where(first, down_other, down_slice))

    def whole(slices):
        gathered = lax.all_gather(slices, "ctx")[:SLICES]
        return gathered.transpose(1, 0, 2, 3).reshape(WIDTH, slices.shape[-1])

    qkv_weights, out_weights, gu_weights, down_weights = [], [], [], []
    for layer in range(2):
        qkv_weights.append(whole(qkv_slices[layer]))
        both = whole(rest_slices[layer])
        out_weights.append(both[:, :WIDTH])
        gu_weights.append(both[:, WIDTH:])
        down_weights.append(lax.all_gather(down_slices[layer], "ctx", tiled=True))

    inverse = THETA ** (-(jnp.arange(HEAD // 2, dtype=F32) * 2.0) / HEAD)

    def tables(positions):
        angles = positions.astype(F32)[:, None] * inverse[None, :]
        return jnp.cos(angles), jnp.sin(angles)

    offset = jnp.arange(BLK, dtype=jnp.int32)
    own = jnp.concatenate([ctx * BLK + offset, (2 * CTX - 1 - ctx) * BLK + offset])
    cos, sin = tables(own)
    scale = jnp.where(jnp.arange(QK_COLS) < HEADS * HEAD, HEAD**-0.5, 1.0)[None, :]
    cos_own = jnp.tile(jnp.concatenate([cos, cos], axis=1), (1, HEADS + KV_HEADS)) * scale
    sin_own = jnp.tile(jnp.concatenate([-sin, sin], axis=1), (1, HEADS + KV_HEADS)) * scale
    cos, sin = tables(jnp.arange(LENGTH, dtype=jnp.int32))
    cos_all = jnp.concatenate([cos, cos] * 2, axis=1)
    sin_all = jnp.concatenate([sin, -sin] * 2, axis=1)

    my_rows = lax.dynamic_index_in_dim(tokens, section, 0).reshape(ROWS, WIDTH)
    my_cotangent = lax.dynamic_index_in_dim(cotangent, section, 0).reshape(ROWS, WIDTH)

    row_f32, row_bf16 = sds((ROWS, WIDTH), F32), sds((ROWS, WIDTH), BF16)
    heads_shape = sds((CTX, ROWS + BLK, 2 * HEAD), BF16)
    att_shape = sds((CTX, BLK, 2 * HEAD), BF16)
    blocks_shape = sds((FSDP, ROWS, SHARD), BF16)
    seq = lambda dtype: pltpu.VMEM((LENGTH, HEAD), dtype)
    partials = [row_f32] + [row_bf16] * 3
    ff_f32, ff_bf16 = sds((FSDP * ROWS, FF_SHARD), F32), sds((FSDP * ROWS, FF_SHARD), BF16)

    kept = []
    parts = [my_rows]
    for layer in range(2):
        gain_attn, gain_ffn = gains[layer]
        x, a_blocks, send = call(
            functools.partial(qkv_body, len(parts)),
            [row_bf16, blocks_shape, heads_shape],
            *parts, gain_attn, qkv_weights[layer], cos_own, sin_own,
            flops=2 * ROWS * WIDTH * QKV_COLS,
        )
        heads = all_to_all(send, "ctx")
        send = call(
            attend_body, [att_shape], heads,
            scratch=[seq(BF16), seq(BF16), seq(BF16), seq(F32)],
            flops=2 * LENGTH * LENGTH * HEAD,
        )[0]
        mixed, b, att_blocks = call(
            mix_body, [row_f32, row_bf16, blocks_shape],
            x, all_to_all(send, "ctx"), out_weights[layer], gain_ffn,
            scratch=[pltpu.VMEM((ROWS, WIDTH), BF16)],
            flops=2 * ROWS * WIDTH * WIDTH,
        )
        b_all = around(b)
        gate, up, *outs = call(
            ffn_body, [ff_f32, ff_f32] + partials,
            *b_all, gu_weights[layer], down_weights[layer],
            flops=2 * FSDP * ROWS * WIDTH * FF_SHARD * 3,
        )
        parts = [mixed] + back_around(outs)
        kept.append((x, a_blocks, heads, mixed, att_blocks, b_all, gate, up))
    last = parts[0]
    for part in parts[1:]:
        last = last + part.astype(F32)
    first_acts, last_acts = kept[1][0], last.astype(BF16)

    g, g_low = my_cotangent, my_cotangent
    grads = [None, None]
    d_inputs = [None, None]
    for layer in (1, 0):
        gain_attn, gain_ffn = gains[layer]
        x, a_blocks, heads, mixed, att_blocks, b_all, gate, up = kept[layer]
        g_all = around(g_low)
        hidden, d_gu, *outs = call(
            ffn_back_body, [ff_bf16, sds((FSDP * ROWS, 2 * FF_SHARD), BF16)] + partials,
            *g_all, gate, up, gu_weights[layer], down_weights[layer],
            flops=2 * FSDP * ROWS * WIDTH * FF_SHARD * 3,
        )
        d_mixed, ga, d_gain_ffn, send = call(
            mix_back_body, [row_f32, row_bf16, sds((1, WIDTH), F32), att_shape],
            g, *back_around(outs), mixed, gain_ffn, out_weights[layer],
            flops=2 * ROWS * WIDTH * WIDTH,
        )
        send = call(
            attend_back_body, [heads_shape],
            heads, all_to_all(send, "ctx"), cos_all, sin_all,
            scratch=[seq(BF16)] * 4 + [seq(F32)] + [pltpu.VMEM((HEAD, LENGTH), F32)] * 2,
            flops=5 * LENGTH * LENGTH * HEAD,
        )[0]
        d_x, d_low, d_rows = call(
            qkv_back_body, [row_f32, row_bf16, sds((ROWS + 16, QKV_COLS), BF16)],
            all_to_all(send, "ctx"), d_mixed, x, gain_attn, qkv_weights[layer], d_gain_ffn,
            flops=2 * ROWS * WIDTH * QKV_COLS,
        )

        grad_gu = t_dot(jnp.concatenate(b_all), d_gu).astype(BF16)
        grad_down = t_dot(hidden, jnp.concatenate(g_all)).astype(BF16)
        grad_gu = grad_gu.reshape(FSDP, SLICES, SLICE, 2 * FF_SHARD).transpose(1, 0, 2, 3)
        grad_gu = jnp.pad(grad_gu, ((0, CTX - SLICES), (0, 0), (0, 0), (0, 0)))
        grad_gu = lax.psum_scatter(
            grad_gu.reshape(CTX * FSDP * SLICE, 2 * FF_SHARD), "ctx", scatter_dimension=0, tiled=True
        ).reshape(FSDP, SLICE, 2 * FF_SHARD)
        gu_slices = jnp.stack(exchange_blocks(grad_gu, fsdp))
        grad_down = lax.psum_scatter(grad_down, "ctx", scatter_dimension=0, tiled=True)

        a_cols = jnp.concatenate(exchange_blocks(a_blocks, fsdp))
        att_cols = jnp.concatenate(exchange_blocks(att_blocks, fsdp))
        ga_all = jnp.concatenate(around(ga))
        rows_all = jnp.stack(around(d_rows))
        grad_qkv = t_dot(a_cols, rows_all[:, :ROWS].reshape(FSDP * ROWS, QKV_COLS))
        grad_out = t_dot(att_cols, ga_all)
        gain_rows = rows_all[:, ROWS : ROWS + 2, :WIDTH].astype(F32).sum(axis=0)
        gain_rows = lax.dynamic_slice_in_dim(gain_rows, fsdp * SHARD, SHARD, 1)
        gain_rows = jnp.pad(gain_rows, ((0, SLICE - 2), (0, QKV_COLS - SHARD)))
        grad_qkv = jnp.concatenate([grad_qkv, gain_rows]).astype(BF16)
        grad_out = jnp.pad(grad_out, ((0, SLICE), (0, 0))).astype(BF16)

        def scatter(rows):
            arrived = all_to_all(rows.reshape(CTX, SLICE, rows.shape[1]), "ctx")
            return arrived.astype(F32).sum(axis=0).astype(BF16)

        grads[layer] = (gu_slices, grad_down, scatter(grad_out), scatter(grad_qkv))
        d_inputs[layer] = (d_x, d_low)
        g, g_low = d_low, d_low

    def across(zero, one):
        keep, give = jnp.where(first, zero, one), jnp.where(first, one, zero)
        return (keep.astype(F32) + swap_sections(give).astype(F32)).astype(BF16)

    gu_slices, down_slice, out_slice, qkv_slice = [across(zero, one) for zero, one in zip(*grads)]
    gu = lax.all_gather(gu_slices, "ctx")[:SLICES]
    down = lax.all_gather(down_slice, "ctx", tiled=True).astype(F32)
    out = lax.all_gather(out_slice, "ctx", tiled=True)[:SHARD].astype(F32)
    qkv = lax.all_gather(qkv_slice, "ctx", tiled=True)
    order = (fsdp - jnp.arange(FSDP)) % FSDP
    gu = gu[:, order].transpose(0, 2, 1, 3).reshape(SHARD, FSDP, 2, FF_SHARD).astype(F32)
    gate_grad = gu[:, :, 0].reshape(SHARD, FF)
    up_grad = gu[:, :, 1].reshape(SHARD, FF)
    gain_rows = qkv[SHARD : SHARD + 2, :SHARD].astype(F32)
    qkv = qkv[:SHARD].astype(F32)

    other_acts = swap_sections(jnp.where(first, last_acts, first_acts))
    mine_acts = jnp.where(first, first_acts, last_acts)
    d_zero, d_one = d_inputs[0][0], d_inputs[1][1].astype(F32)
    other_grads = swap_sections(jnp.where(first, d_one, d_zero))
    mine_grads = jnp.where(first, d_zero, d_one)

    def by_micro(mine, other):
        pair = jnp.stack([jnp.where(first, mine, other), jnp.where(first, other, mine)])
        return pair.reshape(1, 2, 1, 2, BLK, WIDTH)

    kv = KV_HEADS * HEAD
    return (
        by_micro(mine_acts, other_acts),
        by_micro(mine_grads, other_grads),
        gain_rows[0:1],
        qkv[None, :, :WIDTH],
        qkv[None, :, WIDTH : WIDTH + kv],
        qkv[None, :, WIDTH + kv :],
        out[None],
        gain_rows[1:2],
        gate_grad[None],
        up_grad[None],
        down[None],
    )


def solution(mesh):
    rows = P(None, "fsdp", None, "ctx", None)
    gain, matrix = P("section", "fsdp"), P("section", "fsdp", None)
    layer_rows = P("section", None, "fsdp", None, "ctx", None)
    weights = (gain, matrix, matrix, matrix, matrix, gain, matrix, matrix, matrix)
    return jax.shard_map(
        on_device,
        mesh=mesh,
        in_specs=(rows, rows) + weights,
        out_specs=(layer_rows, layer_rows) + weights,
        check_vma=False,
    )
```

time: 1380 us -> 772 us (0.56)
  waiting for transfers between devices: 739 us -> 212 us
  matrix products: 191 us -> 15.5 us
  starting transfers between devices: 16.1 us -> 151 us
  blocking collectives: 247 us -> 148 us
  Pallas kernels: 0 us -> 85.9 us
  other arithmetic: 64.8 us -> 27.5 us
    unnamed x28 -> x12, waiting for transfers between devices: 374 us -> 1.73 us
    dot_general x70 -> x8, matrix products: 191 us -> 15.5 us  [t_dot(): lax.dot_general(a, b, (((0,), (0,)), ((), ())), preferred_element_type=F32)]
    all_gather x8 -> x3, blocking collectives: 201 us -> 80 us  [the longest x1 40.9 us: on_device(): out = lax.all_gather(out_slice, 'ctx', tiled=True)[:SHARD].astype(F32)]
    psum x1 -> x0, waiting for transfers between devices: 97.6 us -> none  [on_device(): lax.psum(query_part.astype(jnp.bfloat16), 'ctx').astype(jnp.float32)]
    reduce_scatter x4, waiting for transfers between devices: 170 us -> 73.1 us  [the longest x2 61.8 us: on_device(): lax.psum_scatter(grad_gu.reshape(CTX * FSDP * SLICE, 2 * FF_SHARD), 'ctx'...]
    pallas_call x0 -> x16, Pallas kernels: none -> 85.9 us  [call(): pl.pallas_call(body, out_shape=outs, scratch_shapes=list(scratch), compil...]
    all_to_all x0 -> x4, blocking collectives: none -> 68.2 us  [all_to_all(): return lax.all_to_all(x, axis, 0, 0)]
    all_to_all x0 -> x10, starting transfers between devices: none -> 68.1 us  [all_to_all(): return lax.all_to_all(x, axis, 0, 0)]
  transfers between devices with their start and end apart: 23 -> 83, of which waited for: 16 -> 28; matrix products, arithmetic and copies ran while one was open for 13% -> 10% of each run, Pallas kernels for 0% -> 10%
where the time goes in v1:
time: 772 us; the launch traced here: 762 us
  waiting for transfers between devices  212 us (27%)
  starting transfers between devices  151 us (20%)
  blocking collectives  148 us (19%)
  local copies, waits for them, and re-layouts  106 us (14%)
  Pallas kernels  85.9 us (11%)
  other arithmetic  27.5 us (4%)
  between operations  15.8 us (2%)
  matrix products  15.5 us (2%)
    pallas_call x16, Pallas kernels, call(): pl.pallas_call(body, out_shape=outs, scratch_shapes=list(scratch), compil...  85.9 us
    all_to_all x4, blocking collectives, all_to_all(): return lax.all_to_all(x, axis, 0, 0)  68.2 us
    all_to_all x10, starting transfers between devices, all_to_all(): return lax.all_to_all(x, axis, 0, 0)  68.1 us
    ppermute x54, starting transfers between devices, shifted(): return lax.ppermute(x, axis, [(i, (i + distance) % n) for i in range(n)])  67.7 us
    reduce_scatter x2, waiting for transfers between devices, on_device(): lax.psum_scatter(grad_gu.reshape(CTX * FSDP * SLICE, 2 * FF_SHARD), 'ctx'...  61.8 us
    ppermute x54, waiting for transfers between devices, shifted(): return lax.ppermute(x, axis, [(i, (i + distance) % n) for i in range(n)])  55.2 us
    all_gather x1, blocking collectives, on_device(): out = lax.all_gather(out_slice, 'ctx', tiled=True)[:SHARD].astype(F32)  40.9 us
    all_gather x4, waiting for transfers between devices, whole(): gathered = lax.all_gather(slices, 'ctx')[:SLICES]  35.1 us
  transfers between devices with their start and end apart: 83, of which 28 were waited for; matrix products, arithmetic and copies ran while one was open for 10% of the time, Pallas kernels for 10%

profile of v1, /device:TPU:1, one launch (start us, length us, event | category | flops | bytes accessed | tf_op | source)
XLA Modules:
  0.0 762.1 jit_solution(18180896189868698668)
XLA Ops:
  10.8 16.6 %all_to_all.70 = bf16[8,16,1600]{2,1,0:T(8,128)(2,1)S(1)} all-to-all(bf16[8,16,1600]{2,1,0:T(8,128)(2,1)S(1)} %broadcast_in_dim.53), channel_id=1, replica_groups=mesh['section'=2,'ctx'=16,'fsdp'=4] {'section','fsdp'}, dimensions={0} | all-to-all | bytes 819200 | tf_op jit(solution)/shard_map/all_to_all | solution.py:288
  29.6 13.3 %all_to_all.71 = bf16[8,16,2240]{2,1,0:T(8,128)(2,1)S(1)} all-to-all(bf16[8,16,2240]{2,1,0:T(8,128)(2,1)S(1)} %bitcast.188), channel_id=1, replica_groups=mesh['section'=2,'ctx'=16,'fsdp'=4] {'section','fsdp'}, dimensions={0} | all-to-all | bytes 1146880 | tf_op jit(solution)/shard_map/all_to_all | solution.py:288
  52.2 16.6 %all-gather.6 = bf16[8,2,240]{2,1,0:T(2,128)(2,1)S(1)} all-gather(bf16[1,2,240]{2,1,0:T(2,128)(2,1)S(1)} %maximum_bitcast_fusion), channel_id=2, replica_groups=mesh['section'=2,'ctx'=16,'fsdp'=4] {'section','fsdp'}, dimensions={0}, use_global_device_ids=true | all-gather | bytes 8640 | tf_op jit(solution)/shard_map/all_gather | solution.py:314
  80.5 18.0 %all-to-all-start.1 = ((bf16[16,144,128]{2,1,0:T(8,128)(2,1)}), bf16[16,144,128]{2,1,0:T(8,128)(2,1)S(1)}, u32[]{:S(2)}, u32[]{:S(2)}) async-start(bf16[16,144,128]{2,1,0:T(8,128)(2,1)} %get-tuple-element.60), calls=%async_computation.1 | async-start | bytes 1179648 | tf_op jit(solution)/shard_map/all_to_all | solution.py:288
  99.1 12.0 %all-to-all-done.1.recv = bf16[16,144,128]{2,1,0:T(8,128)(2,1)S(1)} async-done(((bf16[16,144,128]{2,1,0:T(8,128)(2,1)}), bf16[16,144,128]{2,1,0:T(8,128)(2,1)S(1)}, u32[]{:S(2)}, u32[]{:S(2)}) %all-to-all-start.1) | async-done | bytes 589856 | tf_op jit(solution)/shard_map/all_to_all | solution.py:288
  140.5 8.0 %all-gather.16.cloned.1.call-done.refs_5_.refs_7_ = bf16[640,960]{1,0:T(8,128)(2,1)} async-done(((bf16[40,960]{1,0:T(8,128)(2,1)}), bf16[640,960]{1,0:T(8,128)(2,1)}) %all-gather.16.cloned.1.call-update) | async-done | bytes 1228816 | tf_op jit(solution)/shard_map/all_gather | solution.py:345
  158.5 27.6 %all-gather.26.cloned.1.call-done = bf16[64,16,1600]{2,1,0:T(8,128)(2,1)} async-done(((bf16[4,16,1600]{2,1,0:T(8,128)(2,1)}), bf16[64,16,1600]{2,1,0:T(8,128)(2,1)}) %all-gather.26.cloned.1.call-update) | async-done | bytes 3276816 | tf_op jit(solution)/shard_map/all_gather | solution.py:336
  195.4 20.6 %all_to_all.72.recv = bf16[16,144,128]{2,1,0:T(8,128)(2,1)} all-to-all(bf16[16,144,128]{2,1,0:T(8,128)(2,1)} %get-tuple-element.68), channel_id=1, replica_groups=mesh['section'=2,'ctx'=16,'fsdp'=4] {'ctx'}, dimensions={0} | all-to-all | bytes 1179648 | tf_op jit(solution)/shard_map/all_to_all | solution.py:288
  226.2 7.5 all-gather.28.cloned.1.call-done
  257.4 10.9 %all-gather.18.cloned.1.call-done.refs_5_.refs_7_ = bf16[640,960]{1,0:T(8,128)(2,1)} async-done(((bf16[40,960]{1,0:T(8,128)(2,1)}), bf16[640,960]{1,0:T(8,128)(2,1)}) %all-gather.18.cloned.1.call-update) | async-done | bytes 1228816 | tf_op jit(solution)/shard_map/all_gather | solution.py:345
  275.8 7.0 shard_map.202
  317.9 9.1 %shard_map.204 = bf16[16,144,128]{2,1,0:T(8,128)(2,1)} custom-call(bf16[16,144,128]{2,1,0:T(8,128)(2,1)} %all_to_all.72.recv, bf16[16,48,128]{2,1,0:T(8,128)(2,1)} %copy-done.20, f32[1536,128]{1,0:T(8,128)} %get-tuple-element.220.cos, f32[1536,128]{1,0:T(8,128)} %get-tuple-element.221.sin), custom_call_target="tpu_custom_call" | custom-call | flops 754974720 | bytes 2949120 | tf_op jit(solution)/shard_map/pallas_call | solution.py:44
  327.0 17.6 %all_to_all.73.recv = bf16[16,144,128]{2,1,0:T(8,128)(2,1)} all-to-all(bf16[16,144,128]{2,1,0:T(8,128)(2,1)} %shard_map.204), channel_id=1, replica_groups=mesh['section'=2,'ctx'=16,'fsdp'=4] {'ctx'}, dimensions={0} | all-to-all | bytes 1179648 | tf_op jit(solution)/shard_map/all_to_all | solution.py:288
  361.9 7.0 shard_map.206
  421.5 11.3 %reduce-scatter.9.cloned.1.call-done = bf16[40,960]{1,0:T(8,128)(2,1)} async-done(((bf16[640,960]{1,0:T(8,128)(2,1)}), bf16[40,960]{1,0:T(8,128)(2,1)}) %reduce-scatter.9.cloned.1.call-update) | async-done | bytes 76816 | tf_op jit(solution)/shard_map/reduce_scatter | solution.py:446
  460.2 10.4 %all-to-all-start.8 = ((bf16[16,48,128]{2,1,0:T(8,128)(2,1)}), bf16[16,48,128]{2,1,0:T(8,128)(2,1)S(1)}, u32[]{:S(2)}, u32[]{:S(2)}) async-start(bf16[16,48,128]{2,1,0:T(8,128)(2,1)} %get-tuple-element.91), calls=%async_computation.8 | async-start | bytes 393216 | tf_op jit(solution)/shard_map/all_to_all | solution.py:288
  494.0 9.2 %shard_map.208 = bf16[16,144,128]{2,1,0:T(8,128)(2,1)} custom-call(bf16[16,144,128]{2,1,0:T(8,128)(2,1)} %copy-done.9, bf16[16,48,128]{2,1,0:T(8,128)(2,1)} %copy-done.17, f32[1536,128]{1,0:T(8,128)} %get-tuple-element.220.cos, f32[1536,128]{1,0:T(8,128)} %get-tuple-element.221.sin), custom_call_target="tpu_custom_call" | custom-call | flops 754974720 | bytes 2949120 | tf_op jit(solution)/shard_map/pallas_call | solution.py:44
  507.8 61.8 %reduce-scatter.5.cloned.1.call-done = bf16[64,1280]{1,0:T(8,128)(2,1)} async-done(((bf16[1024,1280]{1,0:T(8,128)(2,1)}), bf16[64,1280]{1,0:T(8,128)(2,1)}) %reduce-scatter.5.cloned.1.call-update) | async-done | bytes 163856 | tf_op jit(solution)/shard_map/reduce_scatter | solution.py:442
  573.6 7.6 all-to-all-start.9
  613.6 6.8 collective-permute-done.30
  631.0 40.9 %all_gather.48 = bf16[256,960]{1,0:T(8,128)(2,1)S(1)} all-gather(bf16[16,960]{1,0:T(8,128)(2,1)S(1)} %add_convert_fusion.4), channel_id=1, replica_groups=mesh['section'=2,'ctx'=16,'fsdp'=4] {'ctx'}, dimensions={0}, use_global_device_ids=true | all-gather | bytes 522240 | tf_op jit(solution)/shard_map/all_gather | solution.py:475
  677.9 22.5 %all_gather.47 = bf16[256,1600]{1,0:T(8,128)(2,1)S(1)} all-gather(bf16[16,1600]{1,0:T(8,128)(2,1)S(1)} %add_convert_fusion.3), channel_id=1, replica_groups=mesh['section'=2,'ctx'=16,'fsdp'=4] {'ctx'}, dimensions={0}, use_global_device_ids=true | all-gather | bytes 870400 | tf_op jit(solution)/shard_map/all_gather | solution.py:476
  723.8 7.0 reshape.241
  730.8 9.7 %fusion.92 = (f32[240,4,1,640]{3,2,0,1:T(1,128)}, f32[240,4,1,640]{3,2,0,1:T(1,128)S(1)}) fusion(f32[240,4,2,640]{3,2,0,1:T(2,128)} %reshape.241), kind=kLoop, calls=%fused_computation.198 | loop fusion | bytes 9830400 | tf_op jit(solution)/shard_map/slice | solution.py:480
  (443 shorter events, 367.2 us)
Async XLA Ops:
  7.2 65.3 %all-gather.22.cloned.1.call-start = ((), (), s32[]{:S(2)}) async-start(), calls=%async_computation.25 | async-start | bytes 3620864 | tf_op jit(solution)/shard_map/all_gather | solution.py:336
  28.2 93.3 %all-gather.24.cloned.1.call-start = ((), (), s32[]{:S(2)}) async-start(), calls=%async_computation.26 | async-start | bytes 5013504 | tf_op jit(solution)/shard_map/all_gather | solution.py:336
  43.8 104.6 %all-gather.16.cloned.1.call-start = ((), (), s32[]{:S(2)}) async-start(), calls=%async_computation.18 | async-start | bytes 1392640 | tf_op jit(solution)/shard_map/all_gather | solution.py:345
  50.9 135.2 %all-gather.26.cloned.1.call-start = ((), (), s32[]{:S(2)}) async-start(), calls=%async_computation.27 | async-start | bytes 3620864 | tf_op jit(solution)/shard_map/all_gather | solution.py:336
  51.5 182.2 %all-gather.28.cloned.1.call-start = ((), (), s32[]{:S(2)}) async-start(), calls=%async_computation.28 | async-start | bytes 5013504 | tf_op jit(solution)/shard_map/all_gather | solution.py:336
  80.5 30.6 %all-to-all-start.1 = ((bf16[16,144,128]{2,1,0:T(8,128)(2,1)}), bf16[16,144,128]{2,1,0:T(8,128)(2,1)S(1)}, u32[]{:S(2)}, u32[]{:S(2)}) async-start(bf16[16,144,128]{2,1,0:T(8,128)(2,1)} %get-tuple-element.60), calls=%async_computation.1 | async-start | bytes 1179648 | tf_op jit(solution)/shard_map/all_to_all | solution.py:288
  98.5 169.8 %all-gather.18.cloned.1.call-start = ((), (), s32[]{:S(2)}) async-start(), calls=%async_computation.19 | async-start | bytes 1392640 | tf_op jit(solution)/shard_map/all_gather | solution.py:345
  155.2 34.9 %collective-permute-start.4 = (bf16[96,960]{1,0:T(8,128)(2,1)}, bf16[96,960]{1,0:T(8,128)(2,1)S(1)}, u32[]{:S(2)}, u32[]{:S(2)}) collective-permute-start(bf16[96,960]{1,0:T(8,128)(2,1)} %get-tuple-element.64), channel_id=1, source_target_pairs={{0,3},{1,0},{2,1},{3,2},{4,7},{5,4},{6,5},{7,6},{8,11},{9,8},{10,9... | collective-permute-start | bytes 552968 | tf_op jit(solution)/shard_map/ppermute | solution.py:267
  157.4 32.7 %collective-permute-start.5 = (bf16[96,960]{1,0:T(8,128)(2,1)}, bf16[96,960]{1,0:T(8,128)(2,1)S(1)}, u32[]{:S(2)}, u32[]{:S(2)}) collective-permute-start(bf16[96,960]{1,0:T(8,128)(2,1)} %get-tuple-element.65), channel_id=1, source_target_pairs={{0,2},{1,3},{2,0},{3,1},{4,6},{5,7},{6,4},{7,5},{8,10},{9,11},{10,... | collective-permute-start | bytes 552968 | tf_op jit(solution)/shard_map/ppermute | solution.py:267
  158.1 32.0 %collective-permute-start.6 = (bf16[96,960]{1,0:T(8,128)(2,1)}, bf16[96,960]{1,0:T(8,128)(2,1)S(1)}, u32[]{:S(2)}, u32[]{:S(2)}) collective-permute-start(bf16[96,960]{1,0:T(8,128)(2,1)} %get-tuple-element.66), channel_id=1, source_target_pairs={{0,1},{1,2},{2,3},{3,0},{4,5},{5,6},{6,7},{7,4},{8,9},{9,10},{10,1... | collective-permute-start | bytes 552968 | tf_op jit(solution)/shard_map/ppermute | solution.py:267
  226.2 195.3 %reduce-scatter.11.cloned.1.call-start = ((), (), s32[]{:S(2)}) async-start(), calls=%async_computation.23 | async-start | bytes 1392640 | tf_op jit(solution)/shard_map/reduce_scatter | solution.py:446
  310.1 122.7 %reduce-scatter.9.cloned.1.call-start = ((), (), s32[]{:S(2)}) async-start(), calls=%async_computation.22 | async-start | bytes 1392640 | tf_op jit(solution)/shard_map/reduce_scatter | solution.py:446
  372.3 130.9 %reduce-scatter.7.cloned.1.call-start = ((), (), s32[]{:S(2)}) async-start(), calls=%async_computation.21 | async-start | bytes 2785280 | tf_op jit(solution)/shard_map/reduce_scatter | solution.py:442
  376.3 193.3 %reduce-scatter.5.cloned.1.call-start = ((), (), s32[]{:S(2)}) async-start(), calls=%async_computation.20 | async-start | bytes 2785280 | tf_op jit(solution)/shard_map/reduce_scatter | solution.py:442
  402.7 34.1 %collective-permute-start.13 = (bf16[96,960]{1,0:T(8,128)(2,1)S(1)}, bf16[96,960]{1,0:T(8,128)(2,1)S(1)}, u32[]{:S(2)}, u32[]{:S(2)}) collective-permute-start(bf16[96,960]{1,0:T(8,128)(2,1)S(1)} %get-tuple-element.162), channel_id=1, source_target_pairs={{0,64},{64,0},{1,65},{65,1},{2,66},{66,2},{3,67},{67,3},{4,68},{68... | collective-permute-start | bytes 552968 | tf_op jit(solution)/shard_map/ppermute | solution.py:284
  419.3 286.5 %all-gather.20.cloned.1.call-start = ((), (), s32[]{:S(2)}) async-start(), calls=%async_computation.24 | async-start | bytes 1392640 | tf_op jit(solution)/shard_map/all_gather | solution.py:474
  487.9 85.6 %all-to-all-start.12 = ((bf16[16,16,960]{2,1,0:T(8,128)(2,1)}), bf16[16,16,960]{2,1,0:T(8,128)(2,1)S(1)}, u32[]{:S(2)}, u32[]{:S(2)}) async-start(bf16[16,16,960]{2,1,0:T(8,128)(2,1)} %bitcast.63), calls=%async_computation.12 | async-start | bytes 1048576 | tf_op jit(solution)/shard_map/all_to_all | solution.py:288
  504.0 77.2 %collective-permute-start.58 = (bf16[16,1280]{1,0:T(8,128)(2,1)S(1)}, bf16[16,1280]{1,0:T(8,128)(2,1)S(1)}, u32[]{:S(2)}, u32[]{:S(2)}) collective-permute-start(bf16[16,1280]{1,0:T(8,128)(2,1)S(1)} %get-tuple-element.197), channel_id=1, source_target_pairs={{0,3},{1,0},{2,1},{3,2},{4,7},{5,4},{6,5},{7,6},{8,11},{9,8},{10,9... | collective-permute-start | bytes 122888 | tf_op jit(solution)/shard_map/ppermute | solution.py:267
  507.2 75.5 %collective-permute-start.57 = (bf16[16,1280]{1,0:T(8,128)(2,1)S(1)}, bf16[16,1280]{1,0:T(8,128)(2,1)S(1)}, u32[]{:S(2)}, u32[]{:S(2)}) collective-permute-start(bf16[16,1280]{1,0:T(8,128)(2,1)S(1)} %get-tuple-element.198), channel_id=1, source_target_pairs={{0,2},{1,3},{2,0},{3,1},{4,6},{5,7},{6,4},{7,5},{8,10},{9,11},{10,... | collective-permute-start | bytes 122888 | tf_op jit(solution)/shard_map/ppermute | solution.py:267
  507.2 77.7 %collective-permute-start.56 = (bf16[16,1280]{1,0:T(8,128)(2,1)S(1)}, bf16[16,1280]{1,0:T(8,128)(2,1)S(1)}, u32[]{:S(2)}, u32[]{:S(2)}) collective-permute-start(bf16[16,1280]{1,0:T(8,128)(2,1)S(1)} %get-tuple-element.199), channel_id=1, source_target_pairs={{0,1},{1,2},{2,3},{3,0},{4,5},{5,6},{6,7},{7,4},{8,9},{9,10},{10,1... | collective-permute-start | bytes 122888 | tf_op jit(solution)/shard_map/ppermute | solution.py:267
  581.1 131.0 %all-gather.30.cloned.1.call-start = ((), (), s32[]{:S(2)}) async-start(), calls=%async_computation.29 | async-start | bytes 2785280 | tf_op jit(solution)/shard_map/all_gather | solution.py:473
  582.6 38.2 %collective-permute-start.29 = (bf16[96,240]{1,0:T(8,128)(2,1)}, bf16[96,240]{1,0:T(8,128)(2,1)}, u32[]{:S(2)}, u32[]{:S(2)}) collective-permute-start(bf16[96,240]{1,0:T(8,128)(2,1)} %get-tuple-element.185), channel_id=1, source_target_pairs={{0,3},{1,0},{2,1},{3,2},{4,7},{5,4},{6,5},{7,6},{8,11},{9,8},{10,9... | collective-permute-start | bytes 138248 | tf_op jit(solution)/shard_map/ppermute | solution.py:267
  624.4 48.8 %all-to-all-start.10 = ((bf16[16,16,1600]{2,1,0:T(8,128)(2,1)}), bf16[16,16,1600]{2,1,0:T(8,128)(2,1)S(1)}, u32[]{:S(2)}, u32[]{:S(2)}) async-start(bf16[16,16,1600]{2,1,0:T(8,128)(2,1)} %bitcast.45), calls=%async_computation.10 | async-start | bytes 1703936 | tf_op jit(solution)/shard_map/all_to_all | solution.py:288
  628.6 44.4 %collective-permute-start.26 = (f32[96,960]{1,0:T(8,128)S(1)}, f32[96,960]{1,0:T(8,128)S(1)}, u32[]{:S(2)}, u32[]{:S(2)}) collective-permute-start(f32[96,960]{1,0:T(8,128)S(1)} %convert_select_fusion), channel_id=1, source_target_pairs={{0,64},{64,0},{1,65},{65,1},{2,66},{66,2},{3,67},{67,3},{4,68},{68... | collective-permute-start | bytes 1105928 | tf_op jit(solution)/shard_map/ppermute | solution.py:284
  (134 other events, 1247.1 us)
Sparse Core Ops, SparseCore 0:
  28.3 37.9 all-gather.21
  68.7 43.2 all-gather.23
  114.3 34.1 all-gather.15
  150.0 36.1 all-gather.25
  188.3 45.3 all-gather.27
  235.3 32.9 all-gather.17
  286.2 59.8 reduce-scatter.10
  372.4 60.3 reduce-scatter.8
  435.2 65.3 reduce-scatter.6
  502.8 66.7 reduce-scatter.4
  571.3 38.7 all-gather.19
  612.3 43.7 all-gather.29

commit v2 on v1

v2 whole, which is shorter than its diff:
```python
import functools

import jax
import jax.numpy as jnp
import numpy as np
from jax import lax
from jax.experimental import pallas as pl
from jax.experimental.pallas import tpu as pltpu
from jax.sharding import PartitionSpec as P

WIDTH = 960
HEADS = 15
KV_HEADS = 5
GROUP = HEADS // KV_HEADS
HEAD = 64
FF = 2560
BLK = 48
ROWS = 2 * BLK
CTX = 16
FSDP = 4
LENGTH = ROWS * CTX
SHARD = WIDTH // FSDP
FF_SHARD = FF // FSDP
QK_COLS = (HEADS + KV_HEADS) * HEAD
QKV_COLS = QK_COLS + KV_HEADS * HEAD
SLICE = 16
SLICES = SHARD // SLICE
DOWN_SLICE = WIDTH // SLICES
OUT_COLS = QKV_COLS + WIDTH
FFN_COLS = 3 * FF_SHARD
QKV_LANES = 1664
OUT_LANES = 1024
TILE = 256

EPSILON = 1e-05
THETA = 10000.0
MASKED = -1e30

F32 = jnp.float32
BF16 = jnp.bfloat16


def sds(shape, dtype):
    return jax.ShapeDtypeStruct(shape, dtype)


def call(body, outs, *args, far=(), scalars=0, scratch=(), flops=0):
    size = sum(a.size * a.dtype.itemsize for a in (*args, *outs))
    specs = [pl.BlockSpec(memory_space=pltpu.SMEM if i < scalars else pltpu.VMEM) for i in range(len(args))]
    return pl.pallas_call(
        body,
        out_shape=outs,
        in_specs=specs + [pl.BlockSpec(memory_space=pl.ANY)] * len(far),
        scratch_shapes=list(scratch),
        compiler_params=pltpu.CompilerParams(vmem_limit_bytes=56 * 1024 * 1024),
        cost_estimate=pl.CostEstimate(flops=flops, bytes_accessed=size, transcendentals=0),
    )(*args, *far)


def dot(a, b):
    return jnp.dot(a, b, preferred_element_type=F32)


def dot_t(a, b):
    return lax.dot_general(a, b, (((1,), (1,)), ((), ())), preferred_element_type=F32)


def t_dot(a, b):
    return lax.dot_general(a, b, (((0,), (0,)), ((), ())), preferred_element_type=F32)


def inverse_rms(x):
    return lax.rsqrt(jnp.mean(x * x, axis=-1, keepdims=True) + EPSILON)


def norm_backward(d, x, gain):
    r = inverse_rms(x)
    n = x * r
    t = d * gain
    return (t - n * jnp.mean(t * n, axis=-1, keepdims=True)) * r, jnp.sum(d * n, axis=0, keepdims=True)


def swap_halves(x):
    cols = x.shape[1]
    lane = lax.broadcasted_iota(jnp.int32, x.shape, 1)
    ahead = pltpu.roll(x, cols - HEAD // 2, 1)
    behind = pltpu.roll(x, HEAD // 2, 1)
    return jnp.where(lane % HEAD < HEAD // 2, ahead, behind)


def source_block(b):
    return (b, 0) if b < CTX else (2 * CTX - 1 - b, 1)


def rotary_constants():
    inverse = (THETA ** (-(np.arange(HEAD // 2, dtype=np.float32) * 2.0) / HEAD)).astype(np.float32)
    angles = np.arange(LENGTH, dtype=np.float32)[:, None] * inverse[None, :]
    cos, sin = np.cos(angles.astype(np.float64)), np.sin(angles.astype(np.float64))
    return (
        np.concatenate([cos] * 4, axis=1).astype(np.float32),
        np.concatenate([-sin, sin] * 2, axis=1).astype(np.float32),
    )


def pack(x):
    return jnp.concatenate([x[:BLK], x[BLK:]], axis=1)


def unpack(x):
    cols = x.shape[1] // 2
    return jnp.concatenate([x[:, :cols], x[:, cols:]], axis=0)


def load_rows(src, lanes, dst, sems):
    copies = [
        pltpu.make_async_copy(src.at[0:SLICES, f * SLICE : (f + 1) * SLICE, lanes], dst.at[f], sems.at[f])
        for f in range(FSDP)
    ]
    for copy in copies:
        copy.start()
    return copies


def load_down(src, lanes, dst, sem):
    copy = pltpu.make_async_copy(src.at[0:SLICES, :, lanes], dst, sem)
    copy.start()
    return [copy]


def wait_all(copies):
    for copy in copies:
        copy.wait()


def rows_of(scratch):
    return scratch[...].reshape(WIDTH, scratch.shape[-1])


def row_scratch(lanes):
    return [pltpu.VMEM((FSDP, SLICES, SLICE, lanes), BF16), pltpu.SemaphoreType.DMA((FSDP,))]


def qkv_body(count, *refs):
    parts, (gain, cos, sin, w_far) = refs[:count], refs[count : count + 4]
    x_out, a_out, send, w_s, sems = refs[count + 4 :]
    copies = load_rows(w_far, slice(0, QKV_LANES), w_s, sems)
    x = parts[0][...].astype(F32)
    if count > 1:
        x = x + parts[1][...]
        for part in parts[2:]:
            x = x + unpack(part[...].astype(F32))
    low = x.astype(BF16)
    x_out[...] = low
    x = low.astype(F32)
    a = x * inverse_rms(x) * gain[...]
    for k in range(FSDP):
        a_out[k] = a[:, k * SHARD : (k + 1) * SHARD].astype(BF16)
    wait_all(copies)
    out = dot(a.astype(BF16), rows_of(w_s))
    qk = out[:, :QK_COLS]
    pairs = (HEADS + KV_HEADS) // 2
    lane = lax.broadcasted_iota(jnp.int32, qk.shape, 1)
    scale = jnp.where(lane < HEADS * HEAD, HEAD**-0.5, 1.0)
    cos_all = jnp.concatenate([cos[...]] * pairs, axis=1) * scale
    sin_all = jnp.concatenate([sin[...]] * pairs, axis=1) * scale
    qk = qk * cos_all + swap_halves(qk) * sin_all
    v = out[:, QK_COLS:QKV_COLS]
    for h in range(HEADS):
        g = h // GROUP
        q_h = qk[:, h * HEAD : (h + 1) * HEAD]
        k_g = qk[:, (HEADS + g) * HEAD : (HEADS + g + 1) * HEAD]
        v_g = v[:, g * HEAD : (g + 1) * HEAD]
        send[h, 0:ROWS] = jnp.concatenate([q_h, k_g], axis=1).astype(BF16)
        send[h, ROWS:] = pack(v_g).astype(BF16)
    for h in range(HEADS, CTX):
        send[h] = jnp.zeros(send.shape[1:], BF16)


def unpack_heads(recv, q_s, k_s, v_s):
    for b in range(2 * CTX):
        c, half = source_block(b)
        rows = slice(b * BLK, (b + 1) * BLK)
        qk = recv[c, half * BLK : (half + 1) * BLK, :].astype(F32)
        v = recv[c, ROWS : ROWS + BLK, :].astype(F32)
        q_s[rows, :] = qk[:, :HEAD].astype(BF16)
        k_s[rows, :] = qk[:, HEAD:].astype(BF16)
        v_s[rows, :] = v[:, half * HEAD : (half + 1) * HEAD].astype(BF16)


def probabilities(q, keys, start):
    scores = dot_t(q, keys)
    row = lax.broadcasted_iota(jnp.int32, scores.shape, 0) + start
    col = lax.broadcasted_iota(jnp.int32, scores.shape, 1)
    scores = jnp.where(col <= row, scores, MASKED)
    weights = jnp.exp(scores - jnp.max(scores, axis=-1, keepdims=True))
    return weights / jnp.sum(weights, axis=-1, keepdims=True)


def attend_body(recv, send, q_s, k_s, v_s, out_s):
    unpack_heads(recv, q_s, k_s, v_s)
    for i in range(LENGTH // TILE):
        start, stop = i * TILE, (i + 1) * TILE
        p = probabilities(q_s[start:stop, :], k_s[:stop, :], start)
        out_s[start:stop, :] = dot(p.astype(BF16), v_s[:stop, :])
    for c in range(CTX):
        last = 2 * CTX - 1 - c
        pair = [out_s[c * BLK : (c + 1) * BLK, :], out_s[last * BLK : (last + 1) * BLK, :]]
        send[c] = jnp.concatenate(pair, axis=1).astype(BF16)


def mix_body(x, recv, gain, w_far, mixed_out, b_out, att_out, att_s, w_s, sems):
    copies = load_rows(w_far, slice(0, OUT_LANES), w_s, sems)
    for h in range(HEADS):
        pair = recv[h].astype(F32)
        cols = slice(h * HEAD, (h + 1) * HEAD)
        att_s[0:BLK, cols] = pair[:, :HEAD].astype(BF16)
        att_s[BLK:, cols] = pair[:, HEAD:].astype(BF16)
    att = att_s[...]
    for k in range(FSDP):
        att_out[k] = att_s[:, k * SHARD : (k + 1) * SHARD]
    wait_all(copies)
    mixed = x[...].astype(F32) + dot(att, rows_of(w_s))[:, :WIDTH]
    mixed_out[...] = mixed
    b_out[...] = pack(mixed * inverse_rms(mixed) * gain[...]).astype(BF16)


def spread(total, outs):
    outs[0][...] = total[0:ROWS]
    for k in range(1, FSDP):
        outs[k][...] = pack(total[k * ROWS : (k + 1) * ROWS]).astype(BF16)


def all_rows(parts):
    return jnp.concatenate([unpack(p[...]) for p in parts], axis=0)


def ffn_body(*refs):
    parts, w_far, (gate_out, up_out), outs = refs[:4], refs[4], refs[5:7], refs[7:11]
    w_s, sems, down_s, down_sem = refs[11:]
    copies = load_rows(w_far, slice(OUT_LANES, OUT_LANES + 2 * FF_SHARD), w_s, sems)
    down = load_down(w_far, slice(OUT_LANES + 2 * FF_SHARD, OUT_LANES + FFN_COLS), down_s, down_sem)
    rows = all_rows(parts)
    wait_all(copies)
    gate_up = dot(rows, rows_of(w_s))
    gate, up = gate_up[:, :FF_SHARD], gate_up[:, FF_SHARD:]
    gate_out[...] = gate
    up_out[...] = up
    hidden = (gate * jax.nn.sigmoid(gate) * up).astype(BF16)
    wait_all(down)
    spread(dot_t(hidden, rows_of(down_s)), outs)


def ffn_back_body(*refs):
    parts, (gate_ref, up_ref, w_far) = refs[:4], refs[4:7]
    hidden_out, d_gu_out = refs[7:9]
    outs = refs[9:13]
    w_s, sems, down_s, down_sem = refs[13:]
    down = load_down(w_far, slice(OUT_LANES + 2 * FF_SHARD, OUT_LANES + FFN_COLS), down_s, down_sem)
    copies = load_rows(w_far, slice(OUT_LANES, OUT_LANES + 2 * FF_SHARD), w_s, sems)
    rows = all_rows(parts)
    gate, up = gate_ref[...], up_ref[...]
    sig = jax.nn.sigmoid(gate)
    act = gate * sig
    hidden_out[...] = (act * up).astype(BF16)
    wait_all(down)
    d_hidden = dot(rows, rows_of(down_s))
    d_gu_out[:, :FF_SHARD] = (d_hidden * up * (sig * (1.0 + gate * (1.0 - sig)))).astype(BF16)
    d_gu_out[:, FF_SHARD:] = (d_hidden * act).astype(BF16)
    wait_all(copies)
    spread(dot_t(d_gu_out[...], rows_of(w_s)), outs)


def ffn_grad_body(*refs):
    b_parts, g_parts, d_gu, hidden, out = refs[:4], refs[4:8], refs[8], refs[9], refs[10]
    gu = t_dot(all_rows(b_parts), d_gu[...]).astype(BF16)
    for f in range(FSDP):
        for c in range(SLICES):
            first = f * SHARD + c * SLICE
            out[c, f * SLICE : (f + 1) * SLICE, 0 : 2 * FF_SHARD] = gu[first : first + SLICE]
    down = t_dot(all_rows(g_parts), hidden[...]).astype(BF16)
    for c in range(SLICES):
        out[c, :, 2 * FF_SHARD :] = down[c * DOWN_SLICE : (c + 1) * DOWN_SLICE]
    for c in range(SLICES, CTX):
        out[c] = jnp.zeros(out.shape[1:], BF16)


def mix_back_body(g, p0, p1, p2, p3, mixed, gain, w_far, d_mixed_out, ga_out, gain_out, send, w_s, sems):
    copies = load_rows(w_far, slice(0, OUT_LANES), w_s, sems)
    d_b = p0[...]
    for part in (p1, p2, p3):
        d_b = d_b + unpack(part[...].astype(F32))
    d_in, d_gain = norm_backward(d_b, mixed[...], gain[...])
    d_mixed = unpack(g[...].astype(F32)) + d_in
    d_mixed_out[...] = d_mixed
    gain_out[...] = d_gain
    ga_out[...] = pack(d_mixed).astype(BF16)
    wide = jnp.concatenate([d_mixed, jnp.zeros((ROWS, OUT_LANES - WIDTH), F32)], axis=1).astype(BF16)
    wait_all(copies)
    d_att = dot_t(wide, rows_of(w_s))
    for h in range(HEADS):
        send[h] = pack(d_att[:, h * HEAD : (h + 1) * HEAD]).astype(BF16)
    for h in range(HEADS, CTX):
        send[h] = jnp.zeros(send.shape[1:], BF16)


def attend_back_body(recv, d_recv, cos, sin, send, q_s, k_s, v_s, d_s, dq_s, dk_s, dv_s):
    unpack_heads(recv, q_s, k_s, v_s)
    for b in range(2 * CTX):
        c, half = source_block(b)
        pair = d_recv[c].astype(F32)
        d_s[b * BLK : (b + 1) * BLK, :] = pair[:, half * HEAD : (half + 1) * HEAD].astype(BF16)
    dk_s[...] = jnp.zeros(dk_s.shape, F32)
    dv_s[...] = jnp.zeros(dv_s.shape, F32)
    for i in range(LENGTH // TILE):
        start, stop = i * TILE, (i + 1) * TILE
        q, d_att = q_s[start:stop, :], d_s[start:stop, :]
        p = probabilities(q, k_s[:stop, :], start)
        d_p = dot_t(d_att, v_s[:stop, :])
        inner = jnp.sum(p * d_p, axis=-1, keepdims=True)
        d_scores = (p * (d_p - inner)).astype(BF16)
        dq_s[start:stop, :] = dot(d_scores, k_s[:stop, :])
        dk_s[:, :stop] += t_dot(q, d_scores)
        dv_s[:, :stop] += t_dot(d_att, p.astype(BF16))
    dk = dk_s[...].T
    dv = dv_s[...].T
    both = jnp.concatenate([dq_s[...] * (HEAD**-0.5), dk], axis=1)
    both = both * cos[...] - swap_halves(both) * sin[...]
    for c in range(CTX):
        last = 2 * CTX - 1 - c
        send[c, 0:BLK] = both[c * BLK : (c + 1) * BLK].astype(BF16)
        send[c, BLK:ROWS] = both[last * BLK : (last + 1) * BLK].astype(BF16)
        pair = [dv[c * BLK : (c + 1) * BLK], dv[last * BLK : (last + 1) * BLK]]
        send[c, ROWS:] = jnp.concatenate(pair, axis=1).astype(BF16)


def qkv_back_body(recv, d_mixed, x_ref, gain, gain_ffn, w_far, d_x_out, low_out, rows_out, rows_s, w_s, sems):
    copies = load_rows(w_far, slice(0, QKV_LANES), w_s, sems)
    rows_s[:, QKV_COLS:] = jnp.zeros((ROWS, QKV_LANES - QKV_COLS), BF16)
    for g in range(KV_HEADS):
        d_k = jnp.zeros((ROWS, HEAD), F32)
        d_v = jnp.zeros((BLK, 2 * HEAD), F32)
        for h in range(g * GROUP, (g + 1) * GROUP):
            qk = recv[h, 0:ROWS].astype(F32)
            rows_s[:, h * HEAD : (h + 1) * HEAD] = qk[:, :HEAD].astype(BF16)
            d_k = d_k + qk[:, HEAD:]
            d_v = d_v + recv[h, ROWS:].astype(F32)
        k_cols = slice((HEADS + g) * HEAD, (HEADS + g + 1) * HEAD)
        v_cols = slice(QK_COLS + g * HEAD, QK_COLS + (g + 1) * HEAD)
        rows_s[:, k_cols] = d_k.astype(BF16)
        rows_s[:, v_cols] = unpack(d_v).astype(BF16)
    rows = rows_s[...]
    rows_out[0:ROWS] = rows
    wait_all(copies)
    d_a = dot_t(rows, rows_of(w_s))
    d_in, d_gain = norm_backward(d_a, x_ref[...].astype(F32), gain[...])
    d_x = d_mixed[...] + d_in
    d_x_out[...] = d_x
    low_out[...] = pack(d_x).astype(BF16)
    gains = jnp.concatenate([d_gain, gain_ffn[...], jnp.zeros((SLICE - 2, WIDTH), F32)], axis=0)
    gains = jnp.concatenate([gains, jnp.zeros((SLICE, QKV_LANES - WIDTH), F32)], axis=1)
    rows_out[ROWS:] = gains.astype(BF16)


def qkv_grad_body(fsdp_ref, *refs):
    blocks, parts, out = refs[:4], refs[4:8], refs[8]
    cols = jnp.concatenate([p[:, :SHARD] for p in blocks], axis=0)
    rows = jnp.concatenate([p[0:ROWS] for p in parts], axis=0)
    grad = t_dot(cols, rows).astype(BF16)
    for c in range(SLICES):
        out[c] = grad[c * SLICE : (c + 1) * SLICE]
    gains = sum(p[ROWS:].astype(F32) for p in parts)
    mine = jnp.zeros((SLICE, SHARD), F32)
    for f in range(FSDP):
        mine = jnp.where(fsdp_ref[0] == f, gains[:, f * SHARD : (f + 1) * SHARD], mine)
    out[SLICES] = jnp.concatenate([mine, jnp.zeros((SLICE, QKV_LANES - SHARD), F32)], axis=1).astype(BF16)


def out_grad_body(*refs):
    blocks, ga_parts, out = refs[:4], refs[4:8], refs[8]
    cols = jnp.concatenate([p[:, SHARD:] for p in blocks], axis=0)
    grad = t_dot(cols, all_rows(ga_parts))
    grad = jnp.concatenate([grad, jnp.zeros((SHARD, OUT_LANES - WIDTH), F32)], axis=1).astype(BF16)
    for c in range(SLICES):
        out[c] = grad[c * SLICE : (c + 1) * SLICE]
    out[SLICES] = jnp.zeros((SLICE, OUT_LANES), BF16)


def rest_result_body(fsdp_ref, gathered, gate, up, down, out):
    for c in range(SLICES):
        rows = slice(c * SLICE, (c + 1) * SLICE)
        for k in range(FSDP):
            member = lax.rem(fsdp_ref[0] + FSDP - k, FSDP)
            cols = pl.ds(pl.multiple_of(member * FF_SHARD, 128), FF_SHARD)
            piece = gathered[c, k * SLICE : (k + 1) * SLICE, : 2 * FF_SHARD].astype(F32)
            gate[rows, cols] = piece[:, :FF_SHARD]
            up[rows, cols] = piece[:, FF_SHARD:]
        down[c * DOWN_SLICE : (c + 1) * DOWN_SLICE] = gathered[c, 0 : FSDP * SLICE, 2 * FF_SHARD : FFN_COLS].astype(F32)
        out[rows] = gathered[c, FSDP * SLICE :, :WIDTH].astype(F32)


def qkv_result_body(gathered, query, key, value, gains, kv_s):
    kv = KV_HEADS * HEAD
    for c in range(SLICES):
        rows = slice(c * SLICE, (c + 1) * SLICE)
        piece = gathered[c].astype(F32)
        query[rows] = piece[:, :WIDTH]
        kv_s[rows] = piece[:, WIDTH:QKV_COLS]
    turned = kv_s[...].T
    key[...] = turned[:kv]
    value[...] = turned[kv:]
    gains[...] = gathered[SLICES][:8, :SHARD].astype(F32)


def shifted(x, axis, distance):
    n = lax.axis_size(axis)
    return lax.ppermute(x, axis, [(i, (i + distance) % n) for i in range(n)])


def around(x):
    return [x] + [shifted(x, "fsdp", k) for k in range(1, FSDP)]


def back_around(parts):
    return [parts[0]] + [shifted(parts[k], "fsdp", -k) for k in range(1, FSDP)]


def exchange_blocks(blocks, index):
    pick = lambda k: lax.dynamic_index_in_dim(blocks, (index + k) % FSDP, 0, keepdims=False)
    return [pick(0)] + [shifted(pick(k), "fsdp", k) for k in range(1, FSDP)]


def swap_sections(x):
    return lax.ppermute(x, "section", [(0, 1), (1, 0)])


def all_to_all(x, axis):
    return lax.all_to_all(x, axis, 0, 0)


def after(x, *earlier):
    return lax.optimization_barrier((x, earlier))[0]


def to_all(x, axis, count):
    return all_to_all(jnp.broadcast_to(x[None], (count,) + x.shape), axis)


def on_device(
    tokens,
    cotangent,
    norm_attn,
    w_query,
    key_projection,
    value_projection,
    w_out,
    norm_ffn,
    w_gate,
    w_up,
    w_down,
):
    section = lax.axis_index("section")
    ctx = lax.axis_index("ctx")
    fsdp = lax.axis_index("fsdp")
    first = section == 0

    place = jnp.minimum(ctx, SLICES - 1)

    def my_slice(rows, count=SLICE):
        return lax.dynamic_slice_in_dim(rows, place * count, count, 0)

    own_gains = jnp.concatenate([norm_attn, norm_ffn], axis=1)
    own_gains = jnp.pad(own_gains, ((0, SLICE - 1), (0, QKV_LANES - 2 * SHARD)))
    qkv = jnp.concatenate([my_slice(w[0]) for w in (w_query, key_projection, value_projection)], axis=1)
    qkv = jnp.pad(qkv, ((0, 0), (0, QKV_LANES - QKV_COLS)))
    qkv = to_all(jnp.where(ctx < SLICES, qkv, own_gains), ("section", "fsdp"), 2 * FSDP)
    qkv = qkv.reshape(2, FSDP * SLICE, QKV_LANES)

    out = jnp.pad(my_slice(w_out[0]), ((0, 0), (0, OUT_LANES - WIDTH)))
    out = jnp.broadcast_to(out[:, None], (SLICE, FSDP, OUT_LANES))
    rest = [my_slice(w[0]).reshape(SLICE, FSDP, FF_SHARD) for w in (w_gate, w_up)]
    rest = jnp.concatenate([out] + rest, axis=2).transpose(1, 0, 2)
    rest = all_to_all(after(jnp.concatenate([rest, rest]), qkv), ("section", "fsdp"))
    rest = rest.reshape(2, FSDP * SLICE, OUT_LANES + 2 * FF_SHARD)
    down = my_slice(w_down[0].T, DOWN_SLICE)
    down_other = swap_sections(after(down, qkv))
    downs = (jnp.where(first, down, down_other), jnp.where(first, down_other, down))
    rest = [jnp.concatenate(pair, axis=1) for pair in zip(rest, downs)]

    qkv_weights, rest_weights = [lax.all_gather(qkv[0], "ctx")], []

    def gains_of(layer):
        rows = qkv_weights[layer][SLICES, ::SLICE, : 2 * SHARD].astype(F32)
        return rows[:, :SHARD].reshape(1, WIDTH), rows[:, SHARD:].reshape(1, WIDTH)

    cos_all, sin_all = rotary_constants()
    cos_all, sin_all = jnp.asarray(cos_all), jnp.asarray(sin_all)

    def own_positions(table):
        pieces = [
            lax.dynamic_slice_in_dim(table, start * BLK, BLK, 0) for start in (ctx, 2 * CTX - 1 - ctx)
        ]
        return jnp.concatenate(pieces)

    cos_own, sin_own = own_positions(cos_all), own_positions(sin_all)

    def mine(x):
        return lax.dynamic_index_in_dim(x, section, 0, keepdims=False).reshape(2, BLK, WIDTH)

    my_rows = mine(tokens).reshape(ROWS, WIDTH)
    my_cotangent = mine(cotangent).transpose(1, 0, 2).reshape(BLK, 2 * WIDTH)

    row_f32, row_bf16 = sds((ROWS, WIDTH), F32), sds((ROWS, WIDTH), BF16)
    packed = sds((BLK, 2 * WIDTH), BF16)
    heads_shape = sds((CTX, ROWS + BLK, 2 * HEAD), BF16)
    att_shape = sds((CTX, BLK, 2 * HEAD), BF16)
    blocks_shape = sds((FSDP, ROWS, SHARD), BF16)
    seq = lambda dtype: pltpu.VMEM((LENGTH, HEAD), dtype)
    partials = [row_f32] + [packed] * 3
    ff_f32, ff_bf16 = sds((FSDP * ROWS, FF_SHARD), F32), sds((FSDP * ROWS, FF_SHARD), BF16)
    qkv_scratch, out_scratch = row_scratch(QKV_LANES), row_scratch(OUT_LANES)
    ffn_scratch = row_scratch(2 * FF_SHARD) + [
        pltpu.VMEM((SLICES, DOWN_SLICE, FF_SHARD), BF16), pltpu.SemaphoreType.DMA,
    ]
    bind = functools.partial

    kept = []
    parts = [my_rows]
    for layer in range(2):
        gain_attn, gain_ffn = gains_of(layer)
        x, a_blocks, send = call(
            bind(qkv_body, len(parts)), [row_bf16, blocks_shape, heads_shape],
            *parts, gain_attn, cos_own, sin_own, far=[qkv_weights[layer]],
            scratch=qkv_scratch, flops=2 * ROWS * WIDTH * QKV_COLS,
        )
        if layer == 0:
            rest_weights.append(lax.all_gather(rest[0], "ctx"))
            qkv_weights.append(lax.all_gather(after(qkv[1], send), "ctx"))
        heads = all_to_all(send, "ctx")
        send = call(
            attend_body, [att_shape], heads,
            scratch=[seq(BF16), seq(BF16), seq(BF16), seq(F32)], flops=2 * LENGTH * LENGTH * HEAD,
        )[0]
        arrived = all_to_all(send, "ctx")
        if layer == 0:
            rest_weights.append(lax.all_gather(after(rest[1], arrived), "ctx"))
        else:
            first_blocks = exchange_blocks(after(kept[0][1], send), fsdp)
            arrived = after(arrived, *first_blocks)
        mixed, b, att_blocks = call(
            mix_body, [row_f32, packed, blocks_shape],
            x, arrived, gain_ffn, far=[rest_weights[layer]],
            scratch=[pltpu.VMEM((ROWS, WIDTH), BF16)] + out_scratch, flops=2 * ROWS * WIDTH * WIDTH,
        )
        b_all = around(b)
        gate, up, *outs = call(
            ffn_body, [ff_f32, ff_f32] + partials, *b_all, far=[rest_weights[layer]],
            scratch=ffn_scratch, flops=2 * FSDP * ROWS * WIDTH * FF_SHARD * 3,
        )
        if layer == 0:
            parts = [mixed] + back_around(outs)
        blocks = jnp.concatenate([a_blocks, att_blocks], axis=2)
        kept.append((x, blocks, heads, mixed, b_all, gate, up, gain_attn, gain_ffn))
    first_acts, last_outs = kept[1][0], outs

    g = my_cotangent
    ffn_grads, out_grads, d_inputs = [None, None], [None, None], [None, None]
    fsdp_index = fsdp.astype(jnp.int32).reshape(1)

    def ffn_gradient(b_all, g_all, d_gu, hidden):
        slices = call(
            ffn_grad_body, [sds((CTX, FSDP * SLICE, FFN_COLS), BF16)], *b_all, *g_all, d_gu, hidden,
            flops=2 * FSDP * ROWS * WIDTH * FFN_COLS,
        )[0]
        return lax.psum_scatter(
            slices.reshape(CTX * FSDP * SLICE, FFN_COLS), "ctx", scatter_dimension=0, tiled=True
        )

    def qkv_gradient(blocks, d_rows):
        return call(
            qkv_grad_body, [sds((CTX, SLICE, QKV_LANES), BF16)], fsdp_index, *blocks, *d_rows,
            scalars=1, flops=2 * FSDP * ROWS * SHARD * QKV_COLS,
        )[0]

    def out_gradient(blocks, ga):
        return call(
            out_grad_body, [sds((CTX, SLICE, OUT_LANES), BF16)], *blocks, *ga,
            flops=2 * FSDP * ROWS * SHARD * WIDTH,
        )[0]

    def reduced(slices):
        return all_to_all(slices, "ctx").astype(F32).sum(axis=0).astype(BF16)

    for layer in (1, 0):
        x, blocks, heads, mixed, b_all, gate, up, gain_attn, gain_ffn = kept[layer]
        g_all = around(g)
        hidden, d_gu, *outs = call(
            ffn_back_body,
            [ff_bf16, sds((FSDP * ROWS, 2 * FF_SHARD), BF16)] + partials,
            *g_all, gate, up, far=[rest_weights[layer]],
            scratch=ffn_scratch, flops=2 * FSDP * ROWS * WIDTH * FF_SHARD * 3,
        )
        if layer == 0:
            ffn_grads[0] = ffn_gradient(b_all, g_all, d_gu, hidden)
        d_mixed, ga, d_gain_ffn, send = call(
            mix_back_body, [row_f32, packed, sds((1, WIDTH), F32), att_shape],
            g, *back_around(outs), mixed, gain_ffn, far=[rest_weights[layer]],
            scratch=out_scratch, flops=2 * ROWS * WIDTH * WIDTH,
        )
        if layer == 1:
            ffn_grads[1] = ffn_gradient(b_all, g_all, after(d_gu, send), hidden)
        if layer == 1:
            blocks = exchange_blocks(after(blocks, send), fsdp)
            late_blocks = blocks
            last_parts = back_around([after(part, send) for part in last_outs])
            beside = [*blocks, *last_parts]
        else:
            blocks = first_blocks
            late_rows = around(after(d_rows, send))
            last_acts = kept[1][3] + last_parts[0]
            for part in last_parts[1:]:
                part = part.reshape(BLK, 2, WIDTH).transpose(1, 0, 2).reshape(ROWS, WIDTH)
                last_acts = last_acts + part.astype(F32)
            last_acts = last_acts.astype(BF16)
            other_acts = swap_sections(after(jnp.where(first, last_acts, first_acts), send))
            beside = [*late_rows, other_acts]
        send = call(
            attend_back_body, [heads_shape],
            heads, all_to_all(send, "ctx"), cos_all, sin_all,
            scratch=[seq(BF16)] * 4 + [seq(F32)] + [pltpu.VMEM((HEAD, LENGTH), F32)] * 2,
            flops=5 * LENGTH * LENGTH * HEAD,
        )[0]
        send = after(send, *beside)
        ga = around(after(ga, send))
        out_grads[layer] = out_gradient(blocks, ga)
        beside = [out_grads[layer]]
        if layer == 0:
            late_slices = qkv_gradient(late_blocks, late_rows)
            beside.append(late_slices)
        d_x, d_low, d_rows = call(
            qkv_back_body,
            [row_f32, packed, sds((ROWS + SLICE, QKV_LANES), BF16)],
            after(all_to_all(send, "ctx"), *beside), d_mixed, x, gain_attn, d_gain_ffn, far=[qkv_weights[layer]],
            scratch=[pltpu.VMEM((ROWS, QKV_LANES), BF16)] + qkv_scratch,
            flops=2 * ROWS * WIDTH * QKV_COLS,
        )
        d_inputs[layer] = (d_x, d_low)
        g = d_low

    def across(zero, one):
        keep, give = jnp.where(first, zero, one), jnp.where(first, one, zero)
        return (keep.astype(F32) + swap_sections(give).astype(F32)).astype(BF16)

    late_slices = reduced(jnp.concatenate([late_slices, *out_grads], axis=2))
    other_grads = swap_sections(jnp.where(first, d_inputs[1][1], d_inputs[0][1]))
    ffn_slices = across(*[after(grad, send) for grad in ffn_grads])
    gate_up = ffn_slices[:, : 2 * FF_SHARD].reshape(FSDP, SLICE, 2 * FF_SHARD)
    gate_up = jnp.concatenate(exchange_blocks(gate_up, fsdp))
    ffn_slices = jnp.concatenate([gate_up, ffn_slices[:, 2 * FF_SHARD :]], axis=1)
    out_grads = [late_slices[:, start : start + OUT_LANES] for start in (QKV_LANES, QKV_LANES + OUT_LANES)]
    d_rows = around(d_rows)
    d_rows[0] = after(d_rows[0], late_slices, other_grads, ffn_slices)
    slices = qkv_gradient(blocks, d_rows)
    out_slices = across(*[after(grad, slices) for grad in out_grads])
    qkv_slices = across(reduced(slices), late_slices[:, :QKV_LANES])
    out_slices = jnp.pad(out_slices, ((0, 0), (0, FFN_COLS - OUT_LANES)))
    gate, up, down, out = call(
        rest_result_body,
        [sds((SHARD, FF), F32), sds((SHARD, FF), F32), sds((WIDTH, FF_SHARD), F32), sds((SHARD, WIDTH), F32)],
        fsdp_index, lax.all_gather(jnp.concatenate([ffn_slices, out_slices]), "ctx"), scalars=1,
    )
    kv = KV_HEADS * HEAD
    query, key, value, gains = call(
        qkv_result_body,
        [sds((SHARD, WIDTH), F32), sds((kv, SHARD), F32), sds((kv, SHARD), F32), sds((8, SHARD), F32)],
        after(to_all(qkv_slices, "ctx", CTX), gate), scratch=[pltpu.VMEM((SHARD, 2 * kv), F32)],
    )
    other_grads = other_grads.reshape(BLK, 2, WIDTH).transpose(1, 0, 2).reshape(ROWS, WIDTH).astype(F32)
    d_one = d_inputs[1][1].reshape(BLK, 2, WIDTH).transpose(1, 0, 2).reshape(ROWS, WIDTH).astype(F32)
    mine_grads = jnp.where(first, d_inputs[0][0], d_one)
    mine_acts = jnp.where(first, first_acts, last_acts)

    def by_micro(own, other):
        pair = jnp.stack([jnp.where(first, own, other), jnp.where(first, other, own)])
        return pair.reshape(1, 2, 1, 2, BLK, WIDTH)

    return (
        by_micro(mine_acts, other_acts),
        by_micro(mine_grads, other_grads),
        gains[0:1],
        query[None],
        key.T[None],
        value.T[None],
        out[None],
        gains[1:2],
        gate[None],
        up[None],
        down.T[None],
    )


def solution(mesh):
    rows = P(None, "fsdp", None, "ctx", None)
    gain, matrix = P("section", "fsdp"), P("section", "fsdp", None)
    layer_rows = P("section", None, "fsdp", None, "ctx", None)
    weights = (gain, matrix, matrix, matrix, matrix, gain, matrix, matrix, matrix)
    return jax.shard_map(
        on_device,
        mesh=mesh,
        in_specs=(rows, rows) + weights,
        out_specs=(layer_rows, layer_rows) + weights,
        check_vma=False,
    )
```

time: 772 us -> 552 us (0.72)
  blocking collectives: 148 us -> 65.1 us
  local copies, waits for them, and re-layouts: 106 us -> 31.2 us
  starting transfers between devices: 151 us -> 108 us
  Pallas kernels: 85.9 us -> 125 us
  waiting for transfers between devices: 212 us -> 184 us
  matrix products: 15.5 us -> 0 us
  other arithmetic: 27.5 us -> 13.5 us
    all_gather x3 -> x0, blocking collectives: 80 us -> none  [the longest x1 40.9 us: on_device(): out = lax.all_gather(out_slice, 'ctx', tiled=True)[:SHARD].astype(F32)]
    reduce_scatter x4 -> x2, waiting for transfers between devices: 73.1 us -> 0.02 us  [ffn_gradient(): lax.psum_scatter(slices.reshape(CTX * FSDP * SLICE, FFN_COLS), 'ctx', sca...]
    slice x22 -> x9, local copies, waits for them, and re-layouts: 43.3 us -> 4.03 us  [the longest x2 1.73 us: gains_of(): rows = qkv_weights[layer][SLICES, ::SLICE, :2 * SHARD].astype(F32)]
    pallas_call x16 -> x24, Pallas kernels: 85.9 us -> 125 us  [call(): pl.pallas_call(body, out_shape=outs, in_specs=specs + [pl.BlockSpec(memor...]
    all_to_all x10, waiting for transfers between devices: 21.7 us -> 47.4 us  [all_to_all(): return lax.all_to_all(x, axis, 0, 0)]
    ppermute x54 -> x45, starting transfers between devices: 67.7 us -> 43.6 us  [shifted(): return lax.ppermute(x, axis, [(i, (i + distance) % n) for i in range(n)])]
    ppermute x54 -> x45, waiting for transfers between devices: 55.2 us -> 74 us  [shifted(): return lax.ppermute(x, axis, [(i, (i + distance) % n) for i in range(n)])]
    all_to_all x10, starting transfers between devices: 68.1 us -> 51 us  [all_to_all(): return lax.all_to_all(x, axis, 0, 0)]
  transfers between devices with their start and end apart: 83 -> 68, of which waited for: 28 -> 40; matrix products, arithmetic and copies ran while one was open for 10% -> 5% of each run, Pallas kernels for 10% -> 19%
where the time goes in v2:
time: 552 us; the launch traced here: 541 us
  waiting for transfers between devices  184 us (33%)
  Pallas kernels  125 us (23%)
  starting transfers between devices  108 us (20%)
  blocking collectives  65.1 us (12%)
  local copies, waits for them, and re-layouts  31.2 us (6%)
  between operations  15.2 us (3%)
  other arithmetic  13.5 us (2%)
    pallas_call x24, Pallas kernels, call(): pl.pallas_call(body, out_shape=outs, in_specs=specs + [pl.BlockSpec(memor...  125 us
    ppermute x45, waiting for transfers between devices, shifted(): return lax.ppermute(x, axis, [(i, (i + distance) % n) for i in range(n)])  74 us
    all_to_all x3, blocking collectives, all_to_all(): return lax.all_to_all(x, axis, 0, 0)  65.1 us
    all_to_all x10, starting transfers between devices, all_to_all(): return lax.all_to_all(x, axis, 0, 0)  51 us
    all_to_all x10, waiting for transfers between devices, all_to_all(): return lax.all_to_all(x, axis, 0, 0)  47.4 us
    ppermute x45, starting transfers between devices, shifted(): return lax.ppermute(x, axis, [(i, (i + distance) % n) for i in range(n)])  43.6 us
    ppermute x6, waiting for transfers between devices, swap_sections(): return lax.ppermute(x, 'section', [(0, 1), (1, 0)])  17.6 us
    all_gather x1, waiting for transfers between devices, on_device(): qkv_weights, rest_weights = ([lax.all_gather(qkv[0], 'ctx')], [])  17.6 us
  transfers between devices with their start and end apart: 68, of which 40 were waited for; matrix products, arithmetic and copies ran while one was open for 5% of the time, Pallas kernels for 19%

profile of v2, /device:TPU:1, one launch (start us, length us, event | category | flops | bytes accessed | tf_op | source)
XLA Modules:
  0.0 541.3 jit_solution(1921354545323378805)
XLA Ops:
  10.2 16.5 %all_to_all.65 = bf16[8,16,1664]{2,1,0:T(8,128)(2,1)S(1)} all-to-all(bf16[8,16,1664]{2,1,0:T(8,128)(2,1)S(1)} %broadcast_in_dim.39), channel_id=1, replica_groups=mesh['section'=2,'ctx'=16,'fsdp'=4] {'section','fsdp'}, dimensions={0} | all-to-all | bytes 851968 | tf_op jit(solution)/shard_map/all_to_all | solution.py:437
  36.8 7.8 %collective-permute-done = bf16[64,640]{1,0:T(8,128)(2,1)S(1)} collective-permute-done((bf16[64,640]{1,0:T(8,128)(2,1)S(1)}, bf16[64,640]{1,0:T(8,128)(2,1)S(1)}, u32[]{:S(2)}, u32[]{:S(2)}) %collective-permute-start) | collective-permute-done | bytes 81952 | tf_op jit(solution)/shard_map/ppermute | solution.py:433
  49.1 17.6 %all-gather.10.cloned.1.call-done.refs_4_.w_far = bf16[16,64,1664]{2,1,0:T(8,128)(2,1)} async-done(((bf16[1,64,1664]{2,1,0:T(8,128)(2,1)}), bf16[16,64,1664]{2,1,0:T(8,128)(2,1)}) %all-gather.10.cloned.1.call-update) | async-done | bytes 3407888 | tf_op jit(solution)/shard_map/all_gather | solution.py:489
  72.9 21.2 %all_to_all.66.recv = bf16[16,144,128]{2,1,0:T(8,128)(2,1)} all-to-all(bf16[16,144,128]{2,1,0:T(8,128)(2,1)} %get-tuple-element.95), channel_id=1, replica_groups=mesh['section'=2,'ctx'=16,'fsdp'=4] {'ctx'}, dimensions={0} | all-to-all | bytes 1179648 | tf_op jit(solution)/shard_map/all_to_all | solution.py:437
  105.2 7.9 %all-to-all-done.2.recv = bf16[16,48,128]{2,1,0:T(8,128)(2,1)S(1)} async-done(((bf16[16,48,128]{2,1,0:T(8,128)(2,1)}), bf16[16,48,128]{2,1,0:T(8,128)(2,1)S(1)}, u32[]{:S(2)}, u32[]{:S(2)}) %all-to-all-start.2) | async-done | bytes 196640 | tf_op jit(solution)/shard_map/all_to_all | solution.py:437
  137.9 6.3 %shard_map.215 = (f32[384,640]{1,0:T(8,128)}, f32[384,640]{1,0:T(8,128)}, f32[96,960]{1,0:T(8,128)}, bf16[48,1920]{1,0:T(8,128)(2,1)}, bf16[48,1920]{1,0:T(8,128)(2,1)}, /*index=5*/bf16[48,1920]{1,0:T(8,128)(2,1)}) custom-call(bf16[48,1920]{1,0:T(8,128)(2,1)} %get-tuple-element.99.refs_0_, bf16[48,1920]{1,0:T(8,128)(2,1)} %copy-done.20, ...), custom_call_target="tpu_custom_call" | custom-call | flops 1415577600 | bytes 3624960 | tf_op jit(solution)/shard_map/pallas_call | solution.py:50
  146.1 12.6 %all-gather.14.cloned.1.call-done = bf16[1024,1664]{1,0:T(8,128)(2,1)} async-done(((bf16[64,1664]{1,0:T(8,128)(2,1)}), bf16[1024,1664]{1,0:T(8,128)(2,1)}) %all-gather.14.cloned.1.call-update) | async-done | bytes 3407888 | tf_op jit(solution)/shard_map/all_gather | solution.py:537
  170.5 17.0 %all-to-all-done.4.recv = bf16[16,144,128]{2,1,0:T(8,128)(2,1)S(1)} async-done(((bf16[16,144,128]{2,1,0:T(8,128)(2,1)}), bf16[16,144,128]{2,1,0:T(8,128)(2,1)S(1)}, u32[]{:S(2)}, u32[]{:S(2)}) %all-to-all-start.4) | async-done | bytes 589856 | tf_op jit(solution)/shard_map/all_to_all | solution.py:437
  188.3 5.7 %shard_map.217 = bf16[16,48,128]{2,1,0:T(8,128)(2,1)} custom-call(bf16[16,144,128]{2,1,0:T(8,128)(2,1)} %copy-done.9), custom_call_target="tpu_custom_call" | custom-call | flops 301989888 | bytes 786432 | tf_op jit(solution)/shard_map/pallas_call | solution.py:50
  231.0 6.3 %shard_map.219 = (f32[384,640]{1,0:T(8,128)}, f32[384,640]{1,0:T(8,128)}, f32[96,960]{1,0:T(8,128)}, bf16[48,1920]{1,0:T(8,128)(2,1)}, bf16[48,1920]{1,0:T(8,128)(2,1)}, /*index=5*/bf16[48,1920]{1,0:T(8,128)(2,1)}) custom-call(bf16[48,1920]{1,0:T(8,128)(2,1)} %get-tuple-element.113.refs_0_, bf16[48,1920]{1,0:T(8,128)(2,1)} %copy-done.23, ...), custom_call_target="tpu_custom_call" | custom-call | flops 1415577600 | bytes 3624960 | tf_op jit(solution)/shard_map/pallas_call | solution.py:50
  238.2 6.1 %shard_map.220 = (bf16[384,640]{1,0:T(8,128)(2,1)}, bf16[384,1280]{1,0:T(8,128)(2,1)}, f32[96,960]{1,0:T(8,128)}, bf16[48,1920]{1,0:T(8,128)(2,1)}, bf16[48,1920]{1,0:T(8,128)(2,1)}, /*index=5*/bf16[48,1920]{1,0:T(8,128)(2,1)}) custom-call(bf16[48,1920]{1,0:T(8,128)(2,1)} %copy-done.6, bf16[48,1920]{1,0:T(8,128)(2,1)} %copy-done.26, ...), custom_call_target="tpu_custom_call" | custom-call | flops 1415577600 | bytes 5099520 | tf_op jit(solution)/shard_map/pallas_call | solution.py:50
  261.3 6.2 %shard_map.232 = bf16[16,64,1920]{2,1,0:T(8,128)(2,1)} custom-call(bf16[48,1920]{1,0:T(8,128)(2,1)} %get-tuple-element.113.refs_0_, bf16[48,1920]{1,0:T(8,128)(2,1)} %copy-done.23, bf16[48,1920]{1,0:T(8,128)(2,1)} %copy-done.22, bf16[48,1920]{1,0:T(8,128)(2,1)} %copy-done.21, bf16[48,1920]{1,0:T(8,128)(2,1)} %copy-done.6, bf16[48,1920]{1,0:T(8,128)(2,1)} %copy-done.26, ...), custom_call_target="tpu_custom_call" | custom-call | flops 1415577600 | bytes 6881280 | tf_op jit(solution)/shard_map/pallas_call | solution.py:50
  282.8 9.2 %shard_map.222 = bf16[16,144,128]{2,1,0:T(8,128)(2,1)} custom-call(bf16[16,144,128]{2,1,0:T(8,128)(2,1)} %copy-done.9, bf16[16,48,128]{2,1,0:T(8,128)(2,1)} %copy-done.16, f32[1536,128]{1,0:T(8,128)} %constant.130.clone.cos, f32[1536,128]{1,0:T(8,128)} %constant.131.clone.sin), custom_call_target="tpu_custom_call" | custom-call | flops 754974720 | bytes 2949120 | tf_op jit(solution)/shard_map/pallas_call | solution.py:50
  292.1 6.8 %all-to-all-start.7 = ((bf16[16,144,128]{2,1,0:T(8,128)(2,1)}), bf16[16,144,128]{2,1,0:T(8,128)(2,1)S(1)}, u32[]{:S(2)}, u32[]{:S(2)}) async-start(bf16[16,144,128]{2,1,0:T(8,128)(2,1)} %shard_map.222), calls=%async_computation.7 | async-start | bytes 1179648 | tf_op jit(solution)/shard_map/all_to_all | solution.py:437
  336.5 6.1 %shard_map.225 = (bf16[384,640]{1,0:T(8,128)(2,1)}, bf16[384,1280]{1,0:T(8,128)(2,1)}, f32[96,960]{1,0:T(8,128)}, bf16[48,1920]{1,0:T(8,128)(2,1)}, bf16[48,1920]{1,0:T(8,128)(2,1)}, /*index=5*/bf16[48,1920]{1,0:T(8,128)(2,1)}) custom-call(bf16[48,1920]{1,0:T(8,128)(2,1)} %get-tuple-element.138.refs_0_.g.refs_4_, bf16[48,1920]{1,0:T(8,128)(2,1)} %copy-done.29, ...), custom_call_target="tpu_custom_call" | custom-call | flops 1415577600 | bytes 5099520 | tf_op jit(solution)/shard_map/pallas_call | solution.py:50
  342.6 6.2 %shard_map.231 = bf16[16,64,1920]{2,1,0:T(8,128)(2,1)} custom-call(bf16[48,1920]{1,0:T(8,128)(2,1)} %get-tuple-element.99.refs_0_, bf16[48,1920]{1,0:T(8,128)(2,1)} %copy-done.20, bf16[48,1920]{1,0:T(8,128)(2,1)} %copy-done.19, bf16[48,1920]{1,0:T(8,128)(2,1)} %copy-done.18, bf16[48,1920]{1,0:T(8,128)(2,1)} %get-tuple-element.138.refs_0_.g.refs_4_, ...), custom_call_target="tpu_custom_call" | custom-call | flops 1415577600 | bytes 6881280 | tf_op jit(solution)/shard_map/pallas_call | solution.py:50
  381.2 9.2 %shard_map.227 = bf16[16,144,128]{2,1,0:T(8,128)(2,1)} custom-call(bf16[16,144,128]{2,1,0:T(8,128)(2,1)} %all_to_all.66.recv, bf16[16,48,128]{2,1,0:T(8,128)(2,1)} %copy-done.17, f32[1536,128]{1,0:T(8,128)} %constant.130.clone.cos, f32[1536,128]{1,0:T(8,128)} %constant.131.clone.sin), custom_call_target="tpu_custom_call" | custom-call | flops 754974720 | bytes 2949120 | tf_op jit(solution)/shard_map/pallas_call | solution.py:50
  394.4 6.4 %all-to-all-start.9 = ((bf16[16,144,128]{2,1,0:T(8,128)(2,1)}), bf16[16,144,128]{2,1,0:T(8,128)(2,1)S(1)}, u32[]{:S(2)}, u32[]{:S(2)}) async-start(bf16[16,144,128]{2,1,0:T(8,128)(2,1)} %shard_map.227), calls=%async_computation.9 | async-start | bytes 1179648 | tf_op jit(solution)/shard_map/all_to_all | solution.py:437
  411.4 6.4 %all-to-all-done.9.recv = bf16[16,144,128]{2,1,0:T(8,128)(2,1)S(1)} async-done(((bf16[16,144,128]{2,1,0:T(8,128)(2,1)}), bf16[16,144,128]{2,1,0:T(8,128)(2,1)S(1)}, u32[]{:S(2)}, u32[]{:S(2)}) %all-to-all-start.9) | async-done | bytes 589856 | tf_op jit(solution)/shard_map/all_to_all | solution.py:437
  435.6 11.8 %all-to-all-done.10 = bf16[16,16,3712]{2,1,0:T(8,128)(2,1)S(1)} async-done(((bf16[16,16,3712]{2,1,0:T(8,128)(2,1)}), bf16[16,16,3712]{2,1,0:T(8,128)(2,1)S(1)}, u32[]{:S(2)}, u32[]{:S(2)}) %all-to-all-start.10) | async-done | bytes 1900576 | tf_op jit(solution)/shard_map/all_to_all | solution.py:437
  470.3 27.4 %all_to_all.67 = bf16[16,16,1664]{2,1,0:T(8,128)(2,1)S(1)} all-to-all(bf16[16,16,1664]{2,1,0:T(8,128)(2,1)S(1)} %copy-done.3), channel_id=1, replica_groups=mesh['section'=2,'ctx'=16,'fsdp'=4] {'ctx'}, dimensions={0} | all-to-all | bytes 1703936 | tf_op jit(solution)/shard_map/all_to_all | solution.py:437
  504.4 6.8 %all-to-all-start.12 = ((bf16[16,16,1664]{2,1,0:T(8,128)(2,1)}), bf16[16,16,1664]{2,1,0:T(8,128)(2,1)S(1)}, u32[]{:S(2)}, u32[]{:S(2)}) async-start(bf16[16,16,1664]{2,1,0:T(8,128)(2,1)} %broadcast_in_dim.41), calls=%async_computation.14 | async-start | bytes 1703936 | tf_op jit(solution)/shard_map/all_to_all | solution.py:437
  514.2 9.2 %all-gather.18.cloned.1.call-done = bf16[1280,1920]{1,0:T(8,128)(2,1)} async-done(((bf16[80,1920]{1,0:T(8,128)(2,1)}), bf16[1280,1920]{1,0:T(8,128)(2,1)}) %all-gather.18.cloned.1.call-update) | async-done | bytes 4915216 | tf_op jit(solution)/shard_map/all_gather | solution.py:669
  523.4 6.1 %shard_map.234 = (f32[240,2560]{1,0:T(8,128)}, f32[240,2560]{1,0:T(8,128)}, f32[960,640]{1,0:T(8,128)}, f32[240,960]{1,0:T(8,128)}) custom-call(s32[1]{0:T(128)} %bitcast.39.fsdp_ref, bf16[16,80,1920]{2,1,0:T(8,128)(2,1)} %bitcast.125), custom_call_target="tpu_custom_call" | custom-call | bytes 13209604 | tf_op jit(solution)/shard_map/pallas_call | solution.py:50
  (361 shorter events, 283.5 us)
Async XLA Ops:
  7.2 59.5 %all-gather.10.cloned.1.call-start = ((), (), s32[]{:S(2)}) async-start(), calls=%async_computation.15 | async-start | bytes 3620864 | tf_op jit(solution)/shard_map/all_gather | solution.py:489
  33.0 85.8 %all-gather.12.cloned.1.call-start = ((), (), s32[]{:S(2)}) async-start(), calls=%async_computation.18 | async-start | bytes 6406144 | tf_op jit(solution)/shard_map/all_gather | solution.py:536
  46.4 112.3 %all-gather.14.cloned.1.call-start = ((), (), s32[]{:S(2)}) async-start(), calls=%async_computation.19 | async-start | bytes 3620864 | tf_op jit(solution)/shard_map/all_gather | solution.py:537
  104.4 106.3 %all-gather.16.cloned.1.call-start = ((), (), s32[]{:S(2)}) async-start(), calls=%async_computation.20 | async-start | bytes 6406144 | tf_op jit(solution)/shard_map/all_gather | solution.py:545
  166.2 21.2 %all-to-all-start.4 = ((bf16[16,144,128]{2,1,0:T(8,128)(2,1)}), bf16[16,144,128]{2,1,0:T(8,128)(2,1)S(1)}, u32[]{:S(2)}, u32[]{:S(2)}) async-start(bf16[16,144,128]{2,1,0:T(8,128)(2,1)} %get-tuple-element.106), calls=%async_computation.4 | async-start | bytes 1179648 | tf_op jit(solution)/shard_map/all_to_all | solution.py:437
  194.0 16.2 %all-to-all-start.5 = ((bf16[16,48,128]{2,1,0:T(8,128)(2,1)}), bf16[16,48,128]{2,1,0:T(8,128)(2,1)S(1)}, u32[]{:S(2)}, u32[]{:S(2)}) async-start(bf16[16,48,128]{2,1,0:T(8,128)(2,1)} %shard_map.217), calls=%async_computation.5 | async-start | bytes 393216 | tf_op jit(solution)/shard_map/all_to_all | solution.py:437
  198.3 253.0 %reduce-scatter.5.cloned.1.call-start = ((), (), s32[]{:S(2)}) async-start(), calls=%async_computation.17 | async-start | bytes 4177920 | tf_op jit(solution)/shard_map/reduce_scatter | solution.py:574
  218.8 18.6 %collective-permute-start.15 = (bf16[48,1920]{1,0:T(8,128)(2,1)S(1)}, bf16[48,1920]{1,0:T(8,128)(2,1)S(1)}, u32[]{:S(2)}, u32[]{:S(2)}) collective-permute-start(bf16[48,1920]{1,0:T(8,128)(2,1)S(1)} %reshape.138.refs_0_.g.refs_4_), channel_id=1, source_target_pairs={{0,3},{1,0},{2,1},{3,2},{4,7},{5,4},{6,5},{7,6},{8,11},{9,8},{10,9... | collective-permute-start | bytes 552968 | tf_op jit(solution)/shard_map/ppermute | solution.py:416
  220.9 16.4 %collective-permute-start.14 = (bf16[48,1920]{1,0:T(8,128)(2,1)S(1)}, bf16[48,1920]{1,0:T(8,128)(2,1)S(1)}, u32[]{:S(2)}, u32[]{:S(2)}) collective-permute-start(bf16[48,1920]{1,0:T(8,128)(2,1)S(1)} %reshape.138.refs_0_.g.refs_4_), channel_id=1, source_target_pairs={{0,2},{1,3},{2,0},{3,1},{4,6},{5,7},{6,4},{7,5},{8,10},{9,11},{10,... | collective-permute-start | bytes 552968 | tf_op jit(solution)/shard_map/ppermute | solution.py:416
  275.7 16.3 %collective-permute-start.19 = (bf16[48,1920]{1,0:T(8,128)(2,1)S(1)}, bf16[48,1920]{1,0:T(8,128)(2,1)S(1)}, u32[]{:S(2)}, u32[]{:S(2)}) collective-permute-start(bf16[48,1920]{1,0:T(8,128)(2,1)S(1)} %copy-done.66), channel_id=1, source_target_pairs={{0,3},{1,0},{2,1},{3,2},{4,7},{5,4},{6,5},{7,6},{8,11},{9,8},{10,9... | collective-permute-start | bytes 552968 | tf_op jit(solution)/shard_map/ppermute | solution.py:416
  275.8 16.3 %collective-permute-start.20 = (bf16[48,1920]{1,0:T(8,128)(2,1)S(1)}, bf16[48,1920]{1,0:T(8,128)(2,1)S(1)}, u32[]{:S(2)}, u32[]{:S(2)}) collective-permute-start(bf16[48,1920]{1,0:T(8,128)(2,1)S(1)} %copy-done.65), channel_id=1, source_target_pairs={{0,2},{1,3},{2,0},{3,1},{4,6},{5,7},{6,4},{7,5},{8,10},{9,11},{10,... | collective-permute-start | bytes 552968 | tf_op jit(solution)/shard_map/ppermute | solution.py:416
  292.1 24.2 %all-to-all-start.7 = ((bf16[16,144,128]{2,1,0:T(8,128)(2,1)}), bf16[16,144,128]{2,1,0:T(8,128)(2,1)S(1)}, u32[]{:S(2)}, u32[]{:S(2)}) async-start(bf16[16,144,128]{2,1,0:T(8,128)(2,1)} %shard_map.222), calls=%async_computation.7 | async-start | bytes 1179648 | tf_op jit(solution)/shard_map/all_to_all | solution.py:437
  298.8 152.5 %reduce-scatter.3.cloned.1.call-start = ((), (), s32[]{:S(2)}) async-start(), calls=%async_computation.16 | async-start | bytes 4177920 | tf_op jit(solution)/shard_map/reduce_scatter | solution.py:574
  371.8 18.6 %collective-permute-start.37 = (bf16[112,1664]{1,0:T(8,128)(2,1)S(1)}, bf16[112,1664]{1,0:T(8,128)(2,1)S(1)}, u32[]{:S(2)}, u32[]{:S(2)}) collective-permute-start(bf16[112,1664]{1,0:T(8,128)(2,1)S(1)} %copy-done.38), channel_id=1, source_target_pairs={{0,3},{1,0},{2,1},{3,2},{4,7},{5,4},{6,5},{7,6},{8,11},{9,8},{10,9... | collective-permute-start | bytes 1118216 | tf_op jit(solution)/shard_map/ppermute | solution.py:416
  372.7 17.7 %collective-permute-start.36 = (bf16[112,1664]{1,0:T(8,128)(2,1)S(1)}, bf16[112,1664]{1,0:T(8,128)(2,1)}, u32[]{:S(2)}, u32[]{:S(2)}) collective-permute-start(bf16[112,1664]{1,0:T(8,128)(2,1)S(1)} %copy-done.38), channel_id=1, source_target_pairs={{0,2},{1,3},{2,0},{3,1},{4,6},{5,7},{6,4},{7,5},{8,10},{9,11},{10,... | collective-permute-start | bytes 1118216 | tf_op jit(solution)/shard_map/ppermute | solution.py:416
  372.7 20.2 %collective-permute-start.35 = (bf16[112,1664]{1,0:T(8,128)(2,1)S(1)}, bf16[112,1664]{1,0:T(8,128)(2,1)}, u32[]{:S(2)}, u32[]{:S(2)}) collective-permute-start(bf16[112,1664]{1,0:T(8,128)(2,1)S(1)} %copy-done.38), channel_id=1, source_target_pairs={{0,1},{1,2},{2,3},{3,0},{4,5},{5,6},{6,7},{7,4},{8,9},{9,10},{10,1... | collective-permute-start | bytes 1118216 | tf_op jit(solution)/shard_map/ppermute | solution.py:416
  394.4 23.5 %all-to-all-start.9 = ((bf16[16,144,128]{2,1,0:T(8,128)(2,1)}), bf16[16,144,128]{2,1,0:T(8,128)(2,1)S(1)}, u32[]{:S(2)}, u32[]{:S(2)}) async-start(bf16[16,144,128]{2,1,0:T(8,128)(2,1)} %shard_map.227), calls=%async_computation.9 | async-start | bytes 1179648 | tf_op jit(solution)/shard_map/all_to_all | solution.py:437
  417.9 29.5 %all-to-all-start.10 = ((bf16[16,16,3712]{2,1,0:T(8,128)(2,1)}), bf16[16,16,3712]{2,1,0:T(8,128)(2,1)S(1)}, u32[]{:S(2)}, u32[]{:S(2)}) async-start(bf16[16,16,3712]{2,1,0:T(8,128)(2,1)} %pad_maximum_fusion), calls=%async_computation.10 | async-start | bytes 3801088 | tf_op jit(solution)/shard_map/all_to_all | solution.py:437
  422.3 101.1 %all-gather.18.cloned.1.call-start = ((), (), s32[]{:S(2)}) async-start(), calls=%async_computation.21 | async-start | bytes 5222400 | tf_op jit(solution)/shard_map/all_gather | solution.py:669
  427.7 23.6 %collective-permute-start.41 = (bf16[48,1920]{1,0:T(8,128)(2,1)S(1)}, bf16[48,1920]{1,0:T(8,128)(2,1)S(1)}, u32[]{:S(2)}, u32[]{:S(2)}) collective-permute-start(bf16[48,1920]{1,0:T(8,128)(2,1)S(1)} %broadcast_select_fusion.5), channel_id=1, source_target_pairs={{0,64},{64,0},{1,65},{65,1},{2,66},{66,2},{3,67},{67,3},{4,68},{68... | collective-permute-start | bytes 552968 | tf_op jit(solution)/shard_map/ppermute | solution.py:433
  430.8 23.1 %collective-permute-start.48 = (bf16[112,1664]{1,0:T(8,128)(2,1)}, bf16[112,1664]{1,0:T(8,128)(2,1)S(1)}, u32[]{:S(2)}, u32[]{:S(2)}) collective-permute-start(bf16[112,1664]{1,0:T(8,128)(2,1)} %get-tuple-element.165.refs_4_), channel_id=1, source_target_pairs={{0,3},{1,0},{2,1},{3,2},{4,7},{5,4},{6,5},{7,6},{8,11},{9,8},{10,9... | collective-permute-start | bytes 1118216 | tf_op jit(solution)/shard_map/ppermute | solution.py:416
  433.2 20.7 %collective-permute-start.47 = (bf16[112,1664]{1,0:T(8,128)(2,1)}, bf16[112,1664]{1,0:T(8,128)(2,1)}, u32[]{:S(2)}, u32[]{:S(2)}) collective-permute-start(bf16[112,1664]{1,0:T(8,128)(2,1)} %get-tuple-element.165.refs_4_), channel_id=1, source_target_pairs={{0,2},{1,3},{2,0},{3,1},{4,6},{5,7},{6,4},{7,5},{8,10},{9,11},{10,... | collective-permute-start | bytes 1118216 | tf_op jit(solution)/shard_map/ppermute | solution.py:416
  434.7 19.2 %collective-permute-start.46 = (bf16[112,1664]{1,0:T(8,128)(2,1)}, bf16[112,1664]{1,0:T(8,128)(2,1)}, u32[]{:S(2)}, u32[]{:S(2)}) collective-permute-start(bf16[112,1664]{1,0:T(8,128)(2,1)} %get-tuple-element.165.refs_4_), channel_id=1, source_target_pairs={{0,1},{1,2},{2,3},{3,0},{4,5},{5,6},{6,7},{7,4},{8,9},{9,10},{10,1... | collective-permute-start | bytes 1118216 | tf_op jit(solution)/shard_map/ppermute | solution.py:416
  504.4 25.1 %all-to-all-start.12 = ((bf16[16,16,1664]{2,1,0:T(8,128)(2,1)}), bf16[16,16,1664]{2,1,0:T(8,128)(2,1)S(1)}, u32[]{:S(2)}, u32[]{:S(2)}) async-start(bf16[16,16,1664]{2,1,0:T(8,128)(2,1)} %broadcast_in_dim.41), calls=%async_computation.14 | async-start | bytes 1703936 | tf_op jit(solution)/shard_map/all_to_all | solution.py:437
  (114 other events, 987.5 us)
Sparse Core Ops, SparseCore 0:
  27.6 39.0 all-gather.9
  69.0 49.7 all-gather.11
  121.1 37.5 all-gather.13
  160.8 49.8 all-gather.15
  267.7 71.1 reduce-scatter.4
  348.9 71.9 reduce-scatter.2
  470.4 52.9 all-gather.17

commit v3 on v2

--- a/solution.py
+++ b/solution.py
@@ -44,17 +44,23 @@
     return jax.ShapeDtypeStruct(shape, dtype)
 
 
-def call(body, outs, *args, far=(), scalars=0, scratch=(), flops=0):
+def call(body, outs, *args, far=(), far_out=False, wait_for=(), scalars=0, scratch=(), flops=0):
+    given = len(args) + len(far)
+
+    def kernel(*refs):
+        body(*refs[:given], *refs[given + len(wait_for) :])
+
     size = sum(a.size * a.dtype.itemsize for a in (*args, *outs))
     specs = [pl.BlockSpec(memory_space=pltpu.SMEM if i < scalars else pltpu.VMEM) for i in range(len(args))]
     return pl.pallas_call(
-        body,
+        kernel,
         out_shape=outs,
-        in_specs=specs + [pl.BlockSpec(memory_space=pl.ANY)] * len(far),
+        out_specs=[pl.BlockSpec(memory_space=pl.ANY if far_out else pltpu.VMEM)] * len(outs),
+        in_specs=specs + [pl.BlockSpec(memory_space=pl.ANY)] * (len(far) + len(wait_for)),
         scratch_shapes=list(scratch),
         compiler_params=pltpu.CompilerParams(vmem_limit_bytes=56 * 1024 * 1024),
         cost_estimate=pl.CostEstimate(flops=flops, bytes_accessed=size, transcendentals=0),
-    )(*args, *far)
+    )(*args, *far, *wait_for)
 
 
 def dot(a, b):
@@ -86,6 +92,10 @@
     ahead = pltpu.roll(x, cols - HEAD // 2, 1)
     behind = pltpu.roll(x, HEAD // 2, 1)
     return jnp.where(lane % HEAD < HEAD // 2, ahead, behind)
+
+
+def by_core(c):
+    return c % 2 * (CTX // 2) + c // 2
 
 
 def source_block(b):
@@ -140,10 +150,10 @@
     return [pltpu.VMEM((FSDP, SLICES, SLICE, lanes), BF16), pltpu.SemaphoreType.DMA((FSDP,))]
 
 
-def qkv_body(count, *refs):
+def qkv_body(count, start, *refs):
     parts, (gain, cos, sin, w_far) = refs[:count], refs[count : count + 4]
     x_out, a_out, send, w_s, sems = refs[count + 4 :]
-    copies = load_rows(w_far, slice(0, QKV_LANES), w_s, sems)
+    copies = load_rows(w_far, slice(start, start + QKV_LANES), w_s, sems)
     x = parts[0][...].astype(F32)
     if count > 1:
         x = x + parts[1][...]
@@ -187,20 +197,24 @@
         v_s[rows, :] = v[:, half * HEAD : (half + 1) * HEAD].astype(BF16)
 
 
-def probabilities(q, keys, start):
+def masked_scores(q, keys, start):
     scores = dot_t(q, keys)
-    row = lax.broadcasted_iota(jnp.int32, scores.shape, 0) + start
-    col = lax.broadcasted_iota(jnp.int32, scores.shape, 1)
-    scores = jnp.where(col <= row, scores, MASKED)
-    weights = jnp.exp(scores - jnp.max(scores, axis=-1, keepdims=True))
-    return weights / jnp.sum(weights, axis=-1, keepdims=True)
-
-
-def attend_body(recv, send, q_s, k_s, v_s, out_s):
+    row = lax.broadcasted_iota(jnp.int32, (TILE, TILE), 0)
+    col = lax.broadcasted_iota(jnp.int32, (TILE, TILE), 1)
+    last = jnp.where(col <= row, scores[:, start:], MASKED)
+    return last if start == 0 else jnp.concatenate([scores[:, :start], last], axis=1)
+
+
+def attend_body(recv, send, log_out, q_s, k_s, v_s, out_s):
     unpack_heads(recv, q_s, k_s, v_s)
     for i in range(LENGTH // TILE):
         start, stop = i * TILE, (i + 1) * TILE
-        p = probabilities(q_s[start:stop, :], k_s[:stop, :], start)
+        scores = masked_scores(q_s[start:stop, :], k_s[:stop, :], start)
+        top = jnp.max(scores, axis=-1, keepdims=True)
+        weights = jnp.exp(scores - top)
+        total = jnp.sum(weights, axis=-1, keepdims=True)
+        log_out[start:stop, :] = top + jnp.log(total)
+        p = weights * (1.0 / total)
         out_s[start:stop, :] = dot(p.astype(BF16), v_s[:stop, :])
     for c in range(CTX):
         last = 2 * CTX - 1 - c
@@ -208,8 +222,8 @@
         send[c] = jnp.concatenate(pair, axis=1).astype(BF16)
 
 
-def mix_body(x, recv, gain, w_far, mixed_out, b_out, att_out, att_s, w_s, sems):
-    copies = load_rows(w_far, slice(0, OUT_LANES), w_s, sems)
+def mix_body(start, x, recv, gain, w_far, mixed_out, b_out, att_out, att_s, w_s, sems):
+    copies = load_rows(w_far, slice(start, start + OUT_LANES), w_s, sems)
     for h in range(HEADS):
         pair = recv[h].astype(F32)
         cols = slice(h * HEAD, (h + 1) * HEAD)
@@ -234,11 +248,11 @@
     return jnp.concatenate([unpack(p[...]) for p in parts], axis=0)
 
 
-def ffn_body(*refs):
+def ffn_body(start, *refs):
     parts, w_far, (gate_out, up_out), outs = refs[:4], refs[4], refs[5:7], refs[7:11]
     w_s, sems, down_s, down_sem = refs[11:]
-    copies = load_rows(w_far, slice(OUT_LANES, OUT_LANES + 2 * FF_SHARD), w_s, sems)
-    down = load_down(w_far, slice(OUT_LANES + 2 * FF_SHARD, OUT_LANES + FFN_COLS), down_s, down_sem)
+    copies = load_rows(w_far, slice(start, start + 2 * FF_SHARD), w_s, sems)
+    down = load_down(w_far, slice(start + 2 * FF_SHARD, start + FFN_COLS), down_s, down_sem)
     rows = all_rows(parts)
     wait_all(copies)
     gate_up = dot(rows, rows_of(w_s))
@@ -250,13 +264,13 @@
     spread(dot_t(hidden, rows_of(down_s)), outs)
 
 
-def ffn_back_body(*refs):
+def ffn_back_body(start, *refs):
     parts, (gate_ref, up_ref, w_far) = refs[:4], refs[4:7]
     hidden_out, d_gu_out = refs[7:9]
     outs = refs[9:13]
     w_s, sems, down_s, down_sem = refs[13:]
-    down = load_down(w_far, slice(OUT_LANES + 2 * FF_SHARD, OUT_LANES + FFN_COLS), down_s, down_sem)
-    copies = load_rows(w_far, slice(OUT_LANES, OUT_LANES + 2 * FF_SHARD), w_s, sems)
+    down = load_down(w_far, slice(start + 2 * FF_SHARD, start + FFN_COLS), down_s, down_sem)
+    copies = load_rows(w_far, slice(start, start + 2 * FF_SHARD), w_s, sems)
     rows = all_rows(parts)
     gate, up = gate_ref[...], up_ref[...]
     sig = jax.nn.sigmoid(gate)
@@ -272,20 +286,30 @@
 
 def ffn_grad_body(*refs):
     b_parts, g_parts, d_gu, hidden, out = refs[:4], refs[4:8], refs[8], refs[9], refs[10]
-    gu = t_dot(all_rows(b_parts), d_gu[...]).astype(BF16)
-    for f in range(FSDP):
-        for c in range(SLICES):
-            first = f * SHARD + c * SLICE
-            out[c, f * SLICE : (f + 1) * SLICE, 0 : 2 * FF_SHARD] = gu[first : first + SLICE]
-    down = t_dot(all_rows(g_parts), hidden[...]).astype(BF16)
-    for c in range(SLICES):
-        out[c, :, 2 * FF_SHARD :] = down[c * DOWN_SLICE : (c + 1) * DOWN_SLICE]
+    stage, sems = refs[11:]
     for c in range(SLICES, CTX):
-        out[c] = jnp.zeros(out.shape[1:], BF16)
-
-
-def mix_back_body(g, p0, p1, p2, p3, mixed, gain, w_far, d_mixed_out, ga_out, gain_out, send, w_s, sems):
-    copies = load_rows(w_far, slice(0, OUT_LANES), w_s, sems)
+        stage[c] = jnp.zeros(stage.shape[1:], BF16)
+    rows = all_rows(b_parts)
+    copies = []
+    for group in range(3):
+        lanes = slice(group * FF_SHARD, (group + 1) * FF_SHARD)
+        if group < 2:
+            grad = t_dot(rows, d_gu[:, lanes]).astype(BF16)
+            for f in range(FSDP):
+                for c in range(SLICES):
+                    first = f * SHARD + c * SLICE
+                    stage[c, f * SLICE : (f + 1) * SLICE, lanes] = grad[first : first + SLICE]
+        else:
+            grad = t_dot(all_rows(g_parts), hidden[...]).astype(BF16)
+            for c in range(SLICES):
+                stage[c, :, lanes] = grad[c * DOWN_SLICE : (c + 1) * DOWN_SLICE]
+        copies.append(pltpu.make_async_copy(stage.at[:, :, lanes], out.at[:, :, lanes], sems.at[group]))
+        copies[-1].start()
+    wait_all(copies)
+
+
+def mix_back_body(start, g, p0, p1, p2, p3, mixed, gain, w_far, d_mixed_out, ga_out, gain_out, send, w_s, sems):
+    copies = load_rows(w_far, slice(start, start + OUT_LANES), w_s, sems)
     d_b = p0[...]
     for part in (p1, p2, p3):
         d_b = d_b + unpack(part[...].astype(F32))
@@ -303,7 +327,7 @@
         send[h] = jnp.zeros(send.shape[1:], BF16)
 
 
-def attend_back_body(recv, d_recv, cos, sin, send, q_s, k_s, v_s, d_s, dq_s, dk_s, dv_s):
+def attend_back_body(recv, d_recv, log_total, cos, sin, send, q_s, k_s, v_s, d_s, dq_s, dk_s, dv_s):
     unpack_heads(recv, q_s, k_s, v_s)
     for b in range(2 * CTX):
         c, half = source_block(b)
@@ -314,7 +338,7 @@
     for i in range(LENGTH // TILE):
         start, stop = i * TILE, (i + 1) * TILE
         q, d_att = q_s[start:stop, :], d_s[start:stop, :]
-        p = probabilities(q, k_s[:stop, :], start)
+        p = jnp.exp(masked_scores(q, k_s[:stop, :], start) - log_total[start:stop, :])
         d_p = dot_t(d_att, v_s[:stop, :])
         inner = jnp.sum(p * d_p, axis=-1, keepdims=True)
         d_scores = (p * (d_p - inner)).astype(BF16)
@@ -333,8 +357,8 @@
         send[c, ROWS:] = jnp.concatenate(pair, axis=1).astype(BF16)
 
 
-def qkv_back_body(recv, d_mixed, x_ref, gain, gain_ffn, w_far, d_x_out, low_out, rows_out, rows_s, w_s, sems):
-    copies = load_rows(w_far, slice(0, QKV_LANES), w_s, sems)
+def qkv_back_body(start, recv, d_mixed, x_ref, gain, gain_ffn, w_far, d_x_out, low_out, rows_out, rows_s, w_s, sems):
+    copies = load_rows(w_far, slice(start, start + QKV_LANES), w_s, sems)
     rows_s[:, QKV_COLS:] = jnp.zeros((ROWS, QKV_LANES - QKV_COLS), BF16)
     for g in range(KV_HEADS):
         d_k = jnp.zeros((ROWS, HEAD), F32)
@@ -362,17 +386,22 @@
 
 
 def qkv_grad_body(fsdp_ref, *refs):
-    blocks, parts, out = refs[:4], refs[4:8], refs[8]
+    blocks, parts, others, out = refs[:4], refs[4:8], refs[8:-1], refs[-1]
+    start = QKV_LANES
+    for other in others:
+        out[:, :, start : start + other.shape[2]] = other[...]
+        start += other.shape[2]
     cols = jnp.concatenate([p[:, :SHARD] for p in blocks], axis=0)
     rows = jnp.concatenate([p[0:ROWS] for p in parts], axis=0)
     grad = t_dot(cols, rows).astype(BF16)
     for c in range(SLICES):
-        out[c] = grad[c * SLICE : (c + 1) * SLICE]
+        out[by_core(c), :, :QKV_LANES] = grad[c * SLICE : (c + 1) * SLICE]
     gains = sum(p[ROWS:].astype(F32) for p in parts)
     mine = jnp.zeros((SLICE, SHARD), F32)
     for f in range(FSDP):
         mine = jnp.where(fsdp_ref[0] == f, gains[:, f * SHARD : (f + 1) * SHARD], mine)
-    out[SLICES] = jnp.concatenate([mine, jnp.zeros((SLICE, QKV_LANES - SHARD), F32)], axis=1).astype(BF16)
+    mine = jnp.concatenate([mine, jnp.zeros((SLICE, QKV_LANES - SHARD), F32)], axis=1)
+    out[by_core(SLICES), :, :QKV_LANES] = mine.astype(BF16)
 
 
 def out_grad_body(*refs):
@@ -381,8 +410,8 @@
     grad = t_dot(cols, all_rows(ga_parts))
     grad = jnp.concatenate([grad, jnp.zeros((SHARD, OUT_LANES - WIDTH), F32)], axis=1).astype(BF16)
     for c in range(SLICES):
-        out[c] = grad[c * SLICE : (c + 1) * SLICE]
-    out[SLICES] = jnp.zeros((SLICE, OUT_LANES), BF16)
+        out[by_core(c)] = grad[c * SLICE : (c + 1) * SLICE]
+    out[by_core(SLICES)] = jnp.zeros((SLICE, OUT_LANES), BF16)
 
 
 def rest_result_body(fsdp_ref, gathered, gate, up, down, out):
@@ -394,12 +423,17 @@
             piece = gathered[c, k * SLICE : (k + 1) * SLICE, : 2 * FF_SHARD].astype(F32)
             gate[rows, cols] = piece[:, :FF_SHARD]
             up[rows, cols] = piece[:, FF_SHARD:]
+        out[rows] = gathered[c, FSDP * SLICE :, :WIDTH].astype(F32)
         down[c * DOWN_SLICE : (c + 1) * DOWN_SLICE] = gathered[c, 0 : FSDP * SLICE, 2 * FF_SHARD : FFN_COLS].astype(F32)
-        out[rows] = gathered[c, FSDP * SLICE :, :WIDTH].astype(F32)
-
-
-def qkv_result_body(gathered, query, key, value, gains, kv_s):
+
+
+def qkv_result_body(core_ref, same, other, query, key, value, gains, kv_s):
     kv = KV_HEADS * HEAD
+    swapped = core_ref[0] == 1
+    gathered = []
+    for c in range(CTX):
+        here, there = (same, other) if c % 2 == 0 else (other, same)
+        gathered.append(jnp.where(swapped, there[c // 2], here[c // 2]))
     for c in range(SLICES):
         rows = slice(c * SLICE, (c + 1) * SLICE)
         piece = gathered[c].astype(F32)
@@ -439,6 +473,14 @@
 
 def after(x, *earlier):
     return lax.optimization_barrier((x, earlier))[0]
+
+
+def core_pair(x):
+    return lax.ppermute(x, "ctx", [(i, i ^ 1) for i in range(CTX)])
+
+
+def same_core(x):
+    return lax.all_to_all(x, "ctx", 0, 0, axis_index_groups=[list(range(k, CTX, 2)) for k in range(2)])
 
 
 def to_all(x, axis, count):
@@ -469,27 +511,29 @@
         return lax.dynamic_slice_in_dim(rows, place * count, count, 0)
 
     own_gains = jnp.concatenate([norm_attn, norm_ffn], axis=1)
-    own_gains = jnp.pad(own_gains, ((0, SLICE - 1), (0, QKV_LANES - 2 * SHARD)))
-    qkv = jnp.concatenate([my_slice(w[0]) for w in (w_query, key_projection, value_projection)], axis=1)
-    qkv = jnp.pad(qkv, ((0, 0), (0, QKV_LANES - QKV_COLS)))
-    qkv = to_all(jnp.where(ctx < SLICES, qkv, own_gains), ("section", "fsdp"), 2 * FSDP)
-    qkv = qkv.reshape(2, FSDP * SLICE, QKV_LANES)
-
-    out = jnp.pad(my_slice(w_out[0]), ((0, 0), (0, OUT_LANES - WIDTH)))
-    out = jnp.broadcast_to(out[:, None], (SLICE, FSDP, OUT_LANES))
-    rest = [my_slice(w[0]).reshape(SLICE, FSDP, FF_SHARD) for w in (w_gate, w_up)]
-    rest = jnp.concatenate([out] + rest, axis=2).transpose(1, 0, 2)
-    rest = all_to_all(after(jnp.concatenate([rest, rest]), qkv), ("section", "fsdp"))
-    rest = rest.reshape(2, FSDP * SLICE, OUT_LANES + 2 * FF_SHARD)
+    own_gains = jnp.pad(own_gains, ((0, SLICE - 1), (0, QKV_LANES + OUT_LANES - 2 * SHARD)))
+    own = [my_slice(w[0]) for w in (w_query, key_projection, value_projection)]
+    own.append(jnp.zeros((SLICE, QKV_LANES - QKV_COLS), BF16))
+    own += [my_slice(w_out[0]), jnp.zeros((SLICE, OUT_LANES - WIDTH), BF16)]
+    own = jnp.where(ctx < SLICES, jnp.concatenate(own, axis=1), own_gains)
+    attention = to_all(own, ("section", "fsdp"), 2 * FSDP).reshape(2, FSDP * SLICE, QKV_LANES + OUT_LANES)
+
+    ffn = [my_slice(w[0]).reshape(SLICE, FSDP, FF_SHARD) for w in (w_gate, w_up)]
+    ffn = jnp.concatenate(ffn, axis=2).transpose(1, 0, 2)
+    ffn = all_to_all(after(jnp.concatenate([ffn, ffn]), attention), ("section", "fsdp"))
+    ffn = ffn.reshape(2, FSDP * SLICE, 2 * FF_SHARD)
     down = my_slice(w_down[0].T, DOWN_SLICE)
-    down_other = swap_sections(after(down, qkv))
+    down_other = swap_sections(after(down, attention))
     downs = (jnp.where(first, down, down_other), jnp.where(first, down_other, down))
-    rest = [jnp.concatenate(pair, axis=1) for pair in zip(rest, downs)]
-
-    qkv_weights, rest_weights = [lax.all_gather(qkv[0], "ctx")], []
+    ffn = [jnp.concatenate(pair, axis=1) for pair in zip(ffn, downs)]
+
+    gathered = lax.all_gather(attention[0], "ctx")
+    qkv_weights, out_weights = [(gathered, 0)], [(gathered, QKV_LANES)]
+    ffn_weights = []
 
     def gains_of(layer):
-        rows = qkv_weights[layer][SLICES, ::SLICE, : 2 * SHARD].astype(F32)
+        source, start = qkv_weights[layer]
+        rows = source[SLICES, ::SLICE, start : start + 2 * SHARD].astype(F32)
         return rows[:, :SHARD].reshape(1, WIDTH), rows[:, SHARD:].reshape(1, WIDTH)
 
     cos_all, sin_all = rotary_constants()
@@ -526,40 +570,48 @@
     kept = []
     parts = [my_rows]
     for layer in range(2):
+        qkv_w, qkv_at = qkv_weights[layer]
         gain_attn, gain_ffn = gains_of(layer)
         x, a_blocks, send = call(
-            bind(qkv_body, len(parts)), [row_bf16, blocks_shape, heads_shape],
-            *parts, gain_attn, cos_own, sin_own, far=[qkv_weights[layer]],
+            bind(qkv_body, len(parts), qkv_at), [row_bf16, blocks_shape, heads_shape],
+            *parts, gain_attn, cos_own, sin_own, far=[qkv_w],
             scratch=qkv_scratch, flops=2 * ROWS * WIDTH * QKV_COLS,
         )
         if layer == 0:
-            rest_weights.append(lax.all_gather(rest[0], "ctx"))
-            qkv_weights.append(lax.all_gather(after(qkv[1], send), "ctx"))
+            gathered = jnp.concatenate([ffn[0], attention[1][:, :QKV_LANES]], axis=1)
+            gathered = lax.all_gather(gathered, "ctx")
+            ffn_weights.append((gathered, 0))
+            qkv_weights.append((gathered, FFN_COLS))
         heads = all_to_all(send, "ctx")
-        send = call(
-            attend_body, [att_shape], heads,
-            scratch=[seq(BF16), seq(BF16), seq(BF16), seq(F32)], flops=2 * LENGTH * LENGTH * HEAD,
-        )[0]
+        beside = []
+        if layer == 1:
+            first_blocks = exchange_blocks(after(kept[0][1], send), fsdp)
+            beside = first_blocks
+        send, log_total = call(
+            attend_body, [att_shape, sds((LENGTH, 1), F32)], heads,
+            wait_for=beside, scratch=[seq(BF16), seq(BF16), seq(BF16), seq(F32)], flops=2 * LENGTH * LENGTH * HEAD,
+        )
         arrived = all_to_all(send, "ctx")
         if layer == 0:
-            rest_weights.append(lax.all_gather(after(rest[1], arrived), "ctx"))
-        else:
-            first_blocks = exchange_blocks(after(kept[0][1], send), fsdp)
-            arrived = after(arrived, *first_blocks)
+            gathered = jnp.concatenate([ffn[1], attention[1][:, QKV_LANES:]], axis=1)
+            gathered = lax.all_gather(after(gathered, arrived), "ctx")
+            ffn_weights.append((gathered, 0))
+            out_weights.append((gathered, FFN_COLS))
+        (out_w, out_at), (ffn_w, ffn_at) = out_weights[layer], ffn_weights[layer]
         mixed, b, att_blocks = call(
-            mix_body, [row_f32, packed, blocks_shape],
-            x, arrived, gain_ffn, far=[rest_weights[layer]],
+            bind(mix_body, out_at), [row_f32, packed, blocks_shape],
+            x, arrived, gain_ffn, far=[out_w],
             scratch=[pltpu.VMEM((ROWS, WIDTH), BF16)] + out_scratch, flops=2 * ROWS * WIDTH * WIDTH,
         )
         b_all = around(b)
         gate, up, *outs = call(
-            ffn_body, [ff_f32, ff_f32] + partials, *b_all, far=[rest_weights[layer]],
+            bind(ffn_body, ffn_at), [ff_f32, ff_f32] + partials, *b_all, far=[ffn_w],
             scratch=ffn_scratch, flops=2 * FSDP * ROWS * WIDTH * FF_SHARD * 3,
         )
         if layer == 0:
             parts = [mixed] + back_around(outs)
         blocks = jnp.concatenate([a_blocks, att_blocks], axis=2)
-        kept.append((x, blocks, heads, mixed, b_all, gate, up, gain_attn, gain_ffn))
+        kept.append((x, blocks, heads, log_total, mixed, b_all, gate, up, gain_attn, gain_ffn))
     first_acts, last_outs = kept[1][0], outs
 
     g = my_cotangent
@@ -568,17 +620,17 @@
 
     def ffn_gradient(b_all, g_all, d_gu, hidden):
         slices = call(
-            ffn_grad_body, [sds((CTX, FSDP * SLICE, FFN_COLS), BF16)], *b_all, *g_all, d_gu, hidden,
+            ffn_grad_body, [sds((CTX, FSDP * SLICE, FFN_COLS), BF16)], *b_all, *g_all, d_gu, hidden, far_out=True,
+            scratch=[pltpu.VMEM((CTX, FSDP * SLICE, FFN_COLS), BF16), pltpu.SemaphoreType.DMA((3,))],
             flops=2 * FSDP * ROWS * WIDTH * FFN_COLS,
         )[0]
-        return lax.psum_scatter(
-            slices.reshape(CTX * FSDP * SLICE, FFN_COLS), "ctx", scatter_dimension=0, tiled=True
-        )
-
-    def qkv_gradient(blocks, d_rows):
+        return slices.reshape(CTX * FSDP * SLICE, FFN_COLS)
+
+    def qkv_gradient(blocks, d_rows, *others, wait_for=()):
+        lanes = QKV_LANES + sum(other.shape[2] for other in others)
         return call(
-            qkv_grad_body, [sds((CTX, SLICE, QKV_LANES), BF16)], fsdp_index, *blocks, *d_rows,
-            scalars=1, flops=2 * FSDP * ROWS * SHARD * QKV_COLS,
+            qkv_grad_body, [sds((CTX, SLICE, lanes), BF16)], fsdp_index, *blocks, *d_rows, *others,
+            wait_for=wait_for, scalars=1, flops=2 * FSDP * ROWS * SHARD * QKV_COLS,
         )[0]
 
     def out_gradient(blocks, ga):
@@ -588,35 +640,35 @@
         )[0]
 
     def reduced(slices):
-        return all_to_all(slices, "ctx").astype(F32).sum(axis=0).astype(BF16)
+        halves = slices.reshape(2, CTX // 2, *slices.shape[1:])
+        keep, give = [lax.dynamic_index_in_dim(halves, k, 0, keepdims=False) for k in (ctx % 2, 1 - ctx % 2)]
+        half = (keep.astype(F32) + core_pair(give).astype(F32)).astype(BF16)
+        return same_core(half).astype(F32).sum(axis=0).astype(BF16)
 
     for layer in (1, 0):
-        x, blocks, heads, mixed, b_all, gate, up, gain_attn, gain_ffn = kept[layer]
+        x, blocks, heads, log_total, mixed, b_all, gate, up, gain_attn, gain_ffn = kept[layer]
+        (qkv_w, qkv_at), (out_w, out_at), (ffn_w, ffn_at) = qkv_weights[layer], out_weights[layer], ffn_weights[layer]
         g_all = around(g)
         hidden, d_gu, *outs = call(
-            ffn_back_body,
+            bind(ffn_back_body, ffn_at),
             [ff_bf16, sds((FSDP * ROWS, 2 * FF_SHARD), BF16)] + partials,
-            *g_all, gate, up, far=[rest_weights[layer]],
+            *g_all, gate, up, far=[ffn_w],
             scratch=ffn_scratch, flops=2 * FSDP * ROWS * WIDTH * FF_SHARD * 3,
         )
-        if layer == 0:
-            ffn_grads[0] = ffn_gradient(b_all, g_all, d_gu, hidden)
+        arrived = back_around(outs)
+        slices = ffn_gradient(b_all, g_all, d_gu, hidden)
+        ffn_grads[layer] = lax.psum_scatter(slices, "ctx", scatter_dimension=0, tiled=True)
         d_mixed, ga, d_gain_ffn, send = call(
-            mix_back_body, [row_f32, packed, sds((1, WIDTH), F32), att_shape],
-            g, *back_around(outs), mixed, gain_ffn, far=[rest_weights[layer]],
+            bind(mix_back_body, out_at), [row_f32, packed, sds((1, WIDTH), F32), att_shape],
+            g, *arrived, mixed, gain_ffn, far=[out_w], wait_for=[slices],
             scratch=out_scratch, flops=2 * ROWS * WIDTH * WIDTH,
         )
         if layer == 1:
-            ffn_grads[1] = ffn_gradient(b_all, g_all, after(d_gu, send), hidden)
-        if layer == 1:
-            blocks = exchange_blocks(after(blocks, send), fsdp)
-            late_blocks = blocks
-            last_parts = back_around([after(part, send) for part in last_outs])
-            beside = [*blocks, *last_parts]
+            ga = around(after(ga, send))
+            beside = ga
         else:
-            blocks = first_blocks
             late_rows = around(after(d_rows, send))
-            last_acts = kept[1][3] + last_parts[0]
+            last_acts = kept[1][4] + last_parts[0]
             for part in last_parts[1:]:
                 part = part.reshape(BLK, 2, WIDTH).transpose(1, 0, 2).reshape(ROWS, WIDTH)
                 last_acts = last_acts + part.astype(F32)
@@ -625,21 +677,26 @@
             beside = [*late_rows, other_acts]
         send = call(
             attend_back_body, [heads_shape],
-            heads, all_to_all(send, "ctx"), cos_all, sin_all,
+            heads, all_to_all(send, "ctx"), log_total, cos_all, sin_all,
             scratch=[seq(BF16)] * 4 + [seq(F32)] + [pltpu.VMEM((HEAD, LENGTH), F32)] * 2,
             flops=5 * LENGTH * LENGTH * HEAD,
         )[0]
         send = after(send, *beside)
-        ga = around(after(ga, send))
-        out_grads[layer] = out_gradient(blocks, ga)
-        beside = [out_grads[layer]]
-        if layer == 0:
+        if layer == 1:
+            blocks = exchange_blocks(after(blocks, send), fsdp)
+            last_parts = back_around([after(part, send) for part in last_outs])
+            out_grads[1] = out_gradient(blocks, ga)
+            beside, late_blocks = [*last_parts, out_grads[1]], blocks
+        else:
+            blocks = first_blocks
+            ga = around(after(ga, send))
             late_slices = qkv_gradient(late_blocks, late_rows)
-            beside.append(late_slices)
+            out_grads[0] = out_gradient(blocks, ga)
+            beside = [late_slices, out_grads[0]]
         d_x, d_low, d_rows = call(
-            qkv_back_body,
+            bind(qkv_back_body, qkv_at),
             [row_f32, packed, sds((ROWS + SLICE, QKV_LANES), BF16)],
-            after(all_to_all(send, "ctx"), *beside), d_mixed, x, gain_attn, d_gain_ffn, far=[qkv_weights[layer]],
+            all_to_all(send, "ctx"), d_mixed, x, gain_attn, d_gain_ffn, far=[qkv_w], wait_for=beside,
             scratch=[pltpu.VMEM((ROWS, QKV_LANES), BF16)] + qkv_scratch,
             flops=2 * ROWS * WIDTH * QKV_COLS,
         )
@@ -650,29 +707,30 @@
         keep, give = jnp.where(first, zero, one), jnp.where(first, one, zero)
         return (keep.astype(F32) + swap_sections(give).astype(F32)).astype(BF16)
 
-    late_slices = reduced(jnp.concatenate([late_slices, *out_grads], axis=2))
-    other_grads = swap_sections(jnp.where(first, d_inputs[1][1], d_inputs[0][1]))
-    ffn_slices = across(*[after(grad, send) for grad in ffn_grads])
+    late_slices = reduced(after(jnp.concatenate([late_slices, *out_grads], axis=2), d_rows))
+    d_rows = around(d_rows)
+    ffn_slices = across(*[after(grad, d_rows[0]) for grad in ffn_grads])
     gate_up = ffn_slices[:, : 2 * FF_SHARD].reshape(FSDP, SLICE, 2 * FF_SHARD)
     gate_up = jnp.concatenate(exchange_blocks(gate_up, fsdp))
     ffn_slices = jnp.concatenate([gate_up, ffn_slices[:, 2 * FF_SHARD :]], axis=1)
+    slices = qkv_gradient(blocks, d_rows, wait_for=[late_slices, ffn_slices])
     out_grads = [late_slices[:, start : start + OUT_LANES] for start in (QKV_LANES, QKV_LANES + OUT_LANES)]
-    d_rows = around(d_rows)
-    d_rows[0] = after(d_rows[0], late_slices, other_grads, ffn_slices)
-    slices = qkv_gradient(blocks, d_rows)
-    out_slices = across(*[after(grad, slices) for grad in out_grads])
+    out_slices = jnp.pad(across(*[after(grad, slices) for grad in out_grads]), ((0, 0), (0, FFN_COLS - OUT_LANES)))
+    rest_slices = jnp.concatenate([ffn_slices, out_slices])
+    other_grads = swap_sections(after(jnp.where(first, d_inputs[1][1], d_inputs[0][1]), slices))
     qkv_slices = across(reduced(slices), late_slices[:, :QKV_LANES])
-    out_slices = jnp.pad(out_slices, ((0, 0), (0, FFN_COLS - OUT_LANES)))
     gate, up, down, out = call(
         rest_result_body,
         [sds((SHARD, FF), F32), sds((SHARD, FF), F32), sds((WIDTH, FF_SHARD), F32), sds((SHARD, WIDTH), F32)],
-        fsdp_index, lax.all_gather(jnp.concatenate([ffn_slices, out_slices]), "ctx"), scalars=1,
+        fsdp_index, lax.all_gather(rest_slices, "ctx"), scalars=1,
     )
     kv = KV_HEADS * HEAD
+    qkv_same = same_core(jnp.broadcast_to(qkv_slices[None], (CTX // 2,) + qkv_slices.shape))
     query, key, value, gains = call(
         qkv_result_body,
         [sds((SHARD, WIDTH), F32), sds((kv, SHARD), F32), sds((kv, SHARD), F32), sds((8, SHARD), F32)],
-        after(to_all(qkv_slices, "ctx", CTX), gate), scratch=[pltpu.VMEM((SHARD, 2 * kv), F32)],
+        (ctx % 2).astype(jnp.int32).reshape(1), qkv_same, core_pair(qkv_same),
+        scratch=[pltpu.VMEM((SHARD, 2 * kv), F32)], scalars=1, wait_for=[gate, other_grads],
     )
     other_grads = other_grads.reshape(BLK, 2, WIDTH).transpose(1, 0, 2).reshape(ROWS, WIDTH).astype(F32)
     d_one = d_inputs[1][1].reshape(BLK, 2, WIDTH).transpose(1, 0, 2).reshape(ROWS, WIDTH).astype(F32)

time: 552 us -> 541 us (0.980)
  blocking collectives: 65.1 us -> 36.1 us
  starting transfers between devices: 108 us -> 126 us
  waiting for transfers between devices: 184 us -> 176 us
  local copies, waits for them, and re-layouts: 31.2 us -> 38.5 us
    all_to_all x3 -> x1, blocking collectives: 65.1 us -> 19.3 us  [all_to_all(): return lax.all_to_all(x, axis, 0, 0)]
    all_gather x5 -> x4, waiting for transfers between devices: 44.8 us -> 23.1 us  [the longest x1 21.9 us: on_device(): gathered = lax.all_gather(attention[0], 'ctx')]
    all_to_all x0 -> x2, waiting for transfers between devices: none -> 19.1 us  [same_core(): lax.all_to_all(x, 'ctx', 0, 0, axis_index_groups=[list(range(k, CTX, 2))...]
    all_to_all x0 -> x1, blocking collectives: none -> 16.8 us  [same_core(): lax.all_to_all(x, 'ctx', 0, 0, axis_index_groups=[list(range(k, CTX, 2))...]
    all_to_all x10 -> x9, waiting for transfers between devices: 47.4 us -> 58.9 us  [all_to_all(): return lax.all_to_all(x, axis, 0, 0)]
    ppermute x45, starting transfers between devices: 43.6 us -> 54.8 us  [shifted(): return lax.ppermute(x, axis, [(i, (i + distance) % n) for i in range(n)])]
    ppermute x6, waiting for transfers between devices: 17.6 us -> 7.76 us  [swap_sections(): return lax.ppermute(x, 'section', [(0, 1), (1, 0)])]
    ppermute x45, waiting for transfers between devices: 74 us -> 65.8 us  [shifted(): return lax.ppermute(x, axis, [(i, (i + distance) % n) for i in range(n)])]
  transfers between devices with their start and end apart: 68 -> 71, of which waited for: 40 -> 40; matrix products, arithmetic and copies ran while one was open for 5% -> 6% of each run, Pallas kernels for 19% -> 19%
where the time goes in v3:
time: 541 us; the launch traced here: 530 us
  waiting for transfers between devices  176 us (33%)
  starting transfers between devices  126 us (23%)
  Pallas kernels  122 us (23%)
  local copies, waits for them, and re-layouts  38.5 us (7%)
  blocking collectives  36.1 us (7%)
  other arithmetic  15.9 us (3%)
  between operations  15.6 us (3%)
    pallas_call x24, Pallas kernels, call(): pl.pallas_call(kernel, out_shape=outs, out_specs=[pl.BlockSpec(memory_spa...  122 us
    ppermute x45, waiting for transfers between devices, shifted(): return lax.ppermute(x, axis, [(i, (i + distance) % n) for i in range(n)])  65.8 us
    all_to_all x9, waiting for transfers between devices, all_to_all(): return lax.all_to_all(x, axis, 0, 0)  58.9 us
    ppermute x45, starting transfers between devices, shifted(): return lax.ppermute(x, axis, [(i, (i + distance) % n) for i in range(n)])  54.8 us
    all_to_all x9, starting transfers between devices, all_to_all(): return lax.all_to_all(x, axis, 0, 0)  49 us
    all_gather x1, waiting for transfers between devices, on_device(): gathered = lax.all_gather(attention[0], 'ctx')  21.9 us
    all_to_all x1, blocking collectives, all_to_all(): return lax.all_to_all(x, axis, 0, 0)  19.3 us
    all_to_all x2, waiting for transfers between devices, same_core(): lax.all_to_all(x, 'ctx', 0, 0, axis_index_groups=[list(range(k, CTX, 2))...  19.1 us
  transfers between devices with their start and end apart: 71, of which 40 were waited for; matrix products, arithmetic and copies ran while one was open for 6% of the time, Pallas kernels for 19%

profile of v3, /device:TPU:1, one launch (start us, length us, event | category | flops | bytes accessed | tf_op | source)
XLA Modules:
  0.0 530.3 jit_solution(7458319505484585701)
XLA Ops:
  10.2 19.3 %all_to_all.65 = bf16[8,16,2688]{2,1,0:T(8,128)(2,1)S(1)} all-to-all(bf16[8,16,2688]{2,1,0:T(8,128)(2,1)S(1)} %broadcast_in_dim.33), channel_id=1, replica_groups=mesh['section'=2,'ctx'=16,'fsdp'=4] {'section','fsdp'}, dimensions={0} | all-to-all | bytes 1376256 | tf_op jit(solution)/shard_map/all_to_all | solution.py:471
  39.3 8.5 %all-to-all-done.3 = bf16[8,16,1280]{2,1,0:T(8,128)(2,1)S(1)} async-done(((bf16[8,16,1280]{2,1,0:T(8,128)(2,1)}), bf16[8,16,1280]{2,1,0:T(8,128)(2,1)S(1)}, u32[]{:S(2)}, u32[]{:S(2)}) %all-to-all-start.3) | async-done | bytes 327712 | tf_op jit(solution)/shard_map/all_to_all | solution.py:471
  51.4 21.9 %all-gather.8.cloned.1.call-done.refs_4_.refs_3_.refs_7_.refs_5_ = bf16[16,64,2688]{2,1,0:T(8,128)(2,1)} async-done(((bf16[1,64,2688]{2,1,0:T(8,128)(2,1)}), bf16[16,64,2688]{2,1,0:T(8,128)(2,1)}) %all-gather.8.cloned.1.call-update) | async-done | bytes 5505040 | tf_op jit(solution)/shard_map/all_gather | solution.py:530
  83.7 15.5 %all-to-all-done.1.refs_0_ = bf16[16,144,128]{2,1,0:T(8,128)(2,1)S(1)} async-done(((bf16[16,144,128]{2,1,0:T(8,128)(2,1)}), bf16[16,144,128]{2,1,0:T(8,128)(2,1)S(1)}, u32[]{:S(2)}, u32[]{:S(2)}) %all-to-all-start.1) | async-done | bytes 589856 | tf_op jit(solution)/shard_map/all_to_all | solution.py:471
  100.0 5.8 %shard_map.213 = (bf16[16,48,128]{2,1,0:T(8,128)(2,1)}, f32[1536,1]{1,0:T(8,128)}) custom-call(bf16[16,144,128]{2,1,0:T(8,128)(2,1)} %copy-done.10), custom_call_target="tpu_custom_call" | custom-call | flops 301989888 | bytes 792576 | tf_op jit(solution)/shard_map/pallas_call | solution.py:55
  112.0 7.9 %all-to-all-done.2.refs_1_ = bf16[16,48,128]{2,1,0:T(8,128)(2,1)S(1)} async-done(((bf16[16,48,128]{2,1,0:T(8,128)(2,1)}), bf16[16,48,128]{2,1,0:T(8,128)(2,1)S(1)}, u32[]{:S(2)}, u32[]{:S(2)}) %all-to-all-start.2) | async-done | bytes 196640 | tf_op jit(solution)/shard_map/all_to_all | solution.py:471
  137.7 6.3 %shard_map.215 = (f32[384,640]{1,0:T(8,128)}, f32[384,640]{1,0:T(8,128)}, f32[96,960]{1,0:T(8,128)}, bf16[48,1920]{1,0:T(8,128)(2,1)}, bf16[48,1920]{1,0:T(8,128)(2,1)}, /*index=5*/bf16[48,1920]{1,0:T(8,128)(2,1)}) custom-call(bf16[48,1920]{1,0:T(8,128)(2,1)} %get-tuple-element.97.refs_0_, bf16[48,1920]{1,0:T(8,128)(2,1)} %copy-done.37, ...), custom_call_target="tpu_custom_call" | custom-call | flops 1415577600 | bytes 3624960 | tf_op jit(solution)/shard_map/pallas_call | solution.py:55
  183.1 5.8 %shard_map.217 = (bf16[16,48,128]{2,1,0:T(8,128)(2,1)}, f32[1536,1]{1,0:T(8,128)}) custom-call(bf16[16,144,128]{2,1,0:T(8,128)(2,1)} %copy-done.11, bf16[96,480]{1,0:T(8,128)(2,1)} %get-tuple-element.194.refs_1_.refs_0_, bf16[96,480]{1,0:T(8,128)(2,1)} %copy-done.44, bf16[96,480]{1,0:T(8,128)(2,1)} %copy-done.45, bf16[96,480]{1,0:T(8,128)(2,1)} %copy-done.46), custom_call_target="tpu_custom_call" | custom-call | flops 301989888 | bytes 792576 | tf_op jit(solution)/shard_map/pallas_call | solution.py:55
  193.5 6.0 %all-to-all-done.5.refs_1_ = bf16[16,48,128]{2,1,0:T(8,128)(2,1)S(1)} async-done(((bf16[16,48,128]{2,1,0:T(8,128)(2,1)}), bf16[16,48,128]{2,1,0:T(8,128)(2,1)S(1)}, u32[]{:S(2)}, u32[]{:S(2)}) %all-to-all-start.5) | async-done | bytes 196640 | tf_op jit(solution)/shard_map/all_to_all | solution.py:471
  217.3 6.3 %shard_map.219 = (f32[384,640]{1,0:T(8,128)}, f32[384,640]{1,0:T(8,128)}, f32[96,960]{1,0:T(8,128)}, bf16[48,1920]{1,0:T(8,128)(2,1)}, bf16[48,1920]{1,0:T(8,128)(2,1)}, /*index=5*/bf16[48,1920]{1,0:T(8,128)(2,1)}) custom-call(bf16[48,1920]{1,0:T(8,128)(2,1)} %get-tuple-element.112.refs_0_, bf16[48,1920]{1,0:T(8,128)(2,1)} %copy-done.27, ...), custom_call_target="tpu_custom_call" | custom-call | flops 1415577600 | bytes 3624960 | tf_op jit(solution)/shard_map/pallas_call | solution.py:55
  224.6 6.1 %shard_map.220 = (bf16[384,640]{1,0:T(8,128)(2,1)}, bf16[384,1280]{1,0:T(8,128)(2,1)}, f32[96,960]{1,0:T(8,128)}, bf16[48,1920]{1,0:T(8,128)(2,1)}, bf16[48,1920]{1,0:T(8,128)(2,1)}, /*index=5*/bf16[48,1920]{1,0:T(8,128)(2,1)}) custom-call(bf16[48,1920]{1,0:T(8,128)(2,1)} %copy-done.7, bf16[48,1920]{1,0:T(8,128)(2,1)} %copy-done.40, ...), custom_call_target="tpu_custom_call" | custom-call | flops 1415577600 | bytes 5099520 | tf_op jit(solution)/shard_map/pallas_call | solution.py:55
  252.9 8.7 %all-to-all-start.6 = ((bf16[16,48,128]{2,1,0:T(8,128)(2,1)}), bf16[16,48,128]{2,1,0:T(8,128)(2,1)S(1)}, u32[]{:S(2)}, u32[]{:S(2)}) async-start(bf16[16,48,128]{2,1,0:T(8,128)(2,1)} %get-tuple-element.122), calls=%async_computation.6 | async-start | bytes 393216 | tf_op jit(solution)/shard_map/all_to_all | solution.py:471
  270.4 8.6 %shard_map.223 = bf16[16,144,128]{2,1,0:T(8,128)(2,1)} custom-call(bf16[16,144,128]{2,1,0:T(8,128)(2,1)} %copy-done.11, bf16[16,48,128]{2,1,0:T(8,128)(2,1)} %copy-done.21, f32[1536,1]{1,0:T(8,128)} %get-tuple-element.123.refs_2_, f32[1536,128]{1,0:T(8,128)} %constant.159.clone.refs_3_, f32[1536,128]{1,0:T(8,128)} %constant.160.clone.refs_4_), custom_call_target="tpu_custom_call" | custom-call | flops 754974720 | bytes 2955264 | tf_op jit(solution)/shard_map/pallas_call | solution.py:55
  292.0 6.6 %collective-permute-done.26.refs_2_.refs_3_ = bf16[96,480]{1,0:T(8,128)(2,1)S(1)} collective-permute-done((bf16[96,480]{1,0:T(8,128)(2,1)S(1)}, bf16[96,480]{1,0:T(8,128)(2,1)S(1)}, u32[]{:S(2)}, u32[]{:S(2)}) %collective-permute-start.26) | collective-permute-done | bytes 92192 | tf_op jit(solution)/shard_map/ppermute | solution.py:450
  323.7 6.1 %shard_map.226 = (bf16[384,640]{1,0:T(8,128)(2,1)}, bf16[384,1280]{1,0:T(8,128)(2,1)}, f32[96,960]{1,0:T(8,128)}, bf16[48,1920]{1,0:T(8,128)(2,1)}, bf16[48,1920]{1,0:T(8,128)(2,1)}, /*index=5*/bf16[48,1920]{1,0:T(8,128)(2,1)}) custom-call(bf16[48,1920]{1,0:T(8,128)(2,1)} %get-tuple-element.139.refs_0_.refs_4_, bf16[48,1920]{1,0:T(8,128)(2,1)} %copy-done.24, ...), custom_call_target="tpu_custom_call" | custom-call | flops 1415577600 | bytes 5099520 | tf_op jit(solution)/shard_map/pallas_call | solution.py:55
  329.8 5.6 %shard_map.227 = bf16[16,64,1920]{2,1,0:T(8,128)(2,1)} custom-call(bf16[48,1920]{1,0:T(8,128)(2,1)} %get-tuple-element.97.refs_0_, bf16[48,1920]{1,0:T(8,128)(2,1)} %copy-done.37, bf16[48,1920]{1,0:T(8,128)(2,1)} %copy-done.38, bf16[48,1920]{1,0:T(8,128)(2,1)} %copy-done.39, bf16[48,1920]{1,0:T(8,128)(2,1)} %get-tuple-element.139.refs_0_.refs_4_, ...), custom_call_target="tpu_custom_call" | custom-call | flops 1415577600 | bytes 6881280 | tf_op jit(solution)/shard_map/pallas_call | solution.py:55
  355.8 5.9 %all-to-all-start.8 = ((bf16[16,48,128]{2,1,0:T(8,128)(2,1)}), bf16[16,48,128]{2,1,0:T(8,128)(2,1)S(1)}, u32[]{:S(2)}, u32[]{:S(2)}) async-start(bf16[16,48,128]{2,1,0:T(8,128)(2,1)} %get-tuple-element.148), calls=%async_computation.8 | async-start | bytes 393216 | tf_op jit(solution)/shard_map/all_to_all | solution.py:471
  371.4 8.5 %shard_map.229 = bf16[16,144,128]{2,1,0:T(8,128)(2,1)} custom-call(bf16[16,144,128]{2,1,0:T(8,128)(2,1)} %copy-done.10, bf16[16,48,128]{2,1,0:T(8,128)(2,1)} %copy-done.19, f32[1536,1]{1,0:T(8,128)} %get-tuple-element.150.refs_2_, f32[1536,128]{1,0:T(8,128)} %constant.159.clone.refs_3_, f32[1536,128]{1,0:T(8,128)} %constant.160.clone.refs_4_), custom_call_target="tpu_custom_call" | custom-call | flops 754974720 | bytes 2955264 | tf_op jit(solution)/shard_map/pallas_call | solution.py:55
  385.3 6.7 %all-to-all-start.9 = ((bf16[16,144,128]{2,1,0:T(8,128)(2,1)}), bf16[16,144,128]{2,1,0:T(8,128)(2,1)S(1)}, u32[]{:S(2)}, u32[]{:S(2)}) async-start(bf16[16,144,128]{2,1,0:T(8,128)(2,1)} %shard_map.229), calls=%async_computation.9 | async-start | bytes 1179648 | tf_op jit(solution)/shard_map/all_to_all | solution.py:471
  400.6 8.2 %all-to-all-done.9.refs_0_ = bf16[16,144,128]{2,1,0:T(8,128)(2,1)S(1)} async-done(((bf16[16,144,128]{2,1,0:T(8,128)(2,1)}), bf16[16,144,128]{2,1,0:T(8,128)(2,1)S(1)}, u32[]{:S(2)}, u32[]{:S(2)}) %all-to-all-start.9) | async-done | bytes 589856 | tf_op jit(solution)/shard_map/all_to_all | solution.py:471
  435.0 6.6 %all-to-all-done.10 = bf16[8,16,3712]{2,1,0:T(8,128)(2,1)S(1)} async-done(((bf16[8,16,3712]{2,1,0:T(8,128)(2,1)}), bf16[8,16,3712]{2,1,0:T(8,128)(2,1)S(1)}, u32[]{:S(2)}, u32[]{:S(2)}) %all-to-all-start.10) | async-done | bytes 950304 | tf_op jit(solution)/shard_map/all_to_all | solution.py:483
  466.6 16.8 %all_to_all.66 = bf16[8,16,1664]{2,1,0:T(8,128)(2,1)S(1)} all-to-all(bf16[8,16,1664]{2,1,0:T(8,128)(2,1)S(1)} %fusion.1), channel_id=1, replica_groups={{0,8,16,24,32,40,48,56},{4,12,20,28,36,44,52,60},{1,9,17,25,33,41,49,57..., dimensions={0} | all-to-all | bytes 851968 | tf_op jit(solution)/shard_map/all_to_all | solution.py:483
  493.6 12.4 %all-to-all-done.12.refs_1_ = bf16[8,16,1664]{2,1,0:T(8,128)(2,1)S(1)} async-done(((bf16[8,16,1664]{2,1,0:T(8,128)(2,1)}), bf16[8,16,1664]{2,1,0:T(8,128)(2,1)S(1)}, u32[]{:S(2)}, u32[]{:S(2)}) %all-to-all-start.12) | async-done | bytes 426016 | tf_op jit(solution)/shard_map/all_to_all | solution.py:483
  512.2 6.1 %shard_map.234 = (f32[240,2560]{1,0:T(8,128)}, f32[240,2560]{1,0:T(8,128)}, f32[960,640]{1,0:T(8,128)}, f32[240,960]{1,0:T(8,128)}) custom-call(s32[1]{0:T(128)} %bitcast.40.refs_0_, bf16[16,80,1920]{2,1,0:T(8,128)(2,1)} %bitcast.139), custom_call_target="tpu_custom_call" | custom-call | bytes 13209604 | tf_op jit(solution)/shard_map/pallas_call | solution.py:55
  (412 shorter events, 298.3 us)
Async XLA Ops:
  7.2 66.0 %all-gather.8.cloned.1.call-start = ((), (), s32[]{:S(2)}) async-start(), calls=%async_computation.15 | async-start | bytes 5849088 | tf_op jit(solution)/shard_map/all_gather | solution.py:530
  38.3 92.9 %all-gather.10.cloned.1.call-start = ((), (), s32[]{:S(2)}) async-start(), calls=%async_computation.18 | async-start | bytes 7798784 | tf_op jit(solution)/shard_map/all_gather | solution.py:582
  79.4 19.7 %all-to-all-start.1 = ((bf16[16,144,128]{2,1,0:T(8,128)(2,1)}), bf16[16,144,128]{2,1,0:T(8,128)(2,1)S(1)}, u32[]{:S(2)}, u32[]{:S(2)}) async-start(bf16[16,144,128]{2,1,0:T(8,128)(2,1)} %get-tuple-element.94), calls=%async_computation.1 | async-start | bytes 1179648 | tf_op jit(solution)/shard_map/all_to_all | solution.py:471
  111.2 88.3 %all-gather.12.cloned.1.call-start = ((), (), s32[]{:S(2)}) async-start(), calls=%async_computation.19 | async-start | bytes 6406144 | tf_op jit(solution)/shard_map/all_gather | solution.py:597
  163.3 19.0 %all-to-all-start.4 = ((bf16[16,144,128]{2,1,0:T(8,128)(2,1)}), bf16[16,144,128]{2,1,0:T(8,128)(2,1)S(1)}, u32[]{:S(2)}, u32[]{:S(2)}) async-start(bf16[16,144,128]{2,1,0:T(8,128)(2,1)} %get-tuple-element.105), calls=%async_computation.4 | async-start | bytes 1179648 | tf_op jit(solution)/shard_map/all_to_all | solution.py:471
  192.8 224.2 %reduce-scatter.5.cloned.1.call-start = ((), (), s32[]{:S(2)}) async-start(), calls=%async_computation.17 | async-start | bytes 4177920 | tf_op jit(solution)/shard_map/reduce_scatter | solution.py:660
  252.9 16.8 %all-to-all-start.6 = ((bf16[16,48,128]{2,1,0:T(8,128)(2,1)}), bf16[16,48,128]{2,1,0:T(8,128)(2,1)S(1)}, u32[]{:S(2)}, u32[]{:S(2)}) async-start(bf16[16,48,128]{2,1,0:T(8,128)(2,1)} %get-tuple-element.122), calls=%async_computation.6 | async-start | bytes 393216 | tf_op jit(solution)/shard_map/all_to_all | solution.py:471
  261.6 17.3 %collective-permute-start.19 = (bf16[48,1920]{1,0:T(8,128)(2,1)}, bf16[48,1920]{1,0:T(8,128)(2,1)S(1)}, u32[]{:S(2)}, u32[]{:S(2)}) collective-permute-start(bf16[48,1920]{1,0:T(8,128)(2,1)} %get-tuple-element.125.refs_4_), channel_id=1, source_target_pairs={{0,1},{1,2},{2,3},{3,0},{4,5},{5,6},{6,7},{7,4},{8,9},{9,10},{10,1... | collective-permute-start | bytes 552968 | tf_op jit(solution)/shard_map/ppermute | solution.py:450
  261.6 17.3 %collective-permute-start.20 = (bf16[48,1920]{1,0:T(8,128)(2,1)}, bf16[48,1920]{1,0:T(8,128)(2,1)S(1)}, u32[]{:S(2)}, u32[]{:S(2)}) collective-permute-start(bf16[48,1920]{1,0:T(8,128)(2,1)} %get-tuple-element.125.refs_4_), channel_id=1, source_target_pairs={{0,2},{1,3},{2,0},{3,1},{4,6},{5,7},{6,4},{7,5},{8,10},{9,11},{10,... | collective-permute-start | bytes 552968 | tf_op jit(solution)/shard_map/ppermute | solution.py:450
  279.0 24.7 %all-to-all-start.7 = ((bf16[16,144,128]{2,1,0:T(8,128)(2,1)}), bf16[16,144,128]{2,1,0:T(8,128)(2,1)S(1)}, u32[]{:S(2)}, u32[]{:S(2)}) async-start(bf16[16,144,128]{2,1,0:T(8,128)(2,1)} %shard_map.223), calls=%async_computation.7 | async-start | bytes 1179648 | tf_op jit(solution)/shard_map/all_to_all | solution.py:471
  283.3 133.7 %reduce-scatter.3.cloned.1.call-start = ((), (), s32[]{:S(2)}) async-start(), calls=%async_computation.16 | async-start | bytes 4177920 | tf_op jit(solution)/shard_map/reduce_scatter | solution.py:660
  284.3 19.4 %collective-permute-start.24 = (bf16[48,1920]{1,0:T(8,128)(2,1)S(1)}, bf16[48,1920]{1,0:T(8,128)(2,1)S(1)}, u32[]{:S(2)}, u32[]{:S(2)}) collective-permute-start(bf16[48,1920]{1,0:T(8,128)(2,1)S(1)} %copy-done.84), channel_id=1, source_target_pairs={{0,1},{1,2},{2,3},{3,0},{4,5},{5,6},{6,7},{7,4},{8,9},{9,10},{10,1... | collective-permute-start | bytes 552968 | tf_op jit(solution)/shard_map/ppermute | solution.py:450
  284.3 19.4 %collective-permute-start.23 = (bf16[48,1920]{1,0:T(8,128)(2,1)S(1)}, bf16[48,1920]{1,0:T(8,128)(2,1)S(1)}, u32[]{:S(2)}, u32[]{:S(2)}) collective-permute-start(bf16[48,1920]{1,0:T(8,128)(2,1)S(1)} %copy-done.83), channel_id=1, source_target_pairs={{0,2},{1,3},{2,0},{3,1},{4,6},{5,7},{6,4},{7,5},{8,10},{9,11},{10,... | collective-permute-start | bytes 552968 | tf_op jit(solution)/shard_map/ppermute | solution.py:450
  361.7 19.5 %collective-permute-start.35 = (bf16[112,1664]{1,0:T(8,128)(2,1)S(1)}, bf16[112,1664]{1,0:T(8,128)(2,1)S(1)}, u32[]{:S(2)}, u32[]{:S(2)}) collective-permute-start(bf16[112,1664]{1,0:T(8,128)(2,1)S(1)} %copy-done.55), channel_id=1, source_target_pairs={{0,1},{1,2},{2,3},{3,0},{4,5},{5,6},{6,7},{7,4},{8,9},{9,10},{10,1... | collective-permute-start | bytes 1118216 | tf_op jit(solution)/shard_map/ppermute | solution.py:450
  361.8 19.4 %collective-permute-start.36 = (bf16[112,1664]{1,0:T(8,128)(2,1)S(1)}, bf16[112,1664]{1,0:T(8,128)(2,1)S(1)}, u32[]{:S(2)}, u32[]{:S(2)}) collective-permute-start(bf16[112,1664]{1,0:T(8,128)(2,1)S(1)} %copy-done.55), channel_id=1, source_target_pairs={{0,2},{1,3},{2,0},{3,1},{4,6},{5,7},{6,4},{7,5},{8,10},{9,11},{10,... | collective-permute-start | bytes 1118216 | tf_op jit(solution)/shard_map/ppermute | solution.py:450
  363.5 18.1 %collective-permute-start.37 = (bf16[112,1664]{1,0:T(8,128)(2,1)S(1)}, bf16[112,1664]{1,0:T(8,128)(2,1)}, u32[]{:S(2)}, u32[]{:S(2)}) collective-permute-start(bf16[112,1664]{1,0:T(8,128)(2,1)S(1)} %copy-done.55), channel_id=1, source_target_pairs={{0,3},{1,0},{2,1},{3,2},{4,7},{5,4},{6,5},{7,6},{8,11},{9,8},{10,9... | collective-permute-start | bytes 1118216 | tf_op jit(solution)/shard_map/ppermute | solution.py:450
  385.3 23.5 %all-to-all-start.9 = ((bf16[16,144,128]{2,1,0:T(8,128)(2,1)}), bf16[16,144,128]{2,1,0:T(8,128)(2,1)S(1)}, u32[]{:S(2)}, u32[]{:S(2)}) async-start(bf16[16,144,128]{2,1,0:T(8,128)(2,1)} %shard_map.229), calls=%async_computation.9 | async-start | bytes 1179648 | tf_op jit(solution)/shard_map/all_to_all | solution.py:471
  423.5 18.2 %all-to-all-start.10 = ((bf16[8,16,3712]{2,1,0:T(8,128)(2,1)}), bf16[8,16,3712]{2,1,0:T(8,128)(2,1)S(1)}, u32[]{:S(2)}, u32[]{:S(2)}) async-start(bf16[8,16,3712]{2,1,0:T(8,128)(2,1)} %fusion), calls=%async_computation.10 | async-start | bytes 1900544 | tf_op jit(solution)/shard_map/all_to_all | solution.py:483
  427.2 85.0 %all-gather.14.cloned.1.call-start = ((), (), s32[]{:S(2)}) async-start(), calls=%async_computation.20 | async-start | bytes 5222400 | tf_op jit(solution)/shard_map/all_gather | solution.py:725
  429.7 22.9 %collective-permute-start.41 = (bf16[112,1664]{1,0:T(8,128)(2,1)S(1)}, bf16[112,1664]{1,0:T(8,128)(2,1)S(1)}, u32[]{:S(2)}, u32[]{:S(2)}) collective-permute-start(bf16[112,1664]{1,0:T(8,128)(2,1)S(1)} %copy-done.51), channel_id=1, source_target_pairs={{0,1},{1,2},{2,3},{3,0},{4,5},{5,6},{6,7},{7,4},{8,9},{9,10},{10,1... | collective-permute-start | bytes 1118216 | tf_op jit(solution)/shard_map/ppermute | solution.py:450
  431.2 21.3 %collective-permute-start.42 = (bf16[112,1664]{1,0:T(8,128)(2,1)S(1)}, bf16[112,1664]{1,0:T(8,128)(2,1)S(1)}, u32[]{:S(2)}, u32[]{:S(2)}) collective-permute-start(bf16[112,1664]{1,0:T(8,128)(2,1)S(1)} %copy-done.51), channel_id=1, source_target_pairs={{0,2},{1,3},{2,0},{3,1},{4,6},{5,7},{6,4},{7,5},{8,10},{9,11},{10,... | collective-permute-start | bytes 1118216 | tf_op jit(solution)/shard_map/ppermute | solution.py:450
  432.9 19.6 %collective-permute-start.43 = (bf16[112,1664]{1,0:T(8,128)(2,1)S(1)}, bf16[112,1664]{1,0:T(8,128)(2,1)S(1)}, u32[]{:S(2)}, u32[]{:S(2)}) collective-permute-start(bf16[112,1664]{1,0:T(8,128)(2,1)S(1)} %copy-done.51), channel_id=1, source_target_pairs={{0,3},{1,0},{2,1},{3,2},{4,7},{5,4},{6,5},{7,6},{8,11},{9,8},{10,9... | collective-permute-start | bytes 1118216 | tf_op jit(solution)/shard_map/ppermute | solution.py:450
  490.0 16.1 %all-to-all-start.12 = ((bf16[8,16,1664]{2,1,0:T(8,128)(2,1)}), bf16[8,16,1664]{2,1,0:T(8,128)(2,1)S(1)}, u32[]{:S(2)}, u32[]{:S(2)}) async-start(bf16[8,16,1664]{2,1,0:T(8,128)(2,1)} %broadcast_in_dim.34), calls=%async_computation.14 | async-start | bytes 851968 | tf_op jit(solution)/shard_map/all_to_all | solution.py:483
  493.5 17.0 %collective-permute-start.49 = (bf16[48,1920]{1,0:T(8,128)(2,1)S(1)}, bf16[48,1920]{1,0:T(8,128)(2,1)S(1)}, u32[]{:S(2)}, u32[]{:S(2)}) collective-permute-start(bf16[48,1920]{1,0:T(8,128)(2,1)S(1)} %broadcast_select_fusion.5), channel_id=1, source_target_pairs={{0,64},{64,0},{1,65},{65,1},{2,66},{66,2},{3,67},{67,3},{4,68},{68... | collective-permute-start | bytes 552968 | tf_op jit(solution)/shard_map/ppermute | solution.py:467
  (138 other events, 1028.5 us)
Sparse Core Ops, SparseCore 0:
  30.4 42.7 all-gather.7
  75.5 55.6 all-gather.9
  133.5 48.5 all-gather.11
  236.5 74.1 reduce-scatter.4
  335.7 74.6 reduce-scatter.2
  462.4 46.8 all-gather.13
